TPU v7x, 256 devices: a whole 4x4x8 slice. The times are simulated.
256 devices in a mesh: seq: 32 (over y, z), head: 8 (over x, core).
Axes of the slice: x: 4, y: 4, z: 8, core: 2. Of those that a mesh axis runs over, the one named last changes fastest.
Arguments:
- residual: bfloat16 [16384, 2048], P('seq', 'head'), may hold values from -1.796875 to 1.796875
- queries: bfloat16 [16384, 2048], P('seq', 'head'), may hold values from -12 to 12
- key_value_pairs: bfloat16 [16384, 2, 1024], P('seq', None, 'head'), may hold values from -12 to 12
- attention_out: bfloat16 [2048, 2048], P('head'), may hold values from -0.1875 to 0.1875
- norm_gain: float32 [2048], replicated, may hold values from 0.1 to 1.9
- query_key_weight: bfloat16 [2048, 2, 2048], P(None, None, 'head'), may hold values from -0.125 to 0.125
- value_gate_weight: bfloat16 [2048, 2, 4096], P(None, None, 'head'), may hold values from -0.125 to 0.125
- write_strength: float32 [32, 16384], P('head', 'seq'), may hold values from 0 to 1
- log_decay: float32 [32, 16384], P('head', 'seq'), may hold values from -1 to 0
- initial_state: float32 [32, 128, 128], P('head'), may hold values from -0.3 to 0.3
- head_gain: float32 [128], replicated, may hold values from 0.1 to 1.9
- delta_output: bfloat16 [4096, 2048], P('head'), may hold values from -0.125 to 0.125
Outputs:
- block_output: bfloat16 [16384, 2048], P('seq', 'head')
All inputs are finite; a program needn't handle non-finite values.
Results may differ from a plain program's by a relative error of at most 0.0079.
Values may be sent and summed in bfloat16 or wider, within the bound.
A program may use at most 128 MiB of HBM per device.

v0:
```python
import math

import jax
import jax.numpy as jnp
from jax import lax
from jax.sharding import PartitionSpec as P

DK = 128
DV = 128
ATTEND_HEAD_SIZE = 128
WINDOW_KEYS = 4096
STRETCH = 64


highest = lax.Precision.HIGHEST
epsilon = 1e-06


def passed_along(shard, axis, by):
    length = lax.axis_size(axis)
    pairs = [(i, i + by) for i in range(length) if 0 <= i + by < length]
    return lax.ppermute(shard, axis, pairs)


def inverse_rms(values):
    return lax.rsqrt(jnp.mean(values * values, axis=-1, keepdims=True) + epsilon)


def attend(queries, key_value_pairs, seq_index):
    row_count = queries.shape[0]
    reach_pieces = WINDOW_KEYS // row_count
    kv_heads = key_value_pairs.shape[2] // ATTEND_HEAD_SIZE
    query_heads = queries.shape[1] // ATTEND_HEAD_SIZE
    group_width = query_heads // kv_heads
    earlier_rows = jnp.concatenate(
        [passed_along(key_value_pairs, "seq", distance) for distance in range(reach_pieces, 0, -1)],
        axis=0,
    )
    window_matrix = jnp.concatenate([earlier_rows, key_value_pairs], axis=0)
    window_length = window_matrix.shape[0]
    key_matrix = window_matrix[:, 0].reshape(window_length, kv_heads, ATTEND_HEAD_SIZE)
    value_matrix = window_matrix[:, 1].reshape(window_length, kv_heads, ATTEND_HEAD_SIZE)
    query_matrix = queries.reshape(row_count, kv_heads, group_width, ATTEND_HEAD_SIZE)
    query_pos = seq_index * row_count + jnp.arange(row_count, dtype=jnp.int32)
    key_pos = (seq_index - reach_pieces) * row_count + jnp.arange(window_length, dtype=jnp.int32)
    distance_grid = query_pos[:, None] - key_pos[None, :]
    allowed = (distance_grid >= 0) & (distance_grid < WINDOW_KEYS) & (key_pos[None, :] >= 0)
    scores = jnp.einsum(
        "qhgd,khd->hgqk", query_matrix, key_matrix, preferred_element_type=jnp.float32
    ) * (1.0 / math.sqrt(ATTEND_HEAD_SIZE))
    scores = jnp.where(allowed, scores, -jnp.inf)
    row_peak = jnp.max(scores, axis=-1, keepdims=True)
    exponentials = jnp.exp(scores - row_peak)
    weights = (exponentials / jnp.sum(exponentials, axis=-1, keepdims=True)).astype(jnp.bfloat16)
    mixed_rows = jnp.einsum(
        "hgqk,khd->qhgd", weights, value_matrix, preferred_element_type=jnp.float32
    )
    return mixed_rows.astype(jnp.bfloat16).reshape(row_count, query_heads * ATTEND_HEAD_SIZE)


def split_stretches(array, value_heads, stretches):
    return array.transpose(1, 0, 2).reshape(value_heads, stretches, STRETCH, array.shape[2])


def body(
    residual,
    queries,
    key_value_pairs,
    attention_out,
    norm_gain,
    query_key_weight,
    value_gate_weight,
    write_strength,
    log_decay,
    initial_state,
    head_gain,
    delta_output,
):
    row_count = residual.shape[0]
    share_width = residual.shape[1]
    model_width = norm_gain.shape[0]
    seq_index = lax.axis_index("seq")
    head_index = lax.axis_index("head")
    attention_mix = attend(queries, key_value_pairs, seq_index)
    branch = jnp.dot(attention_mix, attention_out, preferred_element_type=jnp.float32)
    query_cols = query_key_weight.shape[2]
    value_cols = value_gate_weight.shape[2]
    flat_query_key = query_key_weight.reshape(model_width, 2 * query_cols)
    flat_value_gate = value_gate_weight.reshape(model_width, 2 * value_cols)
    placed = lax.dynamic_update_slice_in_dim(
        jnp.zeros_like(branch), residual.astype(jnp.float32), head_index * share_width, 1
    )
    hidden_full = lax.psum(branch + placed, "head")
    hidden = lax.dynamic_slice_in_dim(hidden_full, head_index * share_width, share_width, 1)
    normed = (hidden_full * inverse_rms(hidden_full) * norm_gain).astype(jnp.bfloat16)
    query_key = jnp.dot(normed, flat_query_key, preferred_element_type=jnp.float32)
    value_gate = jnp.dot(normed, flat_value_gate, preferred_element_type=jnp.float32)
    key_heads = query_cols // DK
    value_heads = value_cols // DV
    group_width = value_heads // key_heads
    stretches = row_count // STRETCH
    query_key = query_key.reshape(row_count, 2, key_heads, DK)
    value_gate = value_gate.reshape(row_count, 2, value_heads, DV)
    delta_query = query_key[:, 0]
    delta_query = (
        delta_query
        * lax.rsqrt(jnp.sum(delta_query * delta_query, axis=-1, keepdims=True) + epsilon)
        * DK ** (-0.5)
    )
    delta_key = query_key[:, 1]
    delta_key = delta_key * lax.rsqrt(
        jnp.sum(delta_key * delta_key, axis=-1, keepdims=True) + epsilon
    )
    query_blocks = split_stretches(
        jnp.repeat(delta_query, group_width, axis=1), value_heads, stretches
    )
    key_blocks = split_stretches(jnp.repeat(delta_key, group_width, axis=1), value_heads, stretches)
    value_blocks = split_stretches(value_gate[:, 0], value_heads, stretches)
    strengths = write_strength.reshape(value_heads, stretches, STRETCH)
    cumulative = jnp.cumsum(log_decay.reshape(value_heads, stretches, STRETCH), axis=-1)
    decays = jnp.exp(cumulative)
    positions = jnp.arange(STRETCH, dtype=jnp.int32)
    lower_inclusive = positions[:, None] >= positions[None, :]
    lower_strict = positions[:, None] > positions[None, :]
    spread = cumulative[..., :, None] - cumulative[..., None, :]
    ratios = jnp.where(lower_inclusive, jnp.exp(jnp.minimum(spread, 0.0)), 0.0)
    key_key = jnp.einsum("hncd,hnsd->hncs", key_blocks, key_blocks, precision=highest)
    coupling = jnp.where(lower_strict, strengths[..., :, None] * ratios * key_key, 0.0)
    system = coupling + jnp.eye(STRETCH, dtype=jnp.float32)
    right_side = jnp.concatenate(
        [(strengths * decays)[..., None] * key_blocks, strengths[..., None] * value_blocks], axis=-1
    )
    solved = lax.linalg.triangular_solve(
        system, right_side, left_side=True, lower=True, unit_diagonal=True
    )
    weight_rows = solved[..., :DK]
    update_rows = solved[..., DK:]
    tail = jnp.exp(cumulative[..., -1:] - cumulative)
    end_decay = decays[..., -1]
    identity = jnp.eye(DK, dtype=jnp.float32)
    transitions = end_decay[..., None, None] * identity - jnp.einsum(
        "hncd,hnc,hnce->hnde", key_blocks, tail, weight_rows, precision=highest
    )
    offsets = jnp.einsum("hncd,hnc,hnce->hnde", key_blocks, tail, update_rows, precision=highest)
    mixing = ratios * jnp.einsum("hncd,hnsd->hncs", query_blocks, key_blocks, precision=highest)

    def compose(running, inputs):
        transition_now, offset_now = inputs
        return (
            (
                jnp.einsum("hde,hef->hdf", transition_now, running[0], precision=highest),
                jnp.einsum("hde,hef->hdf", transition_now, running[1], precision=highest)
                + offset_now,
            ),
            None,
        )

    start_pair = (
        jnp.broadcast_to(identity, (value_heads, DK, DK)),
        jnp.zeros((value_heads, DK, DV), jnp.float32),
    )
    slab_pair, unused_rest = lax.scan(
        compose, start_pair, (jnp.moveaxis(transitions, 1, 0), jnp.moveaxis(offsets, 1, 0))
    )
    slab_transition, slab_offset = slab_pair
    seq_count = lax.axis_size("seq")

    def cycle_turn(counter, incoming):
        finished = (
            jnp.einsum("hde,hef->hdf", slab_transition, incoming, precision=highest) + slab_offset
        )
        passed = passed_along(finished, "seq", 1)
        return jnp.where(seq_index == 0, initial_state, passed)

    entering = lax.fori_loop(0, seq_count - 1, cycle_turn, initial_state)

    def emit_stretch(running_state, inputs):
        query_now, decay_now, weight_now, update_now, mixing_now, transition_now, offset_now = (
            inputs
        )
        projected = jnp.einsum("hcd,hde->hce", query_now, running_state, precision=highest)
        recalled = jnp.einsum("hcd,hde->hce", weight_now, running_state, precision=highest)
        output = decay_now[..., None] * projected + jnp.einsum(
            "hcs,hse->hce", mixing_now, update_now - recalled, precision=highest
        )
        advanced = (
            jnp.einsum("hde,hef->hdf", transition_now, running_state, precision=highest)
            + offset_now
        )
        return (advanced, output)

    stretch_inputs = tuple(
        (
            jnp.moveaxis(array, 1, 0)
            for array in (
                query_blocks,
                decays,
                weight_rows,
                update_rows,
                mixing,
                transitions,
                offsets,
            )
        )
    )
    final_state, stretch_outputs = lax.scan(emit_stretch, entering, stretch_inputs)
    delta_mix = stretch_outputs.transpose(0, 2, 1, 3).reshape(row_count, value_heads, DV)
    gated = delta_mix * inverse_rms(delta_mix) * head_gain * jax.nn.silu(value_gate[:, 1])
    gated = gated.astype(jnp.bfloat16).reshape(row_count, value_heads * DV)
    delta_branch = jnp.dot(gated, delta_output, preferred_element_type=jnp.float32)
    delta_share = lax.psum_scatter(delta_branch, "head", scatter_dimension=1, tiled=True)
    return (hidden + delta_share).astype(jnp.bfloat16)


def solution(mesh):
    return jax.shard_map(
        body,
        mesh=mesh,
        in_specs=(
            P("seq", "head"),
            P("seq", "head"),
            P("seq", None, "head"),
            P("head", None),
            P(),
            P(None, None, "head"),
            P(None, None, "head"),
            P("head", "seq"),
            P("head", "seq"),
            P("head", None, None),
            P(),
            P("head", None),
        ),
        out_specs=P("seq", "head"),
        check_vma=False,
    )
```

profile of v0, /device:TPU:1, one launch (start us, length us, event | category | flops | bytes accessed | tf_op | source)
XLA Modules:
  0.0 917.8 jit_solution(14462025230341080)
XLA Ops:
  12.4 7.5 collective-permute-start.2
  30.5 7.1 collective-permute-start.5
  52.1 14.3 %collective-permute-done.6 = bf16[512,2,128]{2,0,1:T(8,128)(2,1)S(1)} collective-permute-done((bf16[512,2,128]{2,0,1:T(8,128)(2,1)S(1)}, bf16[512,2,128]{2,0,1:T(8,128)(2,1)S(1)}, u32[]{:S(2)}, u32[]{:S(2)}) %collective-permute-start.6) | collective-permute-done | bytes 262176 | tf_op jit(solution)/shard_map/ppermute | solution.py:22
  67.1 10.7 %collective-permute-done.7 = bf16[512,2,128]{2,0,1:T(8,128)(2,1)S(1)} collective-permute-done((bf16[512,2,128]{2,0,1:T(8,128)(2,1)S(1)}, bf16[512,2,128]{2,0,1:T(8,128)(2,1)S(1)}, u32[]{:S(2)}, u32[]{:S(2)}) %collective-permute-start.7) | collective-permute-done | bytes 262176 | tf_op jit(solution)/shard_map/ppermute | solution.py:22
  78.5 5.0 collective-permute-done.8
  85.0 5.4 fusion.28
  90.4 5.8 fusion.27
  96.2 8.4 fusion.44
  117.3 5.3 copy.176
  122.6 6.6 copy.145
  133.7 48.1 %all-reduce.2.cloned.1.call-done = f32[512,2048]{1,0:T(8,128)} async-done(((f32[512,2048]{1,0:T(8,128)}), f32[512,2048]{1,0:T(8,128)}) %all-reduce.2.cloned.1.call-update) | async-done | bytes 4194320 | tf_op jit(solution)/shard_map/psum | solution.py:93
  190.6 5.5 fusion.66
  201.6 158.8 %custom-call.3 = f32[4,8,1,64,64]{3,4,2,1,0:T(8,128)} custom-call(f32[4,8,1,64,64]{4,3,2,1,0:T(8,128)} %fusion.43), custom_call_target="InvertDiagBlocksLowerTriangular" | custom-call | tf_op jit(solution)/shard_map/triangular_solve | solution.py:133
  376.5 23.1 %while.39 = (s32[]{:T(128)}, f32[4,128,128]{2,1,0:T(8,128)S(1)}, f32[4,128,128]{2,1,0:T(8,128)S(1)}, f32[8,4,128,128]{3,2,1,0:T(8,128)}, f32[8,4,128,128]{3,2,1,0:T(8,128)}, /*index=5*/s32[]{:T(128)}, s32[]{:T(128)}) while((s32[]{:T(128)}, f32[4,128,128]{2,1,0:T(8,128)S(1)}, f32[4,128,128]{2,1,0:T(8,128)S(1)}, ...), condition=%wide.region_7.8_spmd.clone, body=%wide.region_6.7_spmd.clone.sunk | while | flops 201457664 | bytes 2885207 | solution.py:162
  405.8 343.2 %while.37 = (s32[]{:T(128)}, f32[4,128,128]{2,1,0:T(8,128)S(1)}, pred[]{:T(512)}, f32[4,128,128]{2,1,0:T(8,128)S(1)}, f32[4,128,128]{2,1,0:T(8,128)S(1)}, /*index=5*/f32[4,128,128]{2,1,0:T(8,128)S(1)}, s32[]{:T(128)}) while((s32[]{:T(128)}, f32[4,128,128]{2,1,0:T(8,128)S(1)}, pred[]{:T(512)}, f32[4,128,128]{2,1,0:T(8,128)S(1)}, ...), condition=%wide.region_9.10_spmd, body=%wide.region_8.9_spmd.sunk | while | flops 100794368 | bytes 3932306 | solution.py:175
  441.5 5.3 collective-permute-start
  451.3 6.0 collective-permute-start
  461.7 6.0 collective-permute-start
  472.3 6.3 collective-permute-start
  484.2 6.6 collective-permute-start
  490.8 5.6 collective-permute-done
  497.5 6.9 collective-permute-start
  504.5 5.5 collective-permute-done
  511.1 5.8 collective-permute-start
  522.2 5.3 collective-permute-start
  531.9 6.3 collective-permute-start
  542.6 6.3 collective-permute-start
  553.4 6.3 collective-permute-start
  564.1 6.0 collective-permute-start
  574.5 6.0 collective-permute-start
  584.9 6.0 collective-permute-start
  595.7 6.3 collective-permute-start
  607.8 6.5 collective-permute-start
  614.3 5.8 collective-permute-done
  621.2 5.7 collective-permute-start
  627.0 5.8 collective-permute-done
  634.0 6.3 collective-permute-start
  646.3 5.9 collective-permute-start
  657.2 5.1 collective-permute-start
  666.8 5.9 collective-permute-start
  677.1 11.4 %collective-permute-start = (f32[4,128,128]{2,1,0:T(8,128)S(1)}, f32[4,128,128]{2,1,0:T(8,128)S(1)}, u32[]{:S(2)}, u32[]{:S(2)}) collective-permute-start(f32[4,128,128]{2,1,0:T(8,128)S(1)} %convolution_add_fusion.6), channel_id=1, source_target_pairs={{0,8},{8,16},{16,24},{24,32},{32,40},{40,48},{48,56},{56,64},{64,7... | collective-permute-start | bytes 786440 | tf_op jit(solution)/shard_map/while/body/eval_jaxpr/ppermute | solution.py:22
  693.0 6.9 collective-permute-start
  704.3 6.3 collective-permute-start
  715.0 6.7 collective-permute-start
  726.2 7.2 collective-permute-start
  737.8 7.2 collective-permute-start
  749.0 47.6 %while.38 = (s32[]{:T(128)}, f32[4,128,128]{2,1,0:T(8,128)S(1)}, f32[8,4,64,128]{3,2,1,0:T(8,128)}, f32[8,4,128,128]{3,2,1,0:T(8,128)}, f32[8,4,128,128]{3,2,1,0...) while((s32[]{:T(128)}, f32[4,128,128]{2,1,0:T(8,128)S(1)}, ...), condition=%wide.region_12.13_spmd, body=%wide.region_11.12_spmd.sunk | while | flops 226656256 | bytes 3283569 | solution.py:206
  809.7 99.1 %reduce-scatter.2.cloned.1.call-done = f32[512,256]{1,0:T(8,128)} async-done(((f32[512,2048]{1,0:T(8,128)}), f32[512,256]{1,0:T(8,128)}) %reduce-scatter.2.cloned.1.call-update) | async-done | bytes 524304 | tf_op jit(solution)/shard_map/reduce_scatter | solution.py:211
  (369 shorter events, 319.0 us)
Async XLA Ops:
  6.5 798.3 %copy-start = (bf16[512,2048]{1,0:T(8,128)(2,1)S(1)}, bf16[512,2048]{1,0:T(8,128)(2,1)}, u32[]{:S(2)}) copy-start(bf16[512,2048]{1,0:T(8,128)(2,1)} %param.29) | copy-start | bytes 6291460
  6.5 175.3 %all-reduce.2.cloned.1.call-start = ((), (), s32[]{:S(2)}) async-start(), calls=%async_computation.1 | async-start | bytes 8388608 | tf_op jit(solution)/shard_map/psum | solution.py:93
  7.7 30.0 %collective-permute-start.1 = (bf16[512,2,128]{2,0,1:T(8,128)(2,1)S(1)}, bf16[512,2,128]{2,0,1:T(8,128)(2,1)}, u32[]{:S(2)}, u32[]{:S(2)}) collective-permute-start(bf16[512,2,128]{2,0,1:T(8,128)(2,1)S(1)} %copy.131), channel_id=1, source_target_pairs={{0,64},{8,72},{16,80},{24,88},{32,96},{40,104},{48,112},{56,120},{... | collective-permute-start | bytes 786440 | tf_op jit(solution)/shard_map/ppermute | solution.py:22
  12.4 28.2 %collective-permute-start.2 = (bf16[512,2,128]{2,0,1:T(8,128)(2,1)S(1)}, bf16[512,2,128]{2,0,1:T(8,128)(2,1)S(1)}, u32[]{:S(2)}, u32[]{:S(2)}) collective-permute-start(bf16[512,2,128]{2,0,1:T(8,128)(2,1)S(1)} %copy.131), channel_id=1, source_target_pairs={{0,56},{8,64},{16,72},{24,80},{32,88},{40,96},{48,104},{56,112},{6... | collective-permute-start | bytes 786440 | tf_op jit(solution)/shard_map/ppermute | solution.py:22
  19.9 26.2 %collective-permute-start.3 = (bf16[512,2,128]{2,0,1:T(8,128)(2,1)S(1)}, bf16[512,2,128]{2,0,1:T(8,128)(2,1)S(1)}, u32[]{:S(2)}, u32[]{:S(2)}) collective-permute-start(bf16[512,2,128]{2,0,1:T(8,128)(2,1)S(1)} %copy.131), channel_id=1, source_target_pairs={{0,48},{8,56},{16,64},{24,72},{32,80},{40,88},{48,96},{56,104},{64... | collective-permute-start | bytes 786440 | tf_op jit(solution)/shard_map/ppermute | solution.py:22
  23.3 27.3 %collective-permute-start.4 = (bf16[512,2,128]{2,0,1:T(8,128)(2,1)S(1)}, bf16[512,2,128]{2,0,1:T(8,128)(2,1)S(1)}, u32[]{:S(2)}, u32[]{:S(2)}) collective-permute-start(bf16[512,2,128]{2,0,1:T(8,128)(2,1)S(1)} %copy.131), channel_id=1, source_target_pairs={{0,40},{8,48},{16,56},{24,64},{32,72},{40,80},{48,88},{56,96},{64,... | collective-permute-start | bytes 786440 | tf_op jit(solution)/shard_map/ppermute | solution.py:22
  30.5 53.8 %copy-start.11 = (bf16[512,2,128]{2,1,0:T(2,128)(2,1)S(1)}, bf16[512,2,128]{2,1,0:T(2,128)(2,1)}, u32[]{:S(2)}) copy-start(bf16[512,2,128]{2,1,0:T(2,128)(2,1)} %param.20) | copy-start | bytes 786436
  30.5 20.9 %collective-permute-start.5 = (bf16[512,2,128]{2,0,1:T(8,128)(2,1)S(1)}, bf16[512,2,128]{2,0,1:T(8,128)(2,1)S(1)}, u32[]{:S(2)}, u32[]{:S(2)}) collective-permute-start(bf16[512,2,128]{2,0,1:T(8,128)(2,1)S(1)} %copy.131), channel_id=1, source_target_pairs={{0,32},{8,40},{16,48},{24,56},{32,64},{40,72},{48,80},{56,88},{64,... | collective-permute-start | bytes 786440 | tf_op jit(solution)/shard_map/ppermute | solution.py:22
  39.4 27.0 %collective-permute-start.6 = (bf16[512,2,128]{2,0,1:T(8,128)(2,1)S(1)}, bf16[512,2,128]{2,0,1:T(8,128)(2,1)S(1)}, u32[]{:S(2)}, u32[]{:S(2)}) collective-permute-start(bf16[512,2,128]{2,0,1:T(8,128)(2,1)S(1)} %copy.131), channel_id=1, source_target_pairs={{0,24},{8,32},{16,40},{24,48},{32,56},{40,64},{48,72},{56,80},{64,... | collective-permute-start | bytes 786440 | tf_op jit(solution)/shard_map/ppermute | solution.py:22
  41.4 43.6 %copy-start.26 = (bf16[512,256]{1,0:T(8,128)(2,1)S(1)}, bf16[512,256]{1,0:T(8,128)(2,1)}, u32[]{:S(2)}) copy-start(bf16[512,256]{1,0:T(8,128)(2,1)} %param.19) | copy-start | bytes 786436
  41.4 36.4 %collective-permute-start.7 = (bf16[512,2,128]{2,0,1:T(8,128)(2,1)S(1)}, bf16[512,2,128]{2,0,1:T(8,128)(2,1)S(1)}, u32[]{:S(2)}, u32[]{:S(2)}) collective-permute-start(bf16[512,2,128]{2,0,1:T(8,128)(2,1)S(1)} %copy.131), channel_id=1, source_target_pairs={{0,16},{8,24},{16,32},{24,40},{32,48},{40,56},{48,64},{56,72},{64,... | collective-permute-start | bytes 786440 | tf_op jit(solution)/shard_map/ppermute | solution.py:22
  46.8 36.7 %collective-permute-start.8 = (bf16[512,2,128]{2,0,1:T(8,128)(2,1)S(1)}, bf16[512,2,128]{2,0,1:T(8,128)(2,1)S(1)}, u32[]{:S(2)}, u32[]{:S(2)}) collective-permute-start(bf16[512,2,128]{2,0,1:T(8,128)(2,1)S(1)} %copy.131), channel_id=1, source_target_pairs={{0,8},{8,16},{16,24},{24,32},{32,40},{40,48},{48,56},{56,64},{64,7... | collective-permute-start | bytes 786440 | tf_op jit(solution)/shard_map/ppermute | solution.py:22
  109.3 799.5 %reduce-scatter.2.cloned.1.call-start = ((), (), s32[]{:S(2)}) async-start(), calls=%async_computation.2 | async-start | bytes 4718592 | tf_op jit(solution)/shard_map/reduce_scatter | solution.py:211
  122.6 9.9 %copy-start.25 = (f32[128]{0:T(128)S(1)}, f32[128]{0:T(128)}, u32[]{:S(2)}) copy-start(f32[128]{0:T(128)} %param.28) | copy-start | bytes 1540
  129.4 55.1 %copy-start.27 = (f32[2048]{0:T(1024)S(1)}, f32[2048]{0:T(1024)}, u32[]{:S(2)}) copy-start(f32[2048]{0:T(1024)} %param.22) | copy-start | bytes 24580
  198.7 172.2 %copy-start.1 = (f32[512,2,2,128]{3,0,2,1:T(8,128)}, f32[512,2,2,128]{3,0,2,1:T(8,128)S(1)}, u32[]{:S(2)}) copy-start(f32[512,2,2,128]{3,0,2,1:T(8,128)S(1)} %broadcast_in_dim.65) | copy-start | bytes 3145732
  376.5 25.3 %copy-start.15 = (pred[64,64]{1,0:T(8,128)(4,1)S(1)}, pred[64,64]{1,0:T(8,128)(4,1)}, u32[]{:S(2)}) copy-start(pred[64,64]{1,0:T(8,128)(4,1)} %get-tuple-element.311) | copy-start | bytes 12292
  406.2 6.5 collective-permute-start
  413.9 8.1 collective-permute-start
  423.1 8.1 collective-permute-start
  432.3 8.1 collective-permute-start
  441.5 8.6 collective-permute-start
  451.3 9.3 %collective-permute-start = (f32[4,128,128]{2,1,0:T(8,128)S(1)}, f32[4,128,128]{2,1,0:T(8,128)S(1)}, u32[]{:S(2)}, u32[]{:S(2)}) collective-permute-start(f32[4,128,128]{2,1,0:T(8,128)S(1)} %convolution_add_fusion.6), channel_id=1, source_target_pairs={{0,8},{8,16},{16,24},{24,32},{32,40},{40,48},{48,56},{56,64},{64,7... | collective-permute-start | bytes 786440 | tf_op jit(solution)/shard_map/while/body/eval_jaxpr/ppermute | solution.py:22
  461.7 9.4 %collective-permute-start = (f32[4,128,128]{2,1,0:T(8,128)S(1)}, f32[4,128,128]{2,1,0:T(8,128)S(1)}, u32[]{:S(2)}, u32[]{:S(2)}) collective-permute-start(f32[4,128,128]{2,1,0:T(8,128)S(1)} %convolution_add_fusion.6), channel_id=1, source_target_pairs={{0,8},{8,16},{16,24},{24,32},{32,40},{40,48},{48,56},{56,64},{64,7... | collective-permute-start | bytes 786440 | tf_op jit(solution)/shard_map/while/body/eval_jaxpr/ppermute | solution.py:22
  472.3 10.8 %collective-permute-start = (f32[4,128,128]{2,1,0:T(8,128)S(1)}, f32[4,128,128]{2,1,0:T(8,128)S(1)}, u32[]{:S(2)}, u32[]{:S(2)}) collective-permute-start(f32[4,128,128]{2,1,0:T(8,128)S(1)} %convolution_add_fusion.6), channel_id=1, source_target_pairs={{0,8},{8,16},{16,24},{24,32},{32,40},{40,48},{48,56},{56,64},{64,7... | collective-permute-start | bytes 786440 | tf_op jit(solution)/shard_map/while/body/eval_jaxpr/ppermute | solution.py:22
  484.2 12.2 %collective-permute-start = (f32[4,128,128]{2,1,0:T(8,128)S(1)}, f32[4,128,128]{2,1,0:T(8,128)S(1)}, u32[]{:S(2)}, u32[]{:S(2)}) collective-permute-start(f32[4,128,128]{2,1,0:T(8,128)S(1)} %convolution_add_fusion.6), channel_id=1, source_target_pairs={{0,8},{8,16},{16,24},{24,32},{32,40},{40,48},{48,56},{56,64},{64,7... | collective-permute-start | bytes 786440 | tf_op jit(solution)/shard_map/while/body/eval_jaxpr/ppermute | solution.py:22
  497.5 12.4 %collective-permute-start = (f32[4,128,128]{2,1,0:T(8,128)S(1)}, f32[4,128,128]{2,1,0:T(8,128)S(1)}, u32[]{:S(2)}, u32[]{:S(2)}) collective-permute-start(f32[4,128,128]{2,1,0:T(8,128)S(1)} %convolution_add_fusion.6), channel_id=1, source_target_pairs={{0,8},{8,16},{16,24},{24,32},{32,40},{40,48},{48,56},{56,64},{64,7... | collective-permute-start | bytes 786440 | tf_op jit(solution)/shard_map/while/body/eval_jaxpr/ppermute | solution.py:22
  511.1 9.9 %collective-permute-start = (f32[4,128,128]{2,1,0:T(8,128)S(1)}, f32[4,128,128]{2,1,0:T(8,128)S(1)}, u32[]{:S(2)}, u32[]{:S(2)}) collective-permute-start(f32[4,128,128]{2,1,0:T(8,128)S(1)} %convolution_add_fusion.6), channel_id=1, source_target_pairs={{0,8},{8,16},{16,24},{24,32},{32,40},{40,48},{48,56},{56,64},{64,7... | collective-permute-start | bytes 786440 | tf_op jit(solution)/shard_map/while/body/eval_jaxpr/ppermute | solution.py:22
  522.2 8.6 collective-permute-start
  531.9 9.6 %collective-permute-start = (f32[4,128,128]{2,1,0:T(8,128)S(1)}, f32[4,128,128]{2,1,0:T(8,128)S(1)}, u32[]{:S(2)}, u32[]{:S(2)}) collective-permute-start(f32[4,128,128]{2,1,0:T(8,128)S(1)} %convolution_add_fusion.6), channel_id=1, source_target_pairs={{0,8},{8,16},{16,24},{24,32},{32,40},{40,48},{48,56},{56,64},{64,7... | collective-permute-start | bytes 786440 | tf_op jit(solution)/shard_map/while/body/eval_jaxpr/ppermute | solution.py:22
  542.6 9.6 %collective-permute-start = (f32[4,128,128]{2,1,0:T(8,128)S(1)}, f32[4,128,128]{2,1,0:T(8,128)S(1)}, u32[]{:S(2)}, u32[]{:S(2)}) collective-permute-start(f32[4,128,128]{2,1,0:T(8,128)S(1)} %convolution_add_fusion.6), channel_id=1, source_target_pairs={{0,8},{8,16},{16,24},{24,32},{32,40},{40,48},{48,56},{56,64},{64,7... | collective-permute-start | bytes 786440 | tf_op jit(solution)/shard_map/while/body/eval_jaxpr/ppermute | solution.py:22
  553.4 9.6 %collective-permute-start = (f32[4,128,128]{2,1,0:T(8,128)S(1)}, f32[4,128,128]{2,1,0:T(8,128)S(1)}, u32[]{:S(2)}, u32[]{:S(2)}) collective-permute-start(f32[4,128,128]{2,1,0:T(8,128)S(1)} %convolution_add_fusion.6), channel_id=1, source_target_pairs={{0,8},{8,16},{16,24},{24,32},{32,40},{40,48},{48,56},{56,64},{64,7... | collective-permute-start | bytes 786440 | tf_op jit(solution)/shard_map/while/body/eval_jaxpr/ppermute | solution.py:22
  564.1 9.3 %collective-permute-start = (f32[4,128,128]{2,1,0:T(8,128)S(1)}, f32[4,128,128]{2,1,0:T(8,128)S(1)}, u32[]{:S(2)}, u32[]{:S(2)}) collective-permute-start(f32[4,128,128]{2,1,0:T(8,128)S(1)} %convolution_add_fusion.6), channel_id=1, source_target_pairs={{0,8},{8,16},{16,24},{24,32},{32,40},{40,48},{48,56},{56,64},{64,7... | collective-permute-start | bytes 786440 | tf_op jit(solution)/shard_map/while/body/eval_jaxpr/ppermute | solution.py:22
  574.5 9.3 %collective-permute-start = (f32[4,128,128]{2,1,0:T(8,128)S(1)}, f32[4,128,128]{2,1,0:T(8,128)S(1)}, u32[]{:S(2)}, u32[]{:S(2)}) collective-permute-start(f32[4,128,128]{2,1,0:T(8,128)S(1)} %convolution_add_fusion.6), channel_id=1, source_target_pairs={{0,8},{8,16},{16,24},{24,32},{32,40},{40,48},{48,56},{56,64},{64,7... | collective-permute-start | bytes 786440 | tf_op jit(solution)/shard_map/while/body/eval_jaxpr/ppermute | solution.py:22
  584.9 9.6 %collective-permute-start = (f32[4,128,128]{2,1,0:T(8,128)S(1)}, f32[4,128,128]{2,1,0:T(8,128)S(1)}, u32[]{:S(2)}, u32[]{:S(2)}) collective-permute-start(f32[4,128,128]{2,1,0:T(8,128)S(1)} %convolution_add_fusion.6), channel_id=1, source_target_pairs={{0,8},{8,16},{16,24},{24,32},{32,40},{40,48},{48,56},{56,64},{64,7... | collective-permute-start | bytes 786440 | tf_op jit(solution)/shard_map/while/body/eval_jaxpr/ppermute | solution.py:22
  595.7 11.0 %collective-permute-start = (f32[4,128,128]{2,1,0:T(8,128)S(1)}, f32[4,128,128]{2,1,0:T(8,128)S(1)}, u32[]{:S(2)}, u32[]{:S(2)}) collective-permute-start(f32[4,128,128]{2,1,0:T(8,128)S(1)} %convolution_add_fusion.6), channel_id=1, source_target_pairs={{0,8},{8,16},{16,24},{24,32},{32,40},{40,48},{48,56},{56,64},{64,7... | collective-permute-start | bytes 786440 | tf_op jit(solution)/shard_map/while/body/eval_jaxpr/ppermute | solution.py:22
  607.8 12.3 %collective-permute-start = (f32[4,128,128]{2,1,0:T(8,128)S(1)}, f32[4,128,128]{2,1,0:T(8,128)S(1)}, u32[]{:S(2)}, u32[]{:S(2)}) collective-permute-start(f32[4,128,128]{2,1,0:T(8,128)S(1)} %convolution_add_fusion.6), channel_id=1, source_target_pairs={{0,8},{8,16},{16,24},{24,32},{32,40},{40,48},{48,56},{56,64},{64,7... | collective-permute-start | bytes 786440 | tf_op jit(solution)/shard_map/while/body/eval_jaxpr/ppermute | solution.py:22
  621.2 11.6 %collective-permute-start = (f32[4,128,128]{2,1,0:T(8,128)S(1)}, f32[4,128,128]{2,1,0:T(8,128)S(1)}, u32[]{:S(2)}, u32[]{:S(2)}) collective-permute-start(f32[4,128,128]{2,1,0:T(8,128)S(1)} %convolution_add_fusion.6), channel_id=1, source_target_pairs={{0,8},{8,16},{16,24},{24,32},{32,40},{40,48},{48,56},{56,64},{64,7... | collective-permute-start | bytes 786440 | tf_op jit(solution)/shard_map/while/body/eval_jaxpr/ppermute | solution.py:22
  634.0 11.2 %collective-permute-start = (f32[4,128,128]{2,1,0:T(8,128)S(1)}, f32[4,128,128]{2,1,0:T(8,128)S(1)}, u32[]{:S(2)}, u32[]{:S(2)}) collective-permute-start(f32[4,128,128]{2,1,0:T(8,128)S(1)} %convolution_add_fusion.6), channel_id=1, source_target_pairs={{0,8},{8,16},{16,24},{24,32},{32,40},{40,48},{48,56},{56,64},{64,7... | collective-permute-start | bytes 786440 | tf_op jit(solution)/shard_map/while/body/eval_jaxpr/ppermute | solution.py:22
  646.3 9.8 %collective-permute-start = (f32[4,128,128]{2,1,0:T(8,128)S(1)}, f32[4,128,128]{2,1,0:T(8,128)S(1)}, u32[]{:S(2)}, u32[]{:S(2)}) collective-permute-start(f32[4,128,128]{2,1,0:T(8,128)S(1)} %convolution_add_fusion.6), channel_id=1, source_target_pairs={{0,8},{8,16},{16,24},{24,32},{32,40},{40,48},{48,56},{56,64},{64,7... | collective-permute-start | bytes 786440 | tf_op jit(solution)/shard_map/while/body/eval_jaxpr/ppermute | solution.py:22
  657.2 8.4 collective-permute-start
  666.8 9.2 %collective-permute-start = (f32[4,128,128]{2,1,0:T(8,128)S(1)}, f32[4,128,128]{2,1,0:T(8,128)S(1)}, u32[]{:S(2)}, u32[]{:S(2)}) collective-permute-start(f32[4,128,128]{2,1,0:T(8,128)S(1)} %convolution_add_fusion.6), channel_id=1, source_target_pairs={{0,8},{8,16},{16,24},{24,32},{32,40},{40,48},{48,56},{56,64},{64,7... | collective-permute-start | bytes 786440 | tf_op jit(solution)/shard_map/while/body/eval_jaxpr/ppermute | solution.py:22
  677.1 14.7 %collective-permute-start = (f32[4,128,128]{2,1,0:T(8,128)S(1)}, f32[4,128,128]{2,1,0:T(8,128)S(1)}, u32[]{:S(2)}, u32[]{:S(2)}) collective-permute-start(f32[4,128,128]{2,1,0:T(8,128)S(1)} %convolution_add_fusion.6), channel_id=1, source_target_pairs={{0,8},{8,16},{16,24},{24,32},{32,40},{40,48},{48,56},{56,64},{64,7... | collective-permute-start | bytes 786440 | tf_op jit(solution)/shard_map/while/body/eval_jaxpr/ppermute | solution.py:22
  693.0 10.1 %collective-permute-start = (f32[4,128,128]{2,1,0:T(8,128)S(1)}, f32[4,128,128]{2,1,0:T(8,128)S(1)}, u32[]{:S(2)}, u32[]{:S(2)}) collective-permute-start(f32[4,128,128]{2,1,0:T(8,128)S(1)} %convolution_add_fusion.6), channel_id=1, source_target_pairs={{0,8},{8,16},{16,24},{24,32},{32,40},{40,48},{48,56},{56,64},{64,7... | collective-permute-start | bytes 786440 | tf_op jit(solution)/shard_map/while/body/eval_jaxpr/ppermute | solution.py:22
  704.3 9.6 %collective-permute-start = (f32[4,128,128]{2,1,0:T(8,128)S(1)}, f32[4,128,128]{2,1,0:T(8,128)S(1)}, u32[]{:S(2)}, u32[]{:S(2)}) collective-permute-start(f32[4,128,128]{2,1,0:T(8,128)S(1)} %convolution_add_fusion.6), channel_id=1, source_target_pairs={{0,8},{8,16},{16,24},{24,32},{32,40},{40,48},{48,56},{56,64},{64,7... | collective-permute-start | bytes 786440 | tf_op jit(solution)/shard_map/while/body/eval_jaxpr/ppermute | solution.py:22
  715.0 10.0 %collective-permute-start = (f32[4,128,128]{2,1,0:T(8,128)S(1)}, f32[4,128,128]{2,1,0:T(8,128)S(1)}, u32[]{:S(2)}, u32[]{:S(2)}) collective-permute-start(f32[4,128,128]{2,1,0:T(8,128)S(1)} %convolution_add_fusion.6), channel_id=1, source_target_pairs={{0,8},{8,16},{16,24},{24,32},{32,40},{40,48},{48,56},{56,64},{64,7... | collective-permute-start | bytes 786440 | tf_op jit(solution)/shard_map/while/body/eval_jaxpr/ppermute | solution.py:22
  726.2 10.5 %collective-permute-start = (f32[4,128,128]{2,1,0:T(8,128)S(1)}, f32[4,128,128]{2,1,0:T(8,128)S(1)}, u32[]{:S(2)}, u32[]{:S(2)}) collective-permute-start(f32[4,128,128]{2,1,0:T(8,128)S(1)} %convolution_add_fusion.6), channel_id=1, source_target_pairs={{0,8},{8,16},{16,24},{24,32},{32,40},{40,48},{48,56},{56,64},{64,7... | collective-permute-start | bytes 786440 | tf_op jit(solution)/shard_map/while/body/eval_jaxpr/ppermute | solution.py:22
  737.8 10.5 %collective-permute-start = (f32[4,128,128]{2,1,0:T(8,128)S(1)}, f32[4,128,128]{2,1,0:T(8,128)S(1)}, u32[]{:S(2)}, u32[]{:S(2)}) collective-permute-start(f32[4,128,128]{2,1,0:T(8,128)S(1)} %convolution_add_fusion.6), channel_id=1, source_target_pairs={{0,8},{8,16},{16,24},{24,32},{32,40},{40,48},{48,56},{56,64},{64,7... | collective-permute-start | bytes 786440 | tf_op jit(solution)/shard_map/while/body/eval_jaxpr/ppermute | solution.py:22
  (51 other events, 84.0 us)
Sparse Core Ops, SparseCore 0:
  109.4 72.3 all-reduce.1
  809.9 98.9 reduce-scatter.1
where the time goes:
time: 931 us; the launch traced here: 918 us
  waiting for transfers between devices  296 us (32%)
  starting transfers between devices  224 us (24%)
  other arithmetic  183 us (20%)
  matrix products  128 us (14%)
  local copies, waits for them, and re-layouts  70.5 us (8%)
  between operations  14.2 us (2%)
    ppermute x39, starting transfers between devices, passed_along(): return lax.ppermute(shard, axis, pairs)  224 us
    another operation x4, other arithmetic, body(): lax.linalg.triangular_solve(system, right_side, left_side=True, lower=Tru...  160 us
    ppermute x39, waiting for transfers between devices, passed_along(): return lax.ppermute(shard, axis, pairs)  148 us
    reduce_scatter x1, waiting for transfers between devices, body(): lax.psum_scatter(delta_branch, 'head', scatter_dimension=1, tiled=True)  99.1 us
    psum x1, waiting for transfers between devices, body(): hidden_full = lax.psum(branch + placed, 'head')  48.1 us
    unnamed x68, local copies, waits for them, and re-layouts  22.7 us
    while x86, local copies, waits for them, and re-layouts  22.2 us
  transfers between devices with their start and end apart: 41, of which 37 were waited for; matrix products, arithmetic and copies ran while one was open for 4% of the time, Pallas kernels for 0%

commit v1 on v0

v1 whole, which is shorter than its diff:
```python
import math

import jax
import jax.numpy as jnp
from jax import lax
from jax.experimental import pallas as pl
from jax.experimental.pallas import tpu as pltpu
from jax.sharding import PartitionSpec as P

DK = 128
DV = 128
ATTEND_HEAD_SIZE = 128
WINDOW_KEYS = 4096
CHUNK = 128
ROWS = 512
KEY_HEADS = 2
VALUE_HEADS = 4
Z = 8
Y = 4
HALF = DV // 2
MESSAGE = DK + HALF + 16
MESH = pl.DeviceIdType.MESH
f32 = jnp.float32
bf16 = jnp.bfloat16


epsilon = 1e-06


def passed_along(shard, axis, by):
    length = lax.axis_size(axis)
    pairs = [(i, i + by) for i in range(length) if 0 <= i + by < length]
    return lax.ppermute(shard, axis, pairs)


def inverse_rms(values):
    return lax.rsqrt(jnp.mean(values * values, axis=-1, keepdims=True) + epsilon)


def attend(queries, key_value_pairs, seq_index):
    row_count = queries.shape[0]
    reach_pieces = WINDOW_KEYS // row_count
    kv_heads = key_value_pairs.shape[2] // ATTEND_HEAD_SIZE
    query_heads = queries.shape[1] // ATTEND_HEAD_SIZE
    group_width = query_heads // kv_heads
    earlier_rows = jnp.concatenate(
        [passed_along(key_value_pairs, "seq", distance) for distance in range(reach_pieces, 0, -1)],
        axis=0,
    )
    window_matrix = jnp.concatenate([earlier_rows, key_value_pairs], axis=0)
    window_length = window_matrix.shape[0]
    key_matrix = window_matrix[:, 0].reshape(window_length, kv_heads, ATTEND_HEAD_SIZE)
    value_matrix = window_matrix[:, 1].reshape(window_length, kv_heads, ATTEND_HEAD_SIZE)
    query_matrix = queries.reshape(row_count, kv_heads, group_width, ATTEND_HEAD_SIZE)
    query_pos = seq_index * row_count + jnp.arange(row_count, dtype=jnp.int32)
    key_pos = (seq_index - reach_pieces) * row_count + jnp.arange(window_length, dtype=jnp.int32)
    distance_grid = query_pos[:, None] - key_pos[None, :]
    allowed = (distance_grid >= 0) & (distance_grid < WINDOW_KEYS) & (key_pos[None, :] >= 0)
    scores = jnp.einsum(
        "qhgd,khd->hgqk", query_matrix, key_matrix, preferred_element_type=jnp.float32
    ) * (1.0 / math.sqrt(ATTEND_HEAD_SIZE))
    scores = jnp.where(allowed, scores, -jnp.inf)
    row_peak = jnp.max(scores, axis=-1, keepdims=True)
    exponentials = jnp.exp(scores - row_peak)
    weights = (exponentials / jnp.sum(exponentials, axis=-1, keepdims=True)).astype(jnp.bfloat16)
    mixed_rows = jnp.einsum(
        "hgqk,khd->qhgd", weights, value_matrix, preferred_element_type=jnp.float32
    )
    return mixed_rows.astype(jnp.bfloat16).reshape(row_count, query_heads * ATTEND_HEAD_SIZE)


def dot(a, b, contract=((1,), (0,))):
    return lax.dot_general(a, b, (contract, ((), ())), preferred_element_type=f32)


def mm(a, b):
    return dot(a.astype(bf16), b.astype(bf16))


def mm_nt(a, b):
    return dot(a.astype(bf16), b.astype(bf16), ((1,), (1,)))


def split(a):
    high = a.astype(bf16)
    return high, (a - high.astype(f32)).astype(bf16)


def mm2(a, b):
    high, low = split(a)
    return dot(high, b) + dot(low, b)


def mm3(a, b):
    high, low = split(a)
    b_high, b_low = split(b)
    return dot(high, b_high) + dot(low, b_high) + dot(high, b_low)


def grid_of(rows, columns):
    shape = (rows, columns)
    return lax.broadcasted_iota(jnp.int32, shape, 0), lax.broadcasted_iota(jnp.int32, shape, 1)


def three_rows(a):
    high = a.astype(bf16).astype(f32)
    mid = (a - high).astype(bf16).astype(f32)
    low = a - high - mid
    row = lax.broadcasted_iota(jnp.int32, (16, a.shape[1]), 0)
    return jnp.where(row == 0, high, jnp.where(row == 1, mid, jnp.where(row == 2, low, 0.0))).astype(bf16)


def sum_rows(block):
    return jnp.sum(block.astype(f32), axis=0, keepdims=True)


def local_kernel(qk_ref, vg_ref, packed_ref, zero_ref, lead_ref, message_ref, prefix):
    i, j = grid_of(CHUNK, CHUNK)
    inclusive, strict = i >= j, i > j
    eye = (i == j).astype(f32)
    lower = inclusive.astype(f32)
    for h in range(VALUE_HEADS):
        prefix[h] = jnp.concatenate([eye, jnp.zeros_like(eye)], axis=1)
    per_turn = 2

    def turn(t, carry):
        items = []
        for u in range(per_turn):
            rows = pl.ds(pl.multiple_of((t * per_turn + u) * CHUNK, CHUNK), CHUNK)
            packed = packed_ref[:, rows]
            columns = packed.T
            total_row = lax.dot_general(
                packed, lower, (((1,), (1,)), ((), ())),
                precision=lax.Precision.HIGHEST, preferred_element_type=f32)
            total_col = lax.dot_general(
                lower, columns, (((1,), (0,)), ((), ())),
                precision=lax.Precision.HIGHEST, preferred_element_type=f32)
            keys = []
            for kh in range(KEY_HEADS):
                q = qk_ref[rows, kh * DK:(kh + 1) * DK]
                q = q * lax.rsqrt(jnp.sum(q * q, axis=-1, keepdims=True) + epsilon) * DK ** (-0.5)
                at = KEY_HEADS * DK + kh * DK
                k = qk_ref[rows, at:at + DK]
                k = k * lax.rsqrt(jnp.sum(k * k, axis=-1, keepdims=True) + epsilon)
                kb = k.astype(bf16)
                keys.append((q, kb, k.T, mm_nt(kb, kb), mm_nt(q, kb)))
            for h in range(VALUE_HEADS):
                q, k, k_t, key_key, query_key = keys[h // 2]
                cum_col, cum_row = total_col[:, h:h + 1], total_row[h:h + 1, :]
                strength_col = columns[:, VALUE_HEADS + h:VALUE_HEADS + h + 1]
                strength_row = packed[VALUE_HEADS + h:VALUE_HEADS + h + 1, :]
                ratio = jnp.where(inclusive, jnp.exp(jnp.minimum(cum_col - cum_row, 0.0)), 0.0)
                coupling = jnp.where(strict, strength_col * ratio * key_key, 0.0)
                items.append(dict(
                    h=h, rows=rows, q=q, k=k, k_t=k_t, coupling=coupling, mixing=ratio * query_key,
                    cum_col=cum_col, cum_row=cum_row, strength_row=strength_row,
                    inverse=eye - jnp.where((i // 2) == (j // 2), coupling, 0.0)))
        size = 2
        while size < CHUNK:
            level = ((i // (2 * size)) == (j // (2 * size))) & ((i // size) != (j // size))
            for it in items:
                it["half"] = mm(jnp.where(level, it["coupling"], 0.0), it["inverse"])
            for it in items:
                it["inverse"] = it["inverse"] - mm(it["inverse"], it["half"])
            size *= 2
        for it in items:
            scaled = it["inverse"] * it["strength_row"]
            v = vg_ref[it["rows"], it["h"] * DV:(it["h"] + 1) * DV]
            w = mm(scaled * jnp.exp(it["cum_row"]), it["k"])
            u = mm(scaled, v)
            it["wu"] = jnp.concatenate([w, u], axis=1).astype(bf16)
        for it in items:
            mixed = mm(it["mixing"], it["wu"])
            it["lead"] = jnp.exp(it["cum_col"]) * it["q"] - mixed[:, :DK]
            it["own"] = mixed[:, DK:]
            end = it["cum_row"][:, CHUNK - 1:]
            it["end"] = jnp.exp(end)
            it["step"] = mm(it["k_t"] * jnp.exp(end - it["cum_row"]), it["wu"])
        for it in items:
            h = it["h"]
            before = prefix[h]
            out = mm(it["lead"], before)
            lead_ref[it["rows"], h * DK:(h + 1) * DK] = out[:, :DK].astype(bf16)
            zero_ref[it["rows"], h * DV:(h + 1) * DV] = out[:, DK:] + it["own"]
            offset = jnp.concatenate([jnp.zeros((DK, DK), f32), it["step"][:, DK:]], axis=1)
            prefix[h] = it["end"] * before - mm(it["step"][:, :DK], before) + offset
        return carry

    lax.fori_loop(0, ROWS // CHUNK // per_turn, turn, 0)
    slab_decay = jnp.exp(jnp.sum(packed_ref[...], axis=1, keepdims=True))
    for h in range(VALUE_HEADS):
        decay = slab_decay[h:h + 1, :]
        change = (prefix[h, :, :DK] - decay * eye).T.astype(bf16)
        offset = prefix[h, :, DK:].T.astype(bf16)
        tail = three_rows(jnp.broadcast_to(decay, (1, DK)))
        for c in range(2):
            message_ref[2 * h + c, :DK] = change
            message_ref[2 * h + c, DK:DK + HALF] = offset[c * HALF:(c + 1) * HALF]
            message_ref[2 * h + c, DK + HALF:] = tail


def local_part(query_key, value_gate, packed):
    return pl.pallas_call(
        local_kernel,
        out_shape=(
            jax.ShapeDtypeStruct((ROWS, VALUE_HEADS * DV), f32),
            jax.ShapeDtypeStruct((ROWS, VALUE_HEADS * DK), bf16),
            jax.ShapeDtypeStruct((Z, MESSAGE, DK), bf16),
        ),
        in_specs=[pl.BlockSpec(memory_space=pltpu.VMEM)] * 3,
        out_specs=[pl.BlockSpec(memory_space=pltpu.VMEM)] * 3,
        scratch_shapes=[pltpu.VMEM((VALUE_HEADS, DK, DK + DV), f32)],
        compiler_params=pltpu.CompilerParams(vmem_limit_bytes=48 * 2**20),
        name="delta_local",
    )(query_key, value_gate, packed)


FAR_FIRST = (4, 3, 5, 2, 6, 1, 7)


def scan_kernel(message_ref, initial_ref, out_ref, row, total, column, prefix, first, back, landed,
                row_send, row_recv, col_send, col_recv, back_send, back_recv):
    s = lax.axis_index("seq")
    y, z = s // Z, s % Z

    def in_row(d):
        return {"seq": y * Z + (z + d) % Z}

    def in_column(d):
        return {"seq": ((y + d) % Y) * Z + z}

    barrier = pltpu.get_barrier_semaphore()
    for d in range(1, Z):
        pl.semaphore_signal(barrier, inc=1, device_id=in_row(d), device_id_type=MESH)
    for d in range(1, Y):
        pl.semaphore_signal(barrier, inc=1, device_id=in_column(d), device_id_type=MESH)
    pl.semaphore_wait(barrier, Z - 1 + Y - 1)

    sends = []
    for d in FAR_FIRST:
        copy = pltpu.make_async_remote_copy(
            src_ref=message_ref.at[(z + d) % Z], dst_ref=row.at[z], send_sem=row_send.at[d],
            recv_sem=row_recv.at[d], device_id=in_row(d), device_id_type=MESH)
        copy.start()
        sends.append(copy)
    row[z] = message_ref[z]
    first[...] = initial_ref[z // 2].T
    i, j = grid_of(DK + HALF, DK)
    x = (i == j).astype(f32)
    decay = jnp.ones((1, DK), f32)
    for copy in sends:
        copy.wait()
    zero = jnp.zeros((DK, DK), f32)
    for place in range(Z):
        prefix[place] = x
        a = sum_rows(row[place, DK + HALF:])
        offset = jnp.concatenate([zero, row[place, DK:DK + HALF].astype(f32)], axis=0)
        x = a * x + mm2(x, row[place, :DK]) + offset
        decay = decay * a
    total[:DK + HALF] = jnp.where(i == j, x - decay, x).astype(bf16)
    total[DK + HALF:] = three_rows(decay)
    sends = []
    for d in (2, 1, 3):
        copy = pltpu.make_async_remote_copy(
            src_ref=total, dst_ref=column.at[y], send_sem=col_send.at[d], recv_sem=col_recv.at[d],
            device_id=in_column(d), device_id_type=MESH)
        copy.start()
        sends.append(copy)
    column[y] = total[...]
    state = first[pl.ds(pl.multiple_of((z % 2) * HALF, HALF), HALF), :]
    for copy in sends:
        copy.wait()
    for place in range(Y - 1):
        a = sum_rows(column[place, DK + HALF:])
        after = a * state + mm2(state, column[place, :DK]) + column[place, DK:DK + HALF].astype(f32)
        state = jnp.where(place < y, after, state)
    for place in range(Z):
        entering = mm3(state, prefix[place, :DK]) + prefix[place, DK:]
        back[place] = entering.astype(bf16)
    sends = []
    for d in FAR_FIRST:
        copy = pltpu.make_async_remote_copy(
            src_ref=back.at[(z + d) % Z], dst_ref=landed.at[z], send_sem=back_send.at[d],
            recv_sem=back_recv.at[d], device_id=in_row(d), device_id_type=MESH)
        copy.start()
        sends.append(copy)
    landed[z] = back[z]
    for copy in sends:
        copy.wait()
    out_ref[...] = landed[...]


def entering_states(messages, initial_state):
    dma = pltpu.SemaphoreType.DMA
    return pl.pallas_call(
        scan_kernel,
        out_shape=jax.ShapeDtypeStruct((Z, HALF, DK), bf16),
        in_specs=[pl.BlockSpec(memory_space=pltpu.VMEM)] * 2,
        out_specs=pl.BlockSpec(memory_space=pltpu.VMEM),
        scratch_shapes=[
            pltpu.VMEM((Z, MESSAGE, DK), bf16),
            pltpu.VMEM((MESSAGE, DK), bf16),
            pltpu.VMEM((Y, MESSAGE, DK), bf16),
            pltpu.VMEM((Z, DK + HALF, DK), f32),
            pltpu.VMEM((DV, DK), f32),
            pltpu.VMEM((Z, HALF, DK), bf16),
            pltpu.VMEM((Z, HALF, DK), bf16),
            dma((Z,)), dma((Z,)), dma((Y,)), dma((Y,)), dma((Z,)), dma((Z,)),
        ],
        compiler_params=pltpu.CompilerParams(
            collective_id=1, has_side_effects=True, vmem_limit_bytes=32 * 2**20),
        name="delta_scan",
    )(messages, initial_state)


def body(
    residual,
    queries,
    key_value_pairs,
    attention_out,
    norm_gain,
    query_key_weight,
    value_gate_weight,
    write_strength,
    log_decay,
    initial_state,
    head_gain,
    delta_output,
):
    row_count = residual.shape[0]
    share_width = residual.shape[1]
    model_width = norm_gain.shape[0]
    seq_index = lax.axis_index("seq")
    head_index = lax.axis_index("head")
    attention_mix = attend(queries, key_value_pairs, seq_index)
    branch = jnp.dot(attention_mix, attention_out, preferred_element_type=jnp.float32)
    query_cols = query_key_weight.shape[2]
    value_cols = value_gate_weight.shape[2]
    flat_query_key = query_key_weight.reshape(model_width, 2 * query_cols)
    flat_value_gate = value_gate_weight.reshape(model_width, 2 * value_cols)
    placed = lax.dynamic_update_slice_in_dim(
        jnp.zeros_like(branch), residual.astype(jnp.float32), head_index * share_width, 1
    )
    hidden_full = lax.psum(branch + placed, "head")
    hidden = lax.dynamic_slice_in_dim(hidden_full, head_index * share_width, share_width, 1)
    normed = (hidden_full * inverse_rms(hidden_full) * norm_gain).astype(jnp.bfloat16)
    query_key = jnp.dot(normed, flat_query_key, preferred_element_type=jnp.float32)
    value_gate = jnp.dot(normed, flat_value_gate, preferred_element_type=jnp.float32)
    value_heads = value_cols // DV
    packed = jnp.concatenate([log_decay, write_strength], axis=0)
    zero_part, lead, messages = local_part(query_key, value_gate, packed)
    states = entering_states(messages, initial_state).reshape(value_heads, DV, DK)
    met = jnp.einsum(
        "thd,hed->the", lead.reshape(row_count, value_heads, DK), states, preferred_element_type=f32
    )
    delta_mix = zero_part.reshape(row_count, value_heads, DV) + met
    gate = value_gate[:, value_cols:].reshape(row_count, value_heads, DV)
    gated = delta_mix * inverse_rms(delta_mix) * head_gain * jax.nn.silu(gate)
    gated = gated.astype(jnp.bfloat16).reshape(row_count, value_heads * DV)
    delta_branch = jnp.dot(gated, delta_output, preferred_element_type=jnp.float32)
    delta_share = lax.psum_scatter(delta_branch, "head", scatter_dimension=1, tiled=True)
    return (hidden + delta_share).astype(jnp.bfloat16)


def solution(mesh):
    return jax.shard_map(
        body,
        mesh=mesh,
        in_specs=(
            P("seq", "head"),
            P("seq", "head"),
            P("seq", None, "head"),
            P("head", None),
            P(),
            P(None, None, "head"),
            P(None, None, "head"),
            P("head", "seq"),
            P("head", "seq"),
            P("head", None, None),
            P(),
            P("head", None),
        ),
        out_specs=P("seq", "head"),
        check_vma=False,
    )
```

time: 931 us -> 288 us (0.31); the launches traced: 918 us -> 285 us
  starting transfers between devices: 224 us -> 33.9 us
  other arithmetic: 183 us -> 19 us
  waiting for transfers between devices: 296 us -> 132 us
  matrix products: 128 us -> 28.5 us
  local copies, waits for them, and re-layouts: 70.5 us -> 24.8 us
  Pallas kernels: 0 us -> 32.7 us
    ppermute x39 -> x8, starting transfers between devices: 224 us -> 33.6 us  [passed_along(): return lax.ppermute(shard, axis, pairs)]
    another operation x5 -> x0, other arithmetic: 161 us -> none  [the longest x4 160 us: body(): lax.linalg.triangular_solve(system, right_side, left_side=True, lower=Tru...]
    ppermute x39 -> x8, waiting for transfers between devices: 148 us -> 27.9 us  [passed_along(): return lax.ppermute(shard, axis, pairs)]
    dot_general x83 -> x1, matrix products: 96 us -> 2.73 us  [body(): jnp.einsum('thd,hed->the', lead.reshape(row_count, value_heads, DK), stat...]
    reduce_scatter x1, waiting for transfers between devices: 99.1 us -> 38.5 us  [body(): lax.psum_scatter(delta_branch, 'head', scatter_dimension=1, tiled=True)]
    pallas_call x0 -> x2, Pallas kernels: none -> 32.7 us  [the longest x1 25.5 us: entering_states(): pl.pallas_call(scan_kernel, out_shape=jax.ShapeDtypeStruct((Z, HALF, DK),...]
    while x86 -> x0, local copies, waits for them, and re-layouts: 22.2 us -> none
    psum x1, waiting for transfers between devices: 48.1 us -> 65.9 us  [body(): hidden_full = lax.psum(branch + placed, 'head')]
  transfers between devices with their start and end apart: 41 -> 10, of which waited for: 37 -> 6; matrix products, arithmetic and copies ran while one was open for 4% -> 6% of each run, Pallas kernels for 0% -> 0%
where the time goes in v1:
time: 288 us; the launch traced here: 285 us
  waiting for transfers between devices  132 us (46%)
  starting transfers between devices  33.9 us (12%)
  Pallas kernels  32.7 us (11%)
  matrix products  28.5 us (10%)
  local copies, waits for them, and re-layouts  24.8 us (9%)
  other arithmetic  19 us (7%)
  between operations  13.6 us (5%)
    psum x1, waiting for transfers between devices, body(): hidden_full = lax.psum(branch + placed, 'head')  65.9 us
    reduce_scatter x1, waiting for transfers between devices, body(): lax.psum_scatter(delta_branch, 'head', scatter_dimension=1, tiled=True)  38.5 us
    ppermute x8, starting transfers between devices, passed_along(): return lax.ppermute(shard, axis, pairs)  33.6 us
    ppermute x8, waiting for transfers between devices, passed_along(): return lax.ppermute(shard, axis, pairs)  27.9 us
    pallas_call x1, Pallas kernels, entering_states(): pl.pallas_call(scan_kernel, out_shape=jax.ShapeDtypeStruct((Z, HALF, DK),...  25.5 us
    unnamed x45, local copies, waits for them, and re-layouts  20.1 us
    dot_general x1, matrix products, attend(): jnp.einsum('hgqk,khd->qhgd', weights, value_matrix, preferred_element_typ...  8.39 us
    pallas_call x1, Pallas kernels, local_part(): pl.pallas_call(local_kernel, out_shape=(jax.ShapeDtypeStruct((ROWS, VALUE...  7.21 us
  transfers between devices with their start and end apart: 10, of which 6 were waited for; matrix products, arithmetic and copies ran while one was open for 6% of the time, Pallas kernels for 0%

profile of v1, /device:TPU:1, one launch (start us, length us, event | category | flops | bytes accessed | tf_op | source)
XLA Modules:
  0.0 284.9 jit_solution(2277989954247271112)
XLA Ops:
  6.5 1.1 copy.13
  7.7 4.7 %collective-permute-start = (bf16[512,2,128]{2,0,1:T(8,128)(2,1)S(1)}, bf16[512,2,128]{2,0,1:T(8,128)(2,1)}, u32[]{:S(2)}, u32[]{:S(2)}) collective-permute-start(bf16[512,2,128]{2,0,1:T(8,128)(2,1)S(1)} %copy.13), channel_id=1, source_target_pairs={{0,64},{8,72},{16,80},{24,88},{32,96},{40,104},{48,112},{56,120},{... | collective-permute-start | bytes 786440 | tf_op jit(solution)/shard_map/ppermute | solution.py:33
  12.4 8.2 %collective-permute-start.1 = (bf16[512,2,128]{2,0,1:T(8,128)(2,1)S(1)}, bf16[512,2,128]{2,0,1:T(8,128)(2,1)}, u32[]{:S(2)}, u32[]{:S(2)}) collective-permute-start(bf16[512,2,128]{2,0,1:T(8,128)(2,1)S(1)} %copy.13), channel_id=1, source_target_pairs={{0,56},{8,64},{16,72},{24,80},{32,88},{40,96},{48,104},{56,112},{6... | collective-permute-start | bytes 786440 | tf_op jit(solution)/shard_map/ppermute | solution.py:33
  20.6 3.4 %collective-permute-start.2 = (bf16[512,2,128]{2,0,1:T(8,128)(2,1)S(1)}, bf16[512,2,128]{2,0,1:T(8,128)(2,1)S(1)}, u32[]{:S(2)}, u32[]{:S(2)}) collective-permute-start(bf16[512,2,128]{2,0,1:T(8,128)(2,1)S(1)} %copy.13), channel_id=1, source_target_pairs={{0,48},{8,56},{16,64},{24,72},{32,80},{40,88},{48,96},{56,104},{64... | collective-permute-start | bytes 786440 | tf_op jit(solution)/shard_map/ppermute | solution.py:33
  24.0 1.8 collective-permute-start.3
  25.8 7.0 %collective-permute-start.4 = (bf16[512,2,128]{2,0,1:T(8,128)(2,1)S(1)}, bf16[512,2,128]{2,0,1:T(8,128)(2,1)S(1)}, u32[]{:S(2)}, u32[]{:S(2)}) collective-permute-start(bf16[512,2,128]{2,0,1:T(8,128)(2,1)S(1)} %copy.13), channel_id=1, source_target_pairs={{0,32},{8,40},{16,48},{24,56},{32,64},{40,72},{48,80},{56,88},{64,... | collective-permute-start | bytes 786440 | tf_op jit(solution)/shard_map/ppermute | solution.py:33
  32.9 4.6 %fusion.5 = pred[512,4608]{0,1:T(8,128)(4,1)} fusion(s32[4608]{0:T(1024)S(1)} %iota_add_fusion, s32[512]{0:T(512)S(1)} %iota_add_fusion.1, pred[4608]{0:T(1024)(128)(4,1)S(1)} %broadcast_compare_fusion), kind=kLoop, calls=%fused_computation.10 | loop fusion | flops 11796480 | bytes 2384384 | tf_op jit(solution)/shard_map/and | solution.py:58
  37.5 1.3 collective-permute-start.5
  38.8 1.7 constant_dynamic-update-slice_fusion.8
  40.5 4.6 %collective-permute-start.6 = (bf16[512,2,128]{2,0,1:T(8,128)(2,1)S(1)}, bf16[512,2,128]{2,0,1:T(8,128)(2,1)S(1)}, u32[]{:S(2)}, u32[]{:S(2)}) collective-permute-start(bf16[512,2,128]{2,0,1:T(8,128)(2,1)S(1)} %copy.13), channel_id=1, source_target_pairs={{0,16},{8,24},{16,32},{24,40},{32,48},{40,56},{48,64},{56,72},{64,... | collective-permute-start | bytes 786440 | tf_op jit(solution)/shard_map/ppermute | solution.py:33
  45.1 1.7 constant_dynamic-update-slice_fusion.7
  46.8 2.6 collective-permute-start.7
  49.5 0.7 constant_dynamic-update-slice_fusion.6
  50.2 0.4 collective-permute-done.3
  50.6 0.7 constant_dynamic-update-slice_fusion.5
  51.3 0.7 constant_dynamic-update-slice_fusion.4
  52.1 13.1 %collective-permute-done.5 = bf16[512,2,128]{2,0,1:T(8,128)(2,1)S(1)} collective-permute-done((bf16[512,2,128]{2,0,1:T(8,128)(2,1)S(1)}, bf16[512,2,128]{2,0,1:T(8,128)(2,1)S(1)}, u32[]{:S(2)}, u32[]{:S(2)}) %collective-permute-start.5) | collective-permute-done | bytes 262176 | tf_op jit(solution)/shard_map/ppermute | solution.py:33
  65.1 0.7 constant_dynamic-update-slice_fusion.3
  65.8 9.6 %collective-permute-done.6 = bf16[512,2,128]{2,0,1:T(8,128)(2,1)S(1)} collective-permute-done((bf16[512,2,128]{2,0,1:T(8,128)(2,1)S(1)}, bf16[512,2,128]{2,0,1:T(8,128)(2,1)S(1)}, u32[]{:S(2)}, u32[]{:S(2)}) %collective-permute-start.6) | collective-permute-done | bytes 262176 | tf_op jit(solution)/shard_map/ppermute | solution.py:33
  75.4 0.7 constant_dynamic-update-slice_fusion.2
  76.1 4.9 %collective-permute-done.7 = bf16[512,2,128]{2,0,1:T(8,128)(2,1)S(1)} collective-permute-done((bf16[512,2,128]{2,0,1:T(8,128)(2,1)S(1)}, bf16[512,2,128]{2,0,1:T(8,128)(2,1)S(1)}, u32[]{:S(2)}, u32[]{:S(2)}) %collective-permute-start.7) | collective-permute-done | bytes 262176 | tf_op jit(solution)/shard_map/ppermute | solution.py:33
  81.0 0.7 constant_dynamic-update-slice_fusion.1
  81.8 0.8 constant_dynamic-update-slice_fusion
  82.5 5.5 %fusion.1 = (f32[2,512]{1,0:T(2,128)S(1)}, f32[4608,512,2]{1,0,2:T(8,128)S(1)}) fusion(pred[512,4608]{0,1:T(8,128)(4,1)} %fusion.5, bf16[4608,2,128]{2,0,1:T(8,128)(2,1)} %constant_dynamic-update-slice_fusion, bf16[512,256]{1,0:T(8,128)(2,1)} %param.13), kind=kOutput, calls=%fused_computation.4 | convolution fusion | flops 1222114304 | bytes 22679552 | tf_op jit(solution)/shard_map/qhgd,khd->hgqk/dot_general | solution.py:59
  88.0 5.8 %fusion = f32[2,512]{1,0:T(2,128)S(1)} fusion(f32[4608,512,2]{1,0,2:T(8,128)S(1)} %get-tuple-element.12, f32[2,512]{1,0:T(2,128)S(1)} %get-tuple-element.11, pred[512,4608]{0,1:T(8,128)(4,1)} %fusion.5), kind=kLoop, calls=%fused_computation.3 | loop fusion | flops 18873344 | bytes 21241856 | tf_op jit(solution)/shard_map/reduce_sum | solution.py:65
  93.8 8.4 %fusion.7 = bf16[128,2,512]{2,0,1:T(8,128)(2,1)S(1)} fusion(f32[2,512]{1,0:T(2,128)S(1)} %fusion, f32[2,512]{1,0:T(2,128)S(1)} %get-tuple-element.11, f32[4608,512,2]{1,0,2:T(8,128)S(1)} %get-tuple-element.12, pred[512,4608]{0,1:T(8,128)(4,1)} %fusion.5, bf16[4608,2,128]{2,0,1:T(8,128)(2,1)} %constant_dynamic-update-slice_fusion), kind=kOutput, calls=%fused_computation.15 | convolution fusion | flops 1231683584 | bytes 22683648 | tf_op jit(solution)/shard_map/hgqk,khd->qhgd/dot_general | solution.py:66
  102.2 2.7 fusion.19
  104.9 1.9 add_dynamic-update-slice_fusion
  107.1 3.5 %copy.36 = bf16[256,8,2,256]{3,1,2,0:T(8,128)(2,1)} copy(bf16[256,8,2,256]{3,2,1,0:T(2,128)(2,1)} %bitcast.78) | data formatting | bytes 4194304
  110.6 3.2 %copy.37 = bf16[256,8,2,512]{3,1,2,0:T(8,128)(2,1)} copy(bf16[256,8,2,512]{3,2,1,0:T(2,128)(2,1)S(1)} %bitcast.74) | data formatting | bytes 8388608
  113.8 65.9 %all-reduce.2.cloned.1.call-done = f32[512,2048]{1,0:T(8,128)} async-done(((f32[512,2048]{1,0:T(8,128)}), f32[512,2048]{1,0:T(8,128)}) %all-reduce.2.cloned.1.call-update) | async-done | bytes 4194320 | tf_op jit(solution)/shard_map/psum | solution.py:344
  179.8 2.7 multiply_reduce_fusion
  182.5 0.7 copy-done.7
  183.2 4.7 %fusion.17.vg_ref = f32[512,1024]{1,0:T(8,128)S(1)} fusion(bf16[2048,1024]{1,0:T(8,128)(2,1)} %bitcast.75, f32[512,2048]{1,0:T(8,128)S(1)} %copy-done.7, f32[2048]{0:T(1024)S(1)} %copy-done.16, f32[512]{0:T(512)S(1)} %add_rsqrt_fusion.1), kind=kOutput, calls=%fused_computation.44 | convolution fusion | flops 2150629376 | bytes 10496000 | tf_op jit(solution)/shard_map/dot_general | solution.py:348
  187.9 1.3 fusion.18.qk_ref
  189.3 7.2 %delta_local.1 = (f32[512,512]{1,0:T(8,128)S(1)}, bf16[512,512]{1,0:T(8,128)(2,1)S(1)}, bf16[8,208,128]{2,1,0:T(8,128)(2,1)S(1)}) custom-call(f32[512,512]{1,0:T(8,128)S(1)} %fusion.18.qk_ref, f32[512,1024]{1,0:T(8,128)S(1)} %fusion.17.vg_ref, f32[8,512]{1,0:T(8,128)S(1)} %pad_maximum_fusion.packed_ref), custom_call_target="tpu_custom_call" | custom-call | tf_op jit(solution)/shard_map/delta_local/pallas_call | solution.py:203
  196.5 1.0 copy-done.2
  197.5 0.8 copy-done.3
  198.4 0.8 copy-done.4
  199.2 2.6 copy.32
  201.8 1.0 copy-done.5
  202.8 25.5 %delta_scan.1 = bf16[8,64,128]{2,1,0:T(8,128)(2,1)S(1)} custom-call(bf16[8,208,128]{2,1,0:T(8,128)(2,1)S(1)} %copy-done.5, f32[4,128,128]{2,1,0:T(8,128)S(1)} %copy-done.6), custom_call_target="tpu_custom_call" | custom-call | tf_op jit(solution)/shard_map/delta_scan/pallas_call | solution.py:295
  228.4 2.7 multiply_reduce_fusion.1
  231.1 1.3 copy.33
  232.4 1.9 multiply_convert_fusion.1
  234.4 3.3 %fusion.20 = f32[512,2048]{1,0:T(8,128)} fusion(bf16[512,512]{0,1:T(8,128)(2,1)S(1)} %bitcast.80, bf16[512,2048]{1,0:T(8,128)(2,1)S(1)} %copy-done), kind=kOutput, calls=%fused_computation.47 | convolution fusion | flops 1073741824 | bytes 6815744 | tf_op jit(solution)/shard_map/dot_general | solution.py:360
  237.7 38.5 %reduce-scatter.2.cloned.1.call-done = f32[512,256]{1,0:T(8,128)} async-done(((f32[512,2048]{1,0:T(8,128)}), f32[512,256]{1,0:T(8,128)}) %reduce-scatter.2.cloned.1.call-update) | async-done | bytes 524304 | tf_op jit(solution)/shard_map/reduce_scatter | solution.py:361
  276.1 2.0 add_convert_fusion
  (45 shorter events, 0.4 us)
Async XLA Ops:
  6.5 227.8 %copy-start = (bf16[512,2048]{1,0:T(8,128)(2,1)S(1)}, bf16[512,2048]{1,0:T(8,128)(2,1)}, u32[]{:S(2)}) copy-start(bf16[512,2048]{1,0:T(8,128)(2,1)} %param.23) | copy-start | bytes 6291460
  6.5 75.2 %copy-start.10 = (bf16[512,2,128]{2,1,0:T(2,128)(2,1)S(1)}, bf16[512,2,128]{2,1,0:T(2,128)(2,1)}, u32[]{:S(2)}) copy-start(bf16[512,2,128]{2,1,0:T(2,128)(2,1)} %param.14) | copy-start | bytes 786436
  6.5 173.2 %all-reduce.2.cloned.1.call-start = ((), (), s32[]{:S(2)}) async-start(), calls=%async_computation.1 | async-start | bytes 8388608 | tf_op jit(solution)/shard_map/psum | solution.py:344
  7.7 29.8 %collective-permute-start = (bf16[512,2,128]{2,0,1:T(8,128)(2,1)S(1)}, bf16[512,2,128]{2,0,1:T(8,128)(2,1)}, u32[]{:S(2)}, u32[]{:S(2)}) collective-permute-start(bf16[512,2,128]{2,0,1:T(8,128)(2,1)S(1)} %copy.13), channel_id=1, source_target_pairs={{0,64},{8,72},{16,80},{24,88},{32,96},{40,104},{48,112},{56,120},{... | collective-permute-start | bytes 786440 | tf_op jit(solution)/shard_map/ppermute | solution.py:33
  12.4 28.1 %collective-permute-start.1 = (bf16[512,2,128]{2,0,1:T(8,128)(2,1)S(1)}, bf16[512,2,128]{2,0,1:T(8,128)(2,1)}, u32[]{:S(2)}, u32[]{:S(2)}) collective-permute-start(bf16[512,2,128]{2,0,1:T(8,128)(2,1)S(1)} %copy.13), channel_id=1, source_target_pairs={{0,56},{8,64},{16,72},{24,80},{32,88},{40,96},{48,104},{56,112},{6... | collective-permute-start | bytes 786440 | tf_op jit(solution)/shard_map/ppermute | solution.py:33
  20.6 26.2 %collective-permute-start.2 = (bf16[512,2,128]{2,0,1:T(8,128)(2,1)S(1)}, bf16[512,2,128]{2,0,1:T(8,128)(2,1)S(1)}, u32[]{:S(2)}, u32[]{:S(2)}) collective-permute-start(bf16[512,2,128]{2,0,1:T(8,128)(2,1)S(1)} %copy.13), channel_id=1, source_target_pairs={{0,48},{8,56},{16,64},{24,72},{32,80},{40,88},{48,96},{56,104},{64... | collective-permute-start | bytes 786440 | tf_op jit(solution)/shard_map/ppermute | solution.py:33
  24.0 26.6 %collective-permute-start.3 = (bf16[512,2,128]{2,0,1:T(8,128)(2,1)S(1)}, bf16[512,2,128]{2,0,1:T(8,128)(2,1)S(1)}, u32[]{:S(2)}, u32[]{:S(2)}) collective-permute-start(bf16[512,2,128]{2,0,1:T(8,128)(2,1)S(1)} %copy.13), channel_id=1, source_target_pairs={{0,40},{8,48},{16,56},{24,64},{32,72},{40,80},{48,88},{56,96},{64,... | collective-permute-start | bytes 786440 | tf_op jit(solution)/shard_map/ppermute | solution.py:33
  25.8 25.5 %collective-permute-start.4 = (bf16[512,2,128]{2,0,1:T(8,128)(2,1)S(1)}, bf16[512,2,128]{2,0,1:T(8,128)(2,1)S(1)}, u32[]{:S(2)}, u32[]{:S(2)}) collective-permute-start(bf16[512,2,128]{2,0,1:T(8,128)(2,1)S(1)} %copy.13), channel_id=1, source_target_pairs={{0,32},{8,40},{16,48},{24,56},{32,64},{40,72},{48,80},{56,88},{64,... | collective-permute-start | bytes 786440 | tf_op jit(solution)/shard_map/ppermute | solution.py:33
  37.5 27.6 %collective-permute-start.5 = (bf16[512,2,128]{2,0,1:T(8,128)(2,1)S(1)}, bf16[512,2,128]{2,0,1:T(8,128)(2,1)S(1)}, u32[]{:S(2)}, u32[]{:S(2)}) collective-permute-start(bf16[512,2,128]{2,0,1:T(8,128)(2,1)S(1)} %copy.13), channel_id=1, source_target_pairs={{0,24},{8,32},{16,40},{24,48},{32,56},{40,64},{48,72},{56,80},{64,... | collective-permute-start | bytes 786440 | tf_op jit(solution)/shard_map/ppermute | solution.py:33
  40.5 34.9 %collective-permute-start.6 = (bf16[512,2,128]{2,0,1:T(8,128)(2,1)S(1)}, bf16[512,2,128]{2,0,1:T(8,128)(2,1)S(1)}, u32[]{:S(2)}, u32[]{:S(2)}) collective-permute-start(bf16[512,2,128]{2,0,1:T(8,128)(2,1)S(1)} %copy.13), channel_id=1, source_target_pairs={{0,16},{8,24},{16,32},{24,40},{32,48},{40,56},{48,64},{56,72},{64,... | collective-permute-start | bytes 786440 | tf_op jit(solution)/shard_map/ppermute | solution.py:33
  46.8 34.2 %collective-permute-start.7 = (bf16[512,2,128]{2,0,1:T(8,128)(2,1)S(1)}, bf16[512,2,128]{2,0,1:T(8,128)(2,1)S(1)}, u32[]{:S(2)}, u32[]{:S(2)}) collective-permute-start(bf16[512,2,128]{2,0,1:T(8,128)(2,1)S(1)} %copy.13), channel_id=1, source_target_pairs={{0,8},{8,16},{16,24},{24,32},{32,40},{40,48},{48,56},{56,64},{64,7... | collective-permute-start | bytes 786440 | tf_op jit(solution)/shard_map/ppermute | solution.py:33
  93.8 8.4 %copy-start.11 = (bf16[256,2048]{1,0:T(8,128)(2,1)S(1)}, bf16[256,2048]{1,0:T(8,128)(2,1)}, u32[]{:S(2)}) copy-start(bf16[256,2048]{1,0:T(8,128)(2,1)} %param.15) | copy-start | bytes 3145732
  102.2 2.7 copy-start.12
  106.9 169.3 %reduce-scatter.2.cloned.1.call-start = ((), (), s32[]{:S(2)}) async-start(), calls=%async_computation.2 | async-start | bytes 4718592 | tf_op jit(solution)/shard_map/reduce_scatter | solution.py:361
  107.1 3.5 %copy-start.8 = (bf16[2048,2,512]{2,1,0:T(2,128)(2,1)S(1)}, bf16[2048,2,512]{2,1,0:T(2,128)(2,1)}, u32[]{:S(2)}) copy-start(bf16[2048,2,512]{2,1,0:T(2,128)(2,1)} %param.18) | copy-start | bytes 12582916
  110.6 3.2 %copy-start.13 = (f32[4,512]{1,0:T(4,128)S(1)}, f32[4,512]{1,0:T(4,128)}, u32[]{:S(2)}) copy-start(f32[4,512]{1,0:T(4,128)} %param.19) | copy-start | bytes 24580
  110.6 3.2 %copy-start.14 = (f32[4,512]{1,0:T(4,128)S(1)}, f32[4,512]{1,0:T(4,128)}, u32[]{:S(2)}) copy-start(f32[4,512]{1,0:T(4,128)} %param.20) | copy-start | bytes 24580
  113.8 68.6 %copy-start.16 = (f32[2048]{0:T(1024)S(1)}, f32[2048]{0:T(1024)}, u32[]{:S(2)}) copy-start(f32[2048]{0:T(1024)} %param.16) | copy-start | bytes 24580
  179.8 3.4 %copy-start.7 = (f32[512,2048]{1,0:T(8,128)S(1)}, f32[512,2048]{1,0:T(8,128)}, u32[]{:S(2)}) copy-start(f32[512,2048]{1,0:T(8,128)} %all-reduce.2.cloned.1.call-done) | copy-start | bytes 12582916
  183.2 4.7 %copy-start.9 = (bf16[256,8,2,256]{3,1,2,0:T(8,128)(2,1)S(1)}, bf16[256,8,2,256]{3,1,2,0:T(8,128)(2,1)}, u32[]{:S(2)}) copy-start(bf16[256,8,2,256]{3,1,2,0:T(8,128)(2,1)} %copy.36) | copy-start | bytes 6291460
  187.9 1.4 copy-start.1
  189.3 12.5 %copy-start.6 = (f32[4,128,128]{2,1,0:T(8,128)S(1)}, f32[4,128,128]{2,1,0:T(8,128)}, u32[]{:S(2)}) copy-start(f32[4,128,128]{2,1,0:T(8,128)} %initial_ref.1) | copy-start | bytes 786436
  196.5 1.0 copy-start.2
  197.5 0.8 copy-start.3
  198.4 0.8 copy-start.4
  199.2 31.9 %slice-start = ((f32[512,1024]{1,0:T(8,128)}), f32[512,512]{1,0:T(8,128)S(1)}, s32[]{:S(2)}) async-start(f32[512,1024]{1,0:T(8,128)} %copy-done.1), calls=%async_computation.3 | async-start | bytes 2097152 | tf_op jit(solution)/shard_map/slice | solution.py:357
  199.2 33.2 %copy-start.15 = (f32[128]{0:T(128)S(1)}, f32[128]{0:T(128)}, u32[]{:S(2)}) copy-start(f32[128]{0:T(128)} %param.22) | copy-start | bytes 1540
  201.8 1.0 copy-start.5
Sparse Core Ops, SparseCore 0:
  107.0 72.7 all-reduce.1
  237.8 38.2 reduce-scatter.1

commit v2 on v1

--- a/solution.py
+++ b/solution.py
@@ -11,6 +11,12 @@
 DV = 128
 ATTEND_HEAD_SIZE = 128
 WINDOW_KEYS = 4096
+X = 4
+HEADS = 8
+MODEL = 2048
+SHARE = 256
+PROJECTED = 1536
+TILE = 256
 CHUNK = 128
 ROWS = 512
 KEY_HEADS = 2
@@ -25,48 +31,6 @@
 
 
 epsilon = 1e-06
-
-
-def passed_along(shard, axis, by):
-    length = lax.axis_size(axis)
-    pairs = [(i, i + by) for i in range(length) if 0 <= i + by < length]
-    return lax.ppermute(shard, axis, pairs)
-
-
-def inverse_rms(values):
-    return lax.rsqrt(jnp.mean(values * values, axis=-1, keepdims=True) + epsilon)
-
-
-def attend(queries, key_value_pairs, seq_index):
-    row_count = queries.shape[0]
-    reach_pieces = WINDOW_KEYS // row_count
-    kv_heads = key_value_pairs.shape[2] // ATTEND_HEAD_SIZE
-    query_heads = queries.shape[1] // ATTEND_HEAD_SIZE
-    group_width = query_heads // kv_heads
-    earlier_rows = jnp.concatenate(
-        [passed_along(key_value_pairs, "seq", distance) for distance in range(reach_pieces, 0, -1)],
-        axis=0,
-    )
-    window_matrix = jnp.concatenate([earlier_rows, key_value_pairs], axis=0)
-    window_length = window_matrix.shape[0]
-    key_matrix = window_matrix[:, 0].reshape(window_length, kv_heads, ATTEND_HEAD_SIZE)
-    value_matrix = window_matrix[:, 1].reshape(window_length, kv_heads, ATTEND_HEAD_SIZE)
-    query_matrix = queries.reshape(row_count, kv_heads, group_width, ATTEND_HEAD_SIZE)
-    query_pos = seq_index * row_count + jnp.arange(row_count, dtype=jnp.int32)
-    key_pos = (seq_index - reach_pieces) * row_count + jnp.arange(window_length, dtype=jnp.int32)
-    distance_grid = query_pos[:, None] - key_pos[None, :]
-    allowed = (distance_grid >= 0) & (distance_grid < WINDOW_KEYS) & (key_pos[None, :] >= 0)
-    scores = jnp.einsum(
-        "qhgd,khd->hgqk", query_matrix, key_matrix, preferred_element_type=jnp.float32
-    ) * (1.0 / math.sqrt(ATTEND_HEAD_SIZE))
-    scores = jnp.where(allowed, scores, -jnp.inf)
-    row_peak = jnp.max(scores, axis=-1, keepdims=True)
-    exponentials = jnp.exp(scores - row_peak)
-    weights = (exponentials / jnp.sum(exponentials, axis=-1, keepdims=True)).astype(jnp.bfloat16)
-    mixed_rows = jnp.einsum(
-        "hgqk,khd->qhgd", weights, value_matrix, preferred_element_type=jnp.float32
-    )
-    return mixed_rows.astype(jnp.bfloat16).reshape(row_count, query_heads * ATTEND_HEAD_SIZE)
 
 
 def dot(a, b, contract=((1,), (0,))):
@@ -215,11 +179,249 @@
     )(query_key, value_gate, packed)
 
 
+def at_head(x, c):
+    return {"head": (x % X) * 2 + c}
+
+
+def send(source, target, send_sem, recv_sem, device):
+    copy = pltpu.make_async_remote_copy(
+        src_ref=source, dst_ref=target, send_sem=send_sem, recv_sem=recv_sem,
+        device_id=device, device_id_type=MESH)
+    copy.start()
+    return copy
+
+
+def greet(devices):
+    barrier = pltpu.get_barrier_semaphore()
+    for device in devices:
+        pl.semaphore_signal(barrier, inc=1, device_id=device, device_id_type=MESH)
+    pl.semaphore_wait(barrier, len(devices))
+
+
+def gather_heads(blocks, send_sem, recv_sem, x, c, use):
+    mid = ROWS // 2
+    own, left, right, far = (((x + d) % X) * 2 + c for d in (0, -1 + X, 1, 2))
+    over = [((x + d) % X) * 2 + 1 - c for d in (0, X - 1, 1, 2)]
+    sibling, to_left, to_right = at_head(x, 1 - c), at_head(x + X - 1, c), at_head(x + 1, c)
+
+    def go(n, block, device, rows=slice(None)):
+        ref = blocks.at[block] if rows == slice(None) else blocks.at[block, rows]
+        return send(ref, ref, send_sem.at[n], recv_sem.at[n], device)
+
+    copies = [go(1, own, to_right), go(2, own, to_left), go(0, own, sibling)]
+    copies[2].wait_recv()
+    use(0, (own, over[0]))
+    copies[0].wait_recv()
+    copies.append(go(3, left, to_right, slice(0, mid)))
+    copies.append(go(4, left, sibling))
+    copies[1].wait_recv()
+    copies.append(go(5, right, to_left, slice(mid, ROWS)))
+    copies.append(go(6, right, sibling))
+    use(1, (left, right))
+    copies[4].wait_recv()
+    copies[6].wait_recv()
+    use(2, (over[1], over[2]))
+    copies[3].wait_recv()
+    copies[5].wait_recv()
+    copies.append(go(7, far, sibling))
+    copies[7].wait_recv()
+    use(3, (far, over[3]))
+    for copy in copies:
+        copy.wait_send()
+
+
+def attend_block(queries, window, place, peak, total, relation):
+    scale = math.log2(math.e) / math.sqrt(ATTEND_HEAD_SIZE)
+    ones = jnp.ones((ROWS, ATTEND_HEAD_SIZE), bf16)
+
+    def tile(t, carry):
+        rows = pl.ds(pl.multiple_of(t * TILE, TILE), TILE)
+        keys = window[place, :, :ATTEND_HEAD_SIZE]
+        values = jnp.concatenate([window[place, :, ATTEND_HEAD_SIZE:], ones], axis=1)
+        scores = mm_nt(queries[rows, :], keys) * scale
+        if relation is not None:
+            i, j = grid_of(TILE, ROWS)
+            i = i + lax.rem(t, ROWS // TILE) * TILE
+            scores = jnp.where(i >= j if relation == "causal" else i < j, scores, -jnp.inf)
+        block_peak = jnp.max(scores, axis=-1, keepdims=True)
+        if relation == "causal":
+            weights = jnp.exp2(scores - block_peak).astype(bf16)
+            total[rows, :] = dot(weights, values)
+            peak[rows, :] = jnp.broadcast_to(block_peak, (TILE, ATTEND_HEAD_SIZE))
+        else:
+            before = peak[rows, :1]
+            now = jnp.maximum(before, block_peak)
+            weights = jnp.exp2(scores - now).astype(bf16)
+            total[rows, :] = total[rows, :] * jnp.exp2(before - now) + dot(weights, values)
+            peak[rows, :] = jnp.broadcast_to(now, (TILE, ATTEND_HEAD_SIZE))
+        return carry
+
+    lax.fori_loop(0, 2 * ROWS // TILE, tile, 0)
+
+
+def front_kernel(queries_ref, pairs_ref, out_weight_ref, residual_ref, gain_ref, qk_weight_ref,
+                 vg_weight_ref, hidden_ref, qk_ref, vg_ref,
+                 queries, window, peak, total, out_weight, mix, normed, branch, projected, squares,
+                 qk_weight, vg_weight,
+                 kv_send, kv_recv, ow_send, ow_recv, mix_send, mix_recv, norm_send, norm_recv,
+                 local_sem):
+    s, head = lax.axis_index("seq"), lax.axis_index("head")
+    seq_count = Y * Z
+    x, c = head // 2, head % 2
+
+    def along(d):
+        return {"seq": (s + d + seq_count) % seq_count}
+
+    def other(d):
+        return {"head": (head + d) % HEADS}
+
+    locals_ = [
+        pltpu.make_async_copy(pairs_ref, window.at[0], local_sem.at[0]),
+        pltpu.make_async_copy(qk_weight_ref, qk_weight, local_sem.at[1]),
+        pltpu.make_async_copy(vg_weight_ref, vg_weight, local_sem.at[2]),
+        pltpu.make_async_copy(
+            out_weight_ref.at[:, pl.ds(pl.multiple_of(head * SHARE, SHARE), SHARE)],
+            out_weight.at[head], local_sem.at[3]),
+    ]
+    for copy in locals_:
+        copy.start()
+    greet([along(1), along(-1), along(-Z)] + [other(d) for d in range(1, HEADS)])
+
+    def hop(n, source, target, by):
+        return send(source, target, kv_send.at[n], kv_recv.at[n], along(by))
+
+    half = ROWS // 2
+    to_next, to_row, before = 1, Z, -1
+    hops = {1: hop(1, pairs_ref, window.at[1], to_next), 8: hop(8, pairs_ref, window.at[8], to_row)}
+    weights = []
+    for d in range(1, HEADS):
+        target = (head + d) % HEADS
+        weights.append(send(
+            out_weight_ref.at[:, pl.ds(pl.multiple_of(target * SHARE, SHARE), SHARE)],
+            out_weight.at[head], ow_send.at[d], ow_recv.at[d], other(d)))
+    for g in range(2):
+        queries[g * ROWS:(g + 1) * ROWS, :] = queries_ref[:, g * ATTEND_HEAD_SIZE:(g + 1) * ATTEND_HEAD_SIZE]
+    locals_[0].wait()
+    attend_block(queries, window, 0, peak, total, "causal")
+
+    def attend_earlier(d):
+        @pl.when(s >= d)
+        def _():
+            attend_block(queries, window, d, peak, total, "window" if d == Z else None)
+
+    hops[1].wait_recv()
+    hops[2] = hop(2, window.at[1], window.at[2], to_next)
+    hops[8].wait_recv()
+    hops[7] = hop(7, window.at[8], window.at[7], before)
+    attend_earlier(1)
+    hops[2].wait_recv()
+    hops[3] = hop(3, window.at[2], window.at[3], to_next)
+    hops[7].wait_recv()
+    hops[6] = hop(6, window.at[7], window.at[6], before)
+    attend_earlier(8)
+    attend_earlier(2)
+    hops[3].wait_recv()
+    hops[4] = hop(4, window.at[3, 0:half], window.at[4, 0:half], to_next)
+    hops[6].wait_recv()
+    hops[5] = hop(5, window.at[6], window.at[5], before)
+    attend_earlier(7)
+    attend_earlier(3)
+    hops[5].wait_recv()
+    hops[0] = hop(0, window.at[5, half:ROWS], window.at[4, half:ROWS], before)
+    attend_earlier(6)
+    attend_earlier(5)
+    hops[4].wait_recv()
+    hops[0].wait_recv()
+    attend_earlier(4)
+    for g in range(2):
+        rows = slice(g * ROWS, (g + 1) * ROWS)
+        mix[head, :, g * ATTEND_HEAD_SIZE:(g + 1) * ATTEND_HEAD_SIZE] = (
+            total[rows, :ATTEND_HEAD_SIZE] / total[rows, ATTEND_HEAD_SIZE:]).astype(bf16)
+    for copy in weights:
+        copy.wait()
+    locals_[3].wait()
+
+    def add_branch(turn, pair):
+        a, b = pair
+        part = dot(mix[a], out_weight[a]) + dot(mix[b], out_weight[b])
+        branch[...] = part if turn == 0 else branch[...] + part
+
+    gather_heads(mix, mix_send, mix_recv, x, c, add_branch)
+    hidden = residual_ref[...].astype(f32) + branch[...]
+    hidden_ref[...] = hidden
+    own = pl.ds(pl.multiple_of(head * SHARE, SHARE), SHARE)
+    normed[head] = (hidden * gain_ref[:, own]).astype(bf16)
+    locals_[1].wait()
+    locals_[2].wait()
+
+    def add_projected(turn, pair):
+        square = None
+        for block in pair:
+            cols = pl.ds(pl.multiple_of(block * SHARE, SHARE), SHARE)
+            value = normed[block].astype(f32) * (1.0 / gain_ref[:, cols])
+            value = value * value
+            value = value[:, :128] + value[:, 128:]
+            square = value if square is None else square + value
+        squares[...] = square if turn == 0 else squares[...] + square
+        a, b = (pl.ds(pl.multiple_of(block * SHARE, SHARE), SHARE) for block in pair)
+        for weight, at in ((qk_weight, 0), (vg_weight, 2 * KEY_HEADS * DK)):
+            for column in range(0, weight.shape[1], 256):
+                cols = slice(column, column + 256)
+                part = dot(normed[pair[0]], weight[a, cols]) + dot(normed[pair[1]], weight[b, cols])
+                to = slice(at + column, at + column + 256)
+                projected[:, to] = part if turn == 0 else projected[:, to] + part
+
+    gather_heads(normed, norm_send, norm_recv, x, c, add_projected)
+    inverse = lax.rsqrt(jnp.sum(squares[...], axis=-1, keepdims=True) * (1.0 / MODEL) + epsilon)
+    qk_ref[...] = projected[:, :512] * inverse
+    vg_ref[...] = projected[:, 512:] * inverse
+    for n in range(9):
+        hops[n].wait_send()
+
+
+def front_part(queries, pairs, attention_out, residual, gain, qk_weight, vg_weight):
+    vmem, hbm = pl.BlockSpec(memory_space=pltpu.VMEM), pl.BlockSpec(memory_space=pl.ANY)
+    dma = pltpu.SemaphoreType.DMA
+    return pl.pallas_call(
+        front_kernel,
+        out_shape=(
+            jax.ShapeDtypeStruct((ROWS, SHARE), f32),
+            jax.ShapeDtypeStruct((ROWS, 512), f32),
+            jax.ShapeDtypeStruct((ROWS, 1024), f32),
+        ),
+        in_specs=[vmem, hbm, hbm, vmem, vmem, hbm, hbm],
+        out_specs=[vmem] * 3,
+        scratch_shapes=[
+            pltpu.VMEM((2 * ROWS, ATTEND_HEAD_SIZE), bf16),
+            pltpu.VMEM((Z + 1, ROWS, 2 * ATTEND_HEAD_SIZE), bf16),
+            pltpu.VMEM((2 * ROWS, ATTEND_HEAD_SIZE), f32),
+            pltpu.VMEM((2 * ROWS, 2 * ATTEND_HEAD_SIZE), f32),
+            pltpu.VMEM((HEADS, SHARE, SHARE), bf16),
+            pltpu.VMEM((HEADS, ROWS, SHARE), bf16),
+            pltpu.VMEM((HEADS, ROWS, SHARE), bf16),
+            pltpu.VMEM((ROWS, SHARE), f32),
+            pltpu.VMEM((ROWS, PROJECTED), f32),
+            pltpu.VMEM((ROWS, 128), f32),
+            pltpu.VMEM((MODEL, 512), bf16),
+            pltpu.VMEM((MODEL, 1024), bf16),
+            dma((9,)), dma((9,)), dma((HEADS,)), dma((HEADS,)), dma((8,)), dma((8,)), dma((8,)),
+            dma((8,)), dma((4,)),
+        ],
+        compiler_params=pltpu.CompilerParams(
+            collective_id=0, has_side_effects=True, vmem_limit_bytes=56 * 2**20),
+        name="front",
+    )(queries, pairs, attention_out, residual, gain, qk_weight, vg_weight)
+
+
 FAR_FIRST = (4, 3, 5, 2, 6, 1, 7)
 
 
-def scan_kernel(message_ref, initial_ref, out_ref, row, total, column, prefix, first, back, landed,
-                row_send, row_recv, col_send, col_recv, back_send, back_recv):
+def scan_kernel(message_ref, initial_ref, zero_ref, lead_ref, vg_ref, gain_ref, weight_ref,
+                hidden_ref, out_ref,
+                row, total, column, prefix, first, back, landed,
+                gate, gated, to_sibling, from_sibling, far, relay, near, arrived,
+                row_send, row_recv, col_send, col_recv, back_send, back_recv,
+                pair_send, pair_recv, out_send, out_recv):
     s = lax.axis_index("seq")
     y, z = s // Z, s % Z
 
@@ -229,12 +431,11 @@
     def in_column(d):
         return {"seq": ((y + d) % Y) * Z + z}
 
-    barrier = pltpu.get_barrier_semaphore()
-    for d in range(1, Z):
-        pl.semaphore_signal(barrier, inc=1, device_id=in_row(d), device_id_type=MESH)
-    for d in range(1, Y):
-        pl.semaphore_signal(barrier, inc=1, device_id=in_column(d), device_id_type=MESH)
-    pl.semaphore_wait(barrier, Z - 1 + Y - 1)
+    head = lax.axis_index("head")
+    x, c = head // 2, head % 2
+    sibling, to_left, to_right = at_head(x, 1 - c), at_head(x + X - 1, c), at_head(x + 1, c)
+    greet([in_row(d) for d in range(1, Z)] + [in_column(d) for d in range(1, Y)]
+          + [sibling, to_left, to_right])
 
     sends = []
     for d in FAR_FIRST:
@@ -246,18 +447,22 @@
     row[z] = message_ref[z]
     first[...] = initial_ref[z // 2].T
     i, j = grid_of(DK + HALF, DK)
-    x = (i == j).astype(f32)
+    run = (i == j).astype(f32)
     decay = jnp.ones((1, DK), f32)
+    for h in range(VALUE_HEADS):
+        cols = slice(h * DV, (h + 1) * DV)
+        u = vg_ref[:, VALUE_HEADS * DV + h * DV:VALUE_HEADS * DV + (h + 1) * DV]
+        gate[:, cols] = gain_ref[...] * (u / (1.0 + jnp.exp(-u)))
     for copy in sends:
         copy.wait()
     zero = jnp.zeros((DK, DK), f32)
     for place in range(Z):
-        prefix[place] = x
+        prefix[place] = run
         a = sum_rows(row[place, DK + HALF:])
         offset = jnp.concatenate([zero, row[place, DK:DK + HALF].astype(f32)], axis=0)
-        x = a * x + mm2(x, row[place, :DK]) + offset
+        run = a * run + mm2(run, row[place, :DK]) + offset
         decay = decay * a
-    total[:DK + HALF] = jnp.where(i == j, x - decay, x).astype(bf16)
+    total[:DK + HALF] = jnp.where(i == j, run - decay, run).astype(bf16)
     total[DK + HALF:] = three_rows(decay)
     sends = []
     for d in (2, 1, 3):
@@ -287,15 +492,54 @@
     landed[z] = back[z]
     for copy in sends:
         copy.wait()
-    out_ref[...] = landed[...]
-
-
-def entering_states(messages, initial_state):
+    for h in range(VALUE_HEADS):
+        cols = slice(h * DV, (h + 1) * DV)
+        state = jnp.concatenate([landed[2 * h], landed[2 * h + 1]], axis=0)
+        delta = zero_ref[:, cols] + mm_nt(lead_ref[:, cols], state)
+        gated[:, cols] = (delta * inverse_rms(delta) * gate[:, cols]).astype(bf16)
+
+    def partial(d, core):
+        at = ((x + d) % X * 2 + core) * SHARE
+        return dot(gated[...], weight_ref[:, pl.ds(pl.multiple_of(at, SHARE), SHARE)])
+
+    order, half = (2, 1, X - 1, 0), ROWS // 2
+    top, bottom = slice(0, half), slice(half, ROWS)
+    pairs = []
+    for n, d in enumerate(order):
+        to_sibling[n] = partial(d, 1 - c).astype(bf16)
+        pairs.append(send(to_sibling.at[n], from_sibling.at[n], pair_send.at[n], pair_recv.at[n], sibling))
+    sends = []
+    pairs[0].wait_recv()
+    far[...] = (partial(2, c) + from_sibling[0].astype(f32)).astype(bf16)
+    sends.append(send(far.at[top], relay.at[0], out_send.at[0], out_recv.at[0], to_right))
+    sends.append(send(far.at[bottom], relay.at[1], out_send.at[1], out_recv.at[1], to_left))
+    for n, rows, device in ((1, top, to_right), (2, bottom, to_left)):
+        value = partial(order[n], c)
+        pairs[n].wait_recv()
+        value = value + from_sibling[n].astype(f32)
+        sends[n - 1].wait_recv()
+        passed = relay[n - 1].astype(f32)
+        if n == 1:
+            near[0] = jnp.concatenate([value[top] + passed, value[bottom]], axis=0).astype(bf16)
+        else:
+            near[1] = jnp.concatenate([value[top], value[bottom] + passed], axis=0).astype(bf16)
+        sends.append(send(near.at[n - 1], arrived.at[n - 1], out_send.at[n + 1], out_recv.at[n + 1], device))
+    value = hidden_ref[...] + partial(0, c)
+    pairs[3].wait_recv()
+    value = value + from_sibling[3].astype(f32)
+    sends[2].wait_recv()
+    sends[3].wait_recv()
+    out_ref[...] = (value + arrived[0].astype(f32) + arrived[1].astype(f32)).astype(bf16)
+    for copy in pairs + sends:
+        copy.wait_send()
+
+
+def back_part(messages, initial_state, zero_part, lead, value_gate, head_gain, delta_output, hidden):
     dma = pltpu.SemaphoreType.DMA
     return pl.pallas_call(
         scan_kernel,
-        out_shape=jax.ShapeDtypeStruct((Z, HALF, DK), bf16),
-        in_specs=[pl.BlockSpec(memory_space=pltpu.VMEM)] * 2,
+        out_shape=jax.ShapeDtypeStruct((ROWS, SHARE), bf16),
+        in_specs=[pl.BlockSpec(memory_space=pltpu.VMEM)] * 8,
         out_specs=pl.BlockSpec(memory_space=pltpu.VMEM),
         scratch_shapes=[
             pltpu.VMEM((Z, MESSAGE, DK), bf16),
@@ -305,61 +549,37 @@
             pltpu.VMEM((DV, DK), f32),
             pltpu.VMEM((Z, HALF, DK), bf16),
             pltpu.VMEM((Z, HALF, DK), bf16),
+            pltpu.VMEM((ROWS, VALUE_HEADS * DV), f32),
+            pltpu.VMEM((ROWS, VALUE_HEADS * DV), bf16),
+            pltpu.VMEM((X, ROWS, SHARE), bf16),
+            pltpu.VMEM((X, ROWS, SHARE), bf16),
+            pltpu.VMEM((ROWS, SHARE), bf16),
+            pltpu.VMEM((2, ROWS // 2, SHARE), bf16),
+            pltpu.VMEM((2, ROWS, SHARE), bf16),
+            pltpu.VMEM((2, ROWS, SHARE), bf16),
             dma((Z,)), dma((Z,)), dma((Y,)), dma((Y,)), dma((Z,)), dma((Z,)),
+            dma((X,)), dma((X,)), dma((X,)), dma((X,)),
         ],
         compiler_params=pltpu.CompilerParams(
-            collective_id=1, has_side_effects=True, vmem_limit_bytes=32 * 2**20),
-        name="delta_scan",
-    )(messages, initial_state)
-
-
-def body(
-    residual,
-    queries,
-    key_value_pairs,
-    attention_out,
-    norm_gain,
-    query_key_weight,
-    value_gate_weight,
-    write_strength,
-    log_decay,
-    initial_state,
-    head_gain,
-    delta_output,
-):
-    row_count = residual.shape[0]
-    share_width = residual.shape[1]
-    model_width = norm_gain.shape[0]
-    seq_index = lax.axis_index("seq")
-    head_index = lax.axis_index("head")
-    attention_mix = attend(queries, key_value_pairs, seq_index)
-    branch = jnp.dot(attention_mix, attention_out, preferred_element_type=jnp.float32)
-    query_cols = query_key_weight.shape[2]
-    value_cols = value_gate_weight.shape[2]
-    flat_query_key = query_key_weight.reshape(model_width, 2 * query_cols)
-    flat_value_gate = value_gate_weight.reshape(model_width, 2 * value_cols)
-    placed = lax.dynamic_update_slice_in_dim(
-        jnp.zeros_like(branch), residual.astype(jnp.float32), head_index * share_width, 1
-    )
-    hidden_full = lax.psum(branch + placed, "head")
-    hidden = lax.dynamic_slice_in_dim(hidden_full, head_index * share_width, share_width, 1)
-    normed = (hidden_full * inverse_rms(hidden_full) * norm_gain).astype(jnp.bfloat16)
-    query_key = jnp.dot(normed, flat_query_key, preferred_element_type=jnp.float32)
-    value_gate = jnp.dot(normed, flat_value_gate, preferred_element_type=jnp.float32)
-    value_heads = value_cols // DV
+            collective_id=1, has_side_effects=True, vmem_limit_bytes=48 * 2**20),
+        name="delta_scan_out",
+    )(messages, initial_state, zero_part, lead, value_gate, head_gain, delta_output, hidden)
+
+
+def inverse_rms(values):
+    return lax.rsqrt(jnp.mean(values * values, axis=-1, keepdims=True) + epsilon)
+
+
+def body(residual, queries, key_value_pairs, attention_out, norm_gain, query_key_weight,
+         value_gate_weight, write_strength, log_decay, initial_state, head_gain, delta_output):
+    hidden, query_key, value_gate = front_part(
+        queries, key_value_pairs.reshape(ROWS, 2 * ATTEND_HEAD_SIZE), attention_out, residual,
+        norm_gain.reshape(1, MODEL), query_key_weight.reshape(MODEL, -1),
+        value_gate_weight.reshape(MODEL, -1))
     packed = jnp.concatenate([log_decay, write_strength], axis=0)
     zero_part, lead, messages = local_part(query_key, value_gate, packed)
-    states = entering_states(messages, initial_state).reshape(value_heads, DV, DK)
-    met = jnp.einsum(
-        "thd,hed->the", lead.reshape(row_count, value_heads, DK), states, preferred_element_type=f32
-    )
-    delta_mix = zero_part.reshape(row_count, value_heads, DV) + met
-    gate = value_gate[:, value_cols:].reshape(row_count, value_heads, DV)
-    gated = delta_mix * inverse_rms(delta_mix) * head_gain * jax.nn.silu(gate)
-    gated = gated.astype(jnp.bfloat16).reshape(row_count, value_heads * DV)
-    delta_branch = jnp.dot(gated, delta_output, preferred_element_type=jnp.float32)
-    delta_share = lax.psum_scatter(delta_branch, "head", scatter_dimension=1, tiled=True)
-    return (hidden + delta_share).astype(jnp.bfloat16)
+    return back_part(messages, initial_state, zero_part, lead, value_gate,
+                     head_gain.reshape(1, DV), delta_output, hidden)
 
 
 def solution(mesh):

time: 288 us -> 160 us (0.56)
  waiting for transfers between devices: 132 us -> 0 us
  Pallas kernels: 32.7 us -> 148 us
  starting transfers between devices: 33.9 us -> 0 us
  matrix products: 28.5 us -> 0 us
  other arithmetic: 19 us -> 0.01 us
  between operations: 13.6 us -> 0.1 us
  local copies, waits for them, and re-layouts: 24.8 us -> 11.6 us
    pallas_call x1 -> x2, Pallas kernels: 25.5 us -> 140 us  [the longest x1 87.9 us: front_part(): pl.pallas_call(front_kernel, out_shape=(jax.ShapeDtypeStruct((ROWS, SHARE...]
    psum x1 -> x0, waiting for transfers between devices: 65.9 us -> none  [body(): hidden_full = lax.psum(branch + placed, 'head')]
    reduce_scatter x1 -> x0, waiting for transfers between devices: 38.5 us -> none  [body(): lax.psum_scatter(delta_branch, 'head', scatter_dimension=1, tiled=True)]
    ppermute x8 -> x0, starting transfers between devices: 33.6 us -> none  [passed_along(): return lax.ppermute(shard, axis, pairs)]
    dot_general x7 -> x0, matrix products: 28.5 us -> none  [the longest x1 8.39 us: attend(): jnp.einsum('hgqk,khd->qhgd', weights, value_matrix, preferred_element_typ...]
    ppermute x8 -> x0, waiting for transfers between devices: 27.9 us -> none  [passed_along(): return lax.ppermute(shard, axis, pairs)]
    unnamed x45 -> x24, local copies, waits for them, and re-layouts: 20.1 us -> 11.6 us
    reduce_sum x2 -> x0, other arithmetic: 8.49 us -> none  [the longest x1 5.8 us: attend(): jnp.sum(exponentials, axis=-1, keepdims=True)]
  transfers between devices with their start and end apart: 10 -> 0, of which waited for: 6 -> 0; matrix products, arithmetic and copies ran while one was open for 6% -> 0% of each run, Pallas kernels for 0% -> 0%
where the time goes in v2:
time: 160 us; the launch traced here: 159 us
  Pallas kernels  148 us (92%)
  local copies, waits for them, and re-layouts  11.6 us (7%)
    pallas_call x1, Pallas kernels, front_part(): pl.pallas_call(front_kernel, out_shape=(jax.ShapeDtypeStruct((ROWS, SHARE...  87.9 us
    pallas_call x1, Pallas kernels, back_part(): pl.pallas_call(scan_kernel, out_shape=jax.ShapeDtypeStruct((ROWS, SHARE),...  52.4 us
    unnamed x24, local copies, waits for them, and re-layouts  11.6 us
    pallas_call x1, Pallas kernels, local_part(): pl.pallas_call(local_kernel, out_shape=(jax.ShapeDtypeStruct((ROWS, VALUE...  7.38 us

profile of v2, /device:TPU:1, one launch (start us, length us, event | category | flops | bytes accessed | tf_op | source)
XLA Modules:
  0.0 159.5 jit_solution(7953233180733393783)
XLA Ops:
  0.0 0.0 copy-start.6
  0.0 5.5 %copy.15 = bf16[256,8,2,512]{3,1,2,0:T(8,128)(2,1)} copy(bf16[256,8,2,512]{3,2,1,0:T(2,128)(2,1)} %bitcast.13) | data formatting | bytes 8388608
  5.5 0.0 copy-done.6
  5.5 0.0 copy-start.7
  5.5 1.8 %copy.14 = bf16[256,8,2,256]{3,1,2,0:T(8,128)(2,1)} copy(bf16[256,8,2,256]{3,2,1,0:T(2,128)(2,1)S(1)} %bitcast.14) | data formatting | bytes 4194304
  7.3 0.0 copy-done.7
  7.3 0.7 copy.17
  8.1 0.0 copy-start.8
  8.1 0.0 copy-start.9
  8.1 0.0 copy-start.4
  8.1 87.9 %front.1 = (f32[512,256]{1,0:T(8,128)}, f32[512,512]{1,0:T(8,128)}, f32[512,1024]{1,0:T(8,128)}) custom-call(bf16[512,256]{1,0:T(8,128)(2,1)} %queries_ref.1, bf16[512,256]{1,0:T(8,128)(2,1)} %bitcast.15, bf16[256,2048]{1,0:T(8,128)(2,1)} %out_weight_ref.1, bf16[512,256]{1,0:T(8,128)(2,1)} %residual_ref.1, f32[1,2048]{1,0:T(1,128)} %bitcast.17, ...), custom_call_target="tpu_custom_call" | custom-call | tf_op jit(solution)/shard_map/front/pallas_call | solution.py:385
  96.0 0.0 copy-start.5
  96.0 0.0 copy-done.8
  96.0 0.0 copy-done.9
  96.1 0.0 copy-start
  96.1 1.6 copy-done
  97.7 0.0 copy-start.2
  97.7 1.2 copy-done.2
  98.9 0.0 copy-start.1
  98.9 0.0 copy-start.3
  98.9 7.4 %delta_local.1 = (f32[512,512]{1,0:T(8,128)S(1)}, bf16[512,512]{1,0:T(8,128)(2,1)S(1)}, bf16[8,208,128]{2,1,0:T(8,128)(2,1)S(1)}) custom-call(f32[512,512]{1,0:T(8,128)S(1)} %copy-done.2, f32[512,1024]{1,0:T(8,128)S(1)} %copy-done, f32[8,512]{1,0:T(8,128)S(1)} %pad_maximum_fusion.packed_ref), custom_call_target="tpu_custom_call" | custom-call | tf_op jit(solution)/shard_map/delta_local/pallas_call | solution.py:167
  106.3 0.0 copy-done.4
  106.3 0.0 copy-done.5
  106.3 0.0 copy-done.1
  106.3 0.0 copy-done.3
  106.3 52.4 %delta_scan_out.1 = bf16[512,256]{1,0:T(8,128)(2,1)S(1)} custom-call(bf16[8,208,128]{2,1,0:T(8,128)(2,1)S(1)} %get-tuple-element.13.message_ref, f32[4,128,128]{2,1,0:T(8,128)S(1)} %copy-done.4, f32[512,512]{1,0:T(8,128)S(1)} %get-tuple-element.14.zero_ref, bf16[512,512]{1,0:T(8,128)(2,1)S(1)} %get-tuple-element.15.lead_ref, f32[512,1024]{1,0:T(8,128)S(1)} %copy-done.1, ...), custom_call_target="tpu_custom_call" | custom-call | tf_op jit(solution)/shard_map/delta_scan_out/pallas_call | solution.py:539
  158.8 0.7 copy.19
  (1 shorter events, 0.0 us)
Async XLA Ops:
  0.0 5.5 %copy-start.6 = (bf16[2048,2,256]{2,1,0:T(2,128)(2,1)S(1)}, bf16[2048,2,256]{2,1,0:T(2,128)(2,1)}, u32[]{:S(2)}) copy-start(bf16[2048,2,256]{2,1,0:T(2,128)(2,1)} %param.17) | copy-start | bytes 6291460
  5.5 1.8 %copy-start.7 = (bf16[512,2,128]{2,1,0:T(2,128)(2,1)S(1)}, bf16[512,2,128]{2,1,0:T(2,128)(2,1)}, u32[]{:S(2)}) copy-start(bf16[512,2,128]{2,1,0:T(2,128)(2,1)} %param.14) | copy-start | bytes 786436
  8.1 87.9 %copy-start.8 = (f32[4,512]{1,0:T(4,128)S(1)}, f32[4,512]{1,0:T(4,128)}, u32[]{:S(2)}) copy-start(f32[4,512]{1,0:T(4,128)} %param.19) | copy-start | bytes 24580
  8.1 88.0 %copy-start.9 = (f32[4,512]{1,0:T(4,128)S(1)}, f32[4,512]{1,0:T(4,128)}, u32[]{:S(2)}) copy-start(f32[4,512]{1,0:T(4,128)} %param.20) | copy-start | bytes 24580
  8.1 98.2 %copy-start.4 = (f32[4,128,128]{2,1,0:T(8,128)S(1)}, f32[4,128,128]{2,1,0:T(8,128)}, u32[]{:S(2)}) copy-start(f32[4,128,128]{2,1,0:T(8,128)} %initial_ref.1) | copy-start | bytes 786436
  96.0 10.3 %copy-start.5 = (f32[128]{0:T(128)S(1)}, f32[128]{0:T(128)}, u32[]{:S(2)}) copy-start(f32[128]{0:T(128)} %param.22) | copy-start | bytes 1540
  96.1 1.6 copy-start
  97.7 1.2 copy-start.2
  98.9 7.4 %copy-start.1 = (f32[512,1024]{1,0:T(8,128)S(1)}, f32[512,1024]{1,0:T(8,128)}, u32[]{:S(2)}) copy-start(f32[512,1024]{1,0:T(8,128)} %get-tuple-element.12.vg_ref) | copy-start | bytes 6291460
  98.9 7.4 %copy-start.3 = (f32[512,256]{1,0:T(8,128)S(1)}, f32[512,256]{1,0:T(8,128)}, u32[]{:S(2)}) copy-start(f32[512,256]{1,0:T(8,128)} %get-tuple-element.16.hidden_ref) | copy-start | bytes 1572868

commit v3 on v2

--- a/solution.py
+++ b/solution.py
@@ -78,7 +78,7 @@
     return jnp.sum(block.astype(f32), axis=0, keepdims=True)
 
 
-def local_kernel(qk_ref, vg_ref, packed_ref, zero_ref, lead_ref, message_ref, prefix):
+def local_slab(projected, inverse_ref, packed_ref, zero_ref, lead_ref, message_ref, prefix):
     i, j = grid_of(CHUNK, CHUNK)
     inclusive, strict = i >= j, i > j
     eye = (i == j).astype(f32)
@@ -101,10 +101,10 @@
                 precision=lax.Precision.HIGHEST, preferred_element_type=f32)
             keys = []
             for kh in range(KEY_HEADS):
-                q = qk_ref[rows, kh * DK:(kh + 1) * DK]
+                q = projected[rows, kh * DK:(kh + 1) * DK] * inverse_ref[rows, :]
                 q = q * lax.rsqrt(jnp.sum(q * q, axis=-1, keepdims=True) + epsilon) * DK ** (-0.5)
                 at = KEY_HEADS * DK + kh * DK
-                k = qk_ref[rows, at:at + DK]
+                k = projected[rows, at:at + DK] * inverse_ref[rows, :]
                 k = k * lax.rsqrt(jnp.sum(k * k, axis=-1, keepdims=True) + epsilon)
                 kb = k.astype(bf16)
                 keys.append((q, kb, k.T, mm_nt(kb, kb), mm_nt(q, kb)))
@@ -129,7 +129,8 @@
             size *= 2
         for it in items:
             scaled = it["inverse"] * it["strength_row"]
-            v = vg_ref[it["rows"], it["h"] * DV:(it["h"] + 1) * DV]
+            at = 2 * KEY_HEADS * DK + it["h"] * DV
+            v = projected[it["rows"], at:at + DV] * inverse_ref[it["rows"], :]
             w = mm(scaled * jnp.exp(it["cum_row"]), it["k"])
             u = mm(scaled, v)
             it["wu"] = jnp.concatenate([w, u], axis=1).astype(bf16)
@@ -163,22 +164,6 @@
             message_ref[2 * h + c, DK + HALF:] = tail
 
 
-def local_part(query_key, value_gate, packed):
-    return pl.pallas_call(
-        local_kernel,
-        out_shape=(
-            jax.ShapeDtypeStruct((ROWS, VALUE_HEADS * DV), f32),
-            jax.ShapeDtypeStruct((ROWS, VALUE_HEADS * DK), bf16),
-            jax.ShapeDtypeStruct((Z, MESSAGE, DK), bf16),
-        ),
-        in_specs=[pl.BlockSpec(memory_space=pltpu.VMEM)] * 3,
-        out_specs=[pl.BlockSpec(memory_space=pltpu.VMEM)] * 3,
-        scratch_shapes=[pltpu.VMEM((VALUE_HEADS, DK, DK + DV), f32)],
-        compiler_params=pltpu.CompilerParams(vmem_limit_bytes=48 * 2**20),
-        name="delta_local",
-    )(query_key, value_gate, packed)
-
-
 def at_head(x, c):
     return {"head": (x % X) * 2 + c}
 
@@ -200,33 +185,44 @@
 
 def gather_heads(blocks, send_sem, recv_sem, x, c, use):
     mid = ROWS // 2
-    own, left, right, far = (((x + d) % X) * 2 + c for d in (0, -1 + X, 1, 2))
+    top, bottom = slice(0, mid), slice(mid, ROWS)
+    own, left, right, far = (((x + d) % X) * 2 + c for d in (0, X - 1, 1, 2))
     over = [((x + d) % X) * 2 + 1 - c for d in (0, X - 1, 1, 2)]
     sibling, to_left, to_right = at_head(x, 1 - c), at_head(x + X - 1, c), at_head(x + 1, c)
-
-    def go(n, block, device, rows=slice(None)):
-        ref = blocks.at[block] if rows == slice(None) else blocks.at[block, rows]
-        return send(ref, ref, send_sem.at[n], recv_sem.at[n], device)
-
-    copies = [go(1, own, to_right), go(2, own, to_left), go(0, own, sibling)]
+    copies = {}
+
+    def go(n, block, device, rows=None):
+        ref = blocks.at[block] if rows is None else blocks.at[block, rows]
+        copies[n] = send(ref, ref, send_sem.at[n], recv_sem.at[n], device)
+
+    go(1, own, to_right, top)
+    go(3, own, to_left, bottom)
+    go(0, own, sibling)
+    go(2, own, to_right, bottom)
+    go(4, own, to_left, top)
+    copies[0].wait_recv()
+    use(0, (own, over[0]))
+    copies[1].wait_recv()
+    go(5, left, to_right, top)
+    copies[3].wait_recv()
+    go(6, right, to_left, bottom)
     copies[2].wait_recv()
-    use(0, (own, over[0]))
-    copies[0].wait_recv()
-    copies.append(go(3, left, to_right, slice(0, mid)))
-    copies.append(go(4, left, sibling))
-    copies[1].wait_recv()
-    copies.append(go(5, right, to_left, slice(mid, ROWS)))
-    copies.append(go(6, right, sibling))
+    go(7, left, sibling)
+    copies[4].wait_recv()
+    go(8, right, sibling)
     use(1, (left, right))
-    copies[4].wait_recv()
+    copies[5].wait_recv()
+    go(9, far, sibling, top)
     copies[6].wait_recv()
+    go(10, far, sibling, bottom)
+    copies[7].wait_recv()
+    copies[8].wait_recv()
     use(2, (over[1], over[2]))
-    copies[3].wait_recv()
-    copies[5].wait_recv()
-    copies.append(go(7, far, sibling))
-    copies[7].wait_recv()
-    use(3, (far, over[3]))
-    for copy in copies:
+    use(3, (far,))
+    copies[9].wait_recv()
+    copies[10].wait_recv()
+    use(4, (over[3],))
+    for copy in copies.values():
         copy.wait_send()
 
 
@@ -259,15 +255,37 @@
     lax.fori_loop(0, 2 * ROWS // TILE, tile, 0)
 
 
-def front_kernel(queries_ref, pairs_ref, out_weight_ref, residual_ref, gain_ref, qk_weight_ref,
-                 vg_weight_ref, hidden_ref, qk_ref, vg_ref,
-                 queries, window, peak, total, out_weight, mix, normed, branch, projected, squares,
-                 qk_weight, vg_weight,
+FAR_FIRST = (4, 3, 5, 2, 6, 1, 7)
+
+
+def straight(raw, weight, at, turn):
+    width = raw.shape[2]
+
+    def step(t, carry):
+        rows = pl.ds(pl.multiple_of(turn * 256 + t * 64, 64), 64)
+        value = raw[rows]
+        weight[rows, at:at + width] = value[:, 0, :]
+        weight[rows, at + width:at + 2 * width] = value[:, 1, :]
+        return carry
+
+    lax.fori_loop(0, 4, step, 0)
+
+
+def layer_kernel(queries_ref, pairs_ref, out_weight_ref, residual_ref, gain_ref, qk_weight_ref,
+                 vg_weight_ref, packed_ref, initial_ref, head_gain_ref, delta_weight_ref, out_ref,
+                 queries, window, peak, total_mix, out_weight, mix, normed, hidden_ref, projected,
+                 squares, qk_raw, vg_raw, weight, delta_weight,
+                 zero_ref, lead_ref, message_ref, slab_prefix,
+                 row, total, column, prefix, first, back, landed,
+                 gate, gated, to_sibling, from_sibling, far, relay, near, arrived,
                  kv_send, kv_recv, ow_send, ow_recv, mix_send, mix_recv, norm_send, norm_recv,
-                 local_sem):
+                 local_sem, row_send, row_recv, col_send, col_recv, back_send, back_recv,
+                 pair_send, pair_recv, out_send, out_recv):
     s, head = lax.axis_index("seq"), lax.axis_index("head")
     seq_count = Y * Z
+    y, z = s // Z, s % Z
     x, c = head // 2, head % 2
+    sibling, to_left, to_right = at_head(x, 1 - c), at_head(x + X - 1, c), at_head(x + 1, c)
 
     def along(d):
         return {"seq": (s + d + seq_count) % seq_count}
@@ -275,24 +293,48 @@
     def other(d):
         return {"head": (head + d) % HEADS}
 
+    def in_row(d):
+        return {"seq": y * Z + (z + d) % Z}
+
+    def in_column(d):
+        return {"seq": ((y + d) % Y) * Z + z}
+
+    own_columns = pl.ds(pl.multiple_of(head * SHARE, SHARE), SHARE)
     locals_ = [
         pltpu.make_async_copy(pairs_ref, window.at[0], local_sem.at[0]),
-        pltpu.make_async_copy(qk_weight_ref, qk_weight, local_sem.at[1]),
-        pltpu.make_async_copy(vg_weight_ref, vg_weight, local_sem.at[2]),
-        pltpu.make_async_copy(
-            out_weight_ref.at[:, pl.ds(pl.multiple_of(head * SHARE, SHARE), SHARE)],
-            out_weight.at[head], local_sem.at[3]),
+        pltpu.make_async_copy(qk_weight_ref, qk_raw, local_sem.at[1]),
+        pltpu.make_async_copy(vg_weight_ref, vg_raw, local_sem.at[2]),
+        pltpu.make_async_copy(out_weight_ref.at[:, own_columns], out_weight.at[head], local_sem.at[3]),
+        pltpu.make_async_copy(delta_weight_ref, delta_weight, local_sem.at[4]),
     ]
-    for copy in locals_:
+    locals_[0].start()
+    greet([along(1), along(-1)] + [other(d) for d in range(1, HEADS)]
+          + [in_row(d) for d in range(1, Z)] + [in_column(d) for d in range(1, Y)])
+
+    half = ROWS // 2
+    halves = (slice(0, half), slice(half, ROWS))
+    hops = {}
+
+    def hop(d, part, by):
+        source = {1: 0, Z: 0}.get(d, d - 1 if by == 1 else d + 1)
+        rows = halves[part]
+        n = 2 * d + part
+        source_ref = pairs_ref.at[rows] if source == 0 else window.at[source, rows]
+        hops[n] = send(source_ref, window.at[d, rows], kv_send.at[n], kv_recv.at[n], along(by))
+
+    def landed_part(d, part, by):
+        hops[2 * d + part].wait_recv()
+        if by == 1 and (d < 3 or (d == 3 and part == 0)):
+            hop(d + 1, part, 1)
+        if by == -1 and (d > 5 or (d == 5 and part == 1)):
+            hop(d - 1, part, -1)
+
+    hop(Z, 1, Z)
+    hop(1, 0, 1)
+    hop(Z, 0, Z)
+    hop(1, 1, 1)
+    for copy in locals_[1:]:
         copy.start()
-    greet([along(1), along(-1), along(-Z)] + [other(d) for d in range(1, HEADS)])
-
-    def hop(n, source, target, by):
-        return send(source, target, kv_send.at[n], kv_recv.at[n], along(by))
-
-    half = ROWS // 2
-    to_next, to_row, before = 1, Z, -1
-    hops = {1: hop(1, pairs_ref, window.at[1], to_next), 8: hop(8, pairs_ref, window.at[8], to_row)}
     weights = []
     for d in range(1, HEADS):
         target = (head + d) % HEADS
@@ -302,140 +344,91 @@
     for g in range(2):
         queries[g * ROWS:(g + 1) * ROWS, :] = queries_ref[:, g * ATTEND_HEAD_SIZE:(g + 1) * ATTEND_HEAD_SIZE]
     locals_[0].wait()
-    attend_block(queries, window, 0, peak, total, "causal")
+    attend_block(queries, window, 0, peak, total_mix, "causal")
 
     def attend_earlier(d):
         @pl.when(s >= d)
         def _():
-            attend_block(queries, window, d, peak, total, "window" if d == Z else None)
-
-    hops[1].wait_recv()
-    hops[2] = hop(2, window.at[1], window.at[2], to_next)
-    hops[8].wait_recv()
-    hops[7] = hop(7, window.at[8], window.at[7], before)
+            attend_block(queries, window, d, peak, total_mix, "window" if d == Z else None)
+
+    def prepare(turn):
+        straight(qk_raw, weight, 0, turn)
+        straight(vg_raw, weight, 2 * KEY_HEADS * DK, turn)
+
+    landed_part(1, 0, 1)
+    landed_part(Z, 1, -1)
+    landed_part(1, 1, 1)
+    landed_part(Z, 0, -1)
     attend_earlier(1)
-    hops[2].wait_recv()
-    hops[3] = hop(3, window.at[2], window.at[3], to_next)
-    hops[7].wait_recv()
-    hops[6] = hop(6, window.at[7], window.at[6], before)
-    attend_earlier(8)
+    landed_part(7, 1, -1)
+    locals_[1].wait()
+    locals_[2].wait()
+    prepare(0)
+    landed_part(2, 0, 1)
+    attend_earlier(Z)
+    landed_part(7, 0, -1)
+    attend_earlier(7)
+    landed_part(2, 1, 1)
+    prepare(1)
+    landed_part(6, 1, -1)
     attend_earlier(2)
-    hops[3].wait_recv()
-    hops[4] = hop(4, window.at[3, 0:half], window.at[4, 0:half], to_next)
-    hops[6].wait_recv()
-    hops[5] = hop(5, window.at[6], window.at[5], before)
-    attend_earlier(7)
+    landed_part(3, 0, 1)
+    prepare(2)
+    landed_part(6, 0, -1)
+    attend_earlier(6)
+    landed_part(3, 1, 1)
+    prepare(3)
+    prepare(4)
+    landed_part(5, 1, -1)
     attend_earlier(3)
-    hops[5].wait_recv()
-    hops[0] = hop(0, window.at[5, half:ROWS], window.at[4, half:ROWS], before)
-    attend_earlier(6)
+    landed_part(4, 0, 1)
+    prepare(5)
+    prepare(6)
+    prepare(7)
+    landed_part(5, 0, -1)
     attend_earlier(5)
-    hops[4].wait_recv()
-    hops[0].wait_recv()
+    landed_part(4, 1, -1)
     attend_earlier(4)
     for g in range(2):
         rows = slice(g * ROWS, (g + 1) * ROWS)
         mix[head, :, g * ATTEND_HEAD_SIZE:(g + 1) * ATTEND_HEAD_SIZE] = (
-            total[rows, :ATTEND_HEAD_SIZE] / total[rows, ATTEND_HEAD_SIZE:]).astype(bf16)
+            total_mix[rows, :ATTEND_HEAD_SIZE] / total_mix[rows, ATTEND_HEAD_SIZE:]).astype(bf16)
     for copy in weights:
         copy.wait()
     locals_[3].wait()
-
-    def add_branch(turn, pair):
-        a, b = pair
-        part = dot(mix[a], out_weight[a]) + dot(mix[b], out_weight[b])
-        branch[...] = part if turn == 0 else branch[...] + part
+    locals_[4].wait()
+    for copy in hops.values():
+        copy.wait_send()
+
+    def add_branch(turn, blocks):
+        part = sum(dot(mix[b], out_weight[b]) for b in blocks)
+        hidden_ref[...] = part if turn == 0 else hidden_ref[...] + part
 
     gather_heads(mix, mix_send, mix_recv, x, c, add_branch)
-    hidden = residual_ref[...].astype(f32) + branch[...]
+    hidden = residual_ref[...].astype(f32) + hidden_ref[...]
     hidden_ref[...] = hidden
-    own = pl.ds(pl.multiple_of(head * SHARE, SHARE), SHARE)
-    normed[head] = (hidden * gain_ref[:, own]).astype(bf16)
-    locals_[1].wait()
-    locals_[2].wait()
-
-    def add_projected(turn, pair):
+    normed[head] = (hidden * gain_ref[:, own_columns]).astype(bf16)
+
+    def add_projected(turn, blocks):
         square = None
-        for block in pair:
+        for block in blocks:
             cols = pl.ds(pl.multiple_of(block * SHARE, SHARE), SHARE)
             value = normed[block].astype(f32) * (1.0 / gain_ref[:, cols])
             value = value * value
             value = value[:, :128] + value[:, 128:]
             square = value if square is None else square + value
         squares[...] = square if turn == 0 else squares[...] + square
-        a, b = (pl.ds(pl.multiple_of(block * SHARE, SHARE), SHARE) for block in pair)
-        for weight, at in ((qk_weight, 0), (vg_weight, 2 * KEY_HEADS * DK)):
-            for column in range(0, weight.shape[1], 256):
-                cols = slice(column, column + 256)
-                part = dot(normed[pair[0]], weight[a, cols]) + dot(normed[pair[1]], weight[b, cols])
-                to = slice(at + column, at + column + 256)
-                projected[:, to] = part if turn == 0 else projected[:, to] + part
+        for at in range(0, PROJECTED, 256):
+            cols = slice(at, at + 256)
+            part = sum(
+                dot(normed[b], weight[pl.ds(pl.multiple_of(b * SHARE, SHARE), SHARE), cols])
+                for b in blocks)
+            projected[:, cols] = part if turn == 0 else projected[:, cols] + part
 
     gather_heads(normed, norm_send, norm_recv, x, c, add_projected)
     inverse = lax.rsqrt(jnp.sum(squares[...], axis=-1, keepdims=True) * (1.0 / MODEL) + epsilon)
-    qk_ref[...] = projected[:, :512] * inverse
-    vg_ref[...] = projected[:, 512:] * inverse
-    for n in range(9):
-        hops[n].wait_send()
-
-
-def front_part(queries, pairs, attention_out, residual, gain, qk_weight, vg_weight):
-    vmem, hbm = pl.BlockSpec(memory_space=pltpu.VMEM), pl.BlockSpec(memory_space=pl.ANY)
-    dma = pltpu.SemaphoreType.DMA
-    return pl.pallas_call(
-        front_kernel,
-        out_shape=(
-            jax.ShapeDtypeStruct((ROWS, SHARE), f32),
-            jax.ShapeDtypeStruct((ROWS, 512), f32),
-            jax.ShapeDtypeStruct((ROWS, 1024), f32),
-        ),
-        in_specs=[vmem, hbm, hbm, vmem, vmem, hbm, hbm],
-        out_specs=[vmem] * 3,
-        scratch_shapes=[
-            pltpu.VMEM((2 * ROWS, ATTEND_HEAD_SIZE), bf16),
-            pltpu.VMEM((Z + 1, ROWS, 2 * ATTEND_HEAD_SIZE), bf16),
-            pltpu.VMEM((2 * ROWS, ATTEND_HEAD_SIZE), f32),
-            pltpu.VMEM((2 * ROWS, 2 * ATTEND_HEAD_SIZE), f32),
-            pltpu.VMEM((HEADS, SHARE, SHARE), bf16),
-            pltpu.VMEM((HEADS, ROWS, SHARE), bf16),
-            pltpu.VMEM((HEADS, ROWS, SHARE), bf16),
-            pltpu.VMEM((ROWS, SHARE), f32),
-            pltpu.VMEM((ROWS, PROJECTED), f32),
-            pltpu.VMEM((ROWS, 128), f32),
-            pltpu.VMEM((MODEL, 512), bf16),
-            pltpu.VMEM((MODEL, 1024), bf16),
-            dma((9,)), dma((9,)), dma((HEADS,)), dma((HEADS,)), dma((8,)), dma((8,)), dma((8,)),
-            dma((8,)), dma((4,)),
-        ],
-        compiler_params=pltpu.CompilerParams(
-            collective_id=0, has_side_effects=True, vmem_limit_bytes=56 * 2**20),
-        name="front",
-    )(queries, pairs, attention_out, residual, gain, qk_weight, vg_weight)
-
-
-FAR_FIRST = (4, 3, 5, 2, 6, 1, 7)
-
-
-def scan_kernel(message_ref, initial_ref, zero_ref, lead_ref, vg_ref, gain_ref, weight_ref,
-                hidden_ref, out_ref,
-                row, total, column, prefix, first, back, landed,
-                gate, gated, to_sibling, from_sibling, far, relay, near, arrived,
-                row_send, row_recv, col_send, col_recv, back_send, back_recv,
-                pair_send, pair_recv, out_send, out_recv):
-    s = lax.axis_index("seq")
-    y, z = s // Z, s % Z
-
-    def in_row(d):
-        return {"seq": y * Z + (z + d) % Z}
-
-    def in_column(d):
-        return {"seq": ((y + d) % Y) * Z + z}
-
-    head = lax.axis_index("head")
-    x, c = head // 2, head % 2
-    sibling, to_left, to_right = at_head(x, 1 - c), at_head(x + X - 1, c), at_head(x + 1, c)
-    greet([in_row(d) for d in range(1, Z)] + [in_column(d) for d in range(1, Y)]
-          + [sibling, to_left, to_right])
+    squares[...] = jnp.broadcast_to(inverse, (ROWS, 128))
+    local_slab(projected, squares, packed_ref, zero_ref, lead_ref, message_ref, slab_prefix)
 
     sends = []
     for d in FAR_FIRST:
@@ -451,8 +444,9 @@
     decay = jnp.ones((1, DK), f32)
     for h in range(VALUE_HEADS):
         cols = slice(h * DV, (h + 1) * DV)
-        u = vg_ref[:, VALUE_HEADS * DV + h * DV:VALUE_HEADS * DV + (h + 1) * DV]
-        gate[:, cols] = gain_ref[...] * (u / (1.0 + jnp.exp(-u)))
+        at = 2 * KEY_HEADS * DK + (VALUE_HEADS + h) * DV
+        u = projected[:, at:at + DV] * squares[...]
+        gate[:, cols] = head_gain_ref[...] * (u / (1.0 + jnp.exp(-u)))
     for copy in sends:
         copy.wait()
     zero = jnp.zeros((DK, DK), f32)
@@ -500,7 +494,7 @@
 
     def partial(d, core):
         at = ((x + d) % X * 2 + core) * SHARE
-        return dot(gated[...], weight_ref[:, pl.ds(pl.multiple_of(at, SHARE), SHARE)])
+        return dot(gated[...], delta_weight[:, pl.ds(pl.multiple_of(at, SHARE), SHARE)])
 
     order, half = (2, 1, X - 1, 0), ROWS // 2
     top, bottom = slice(0, half), slice(half, ROWS)
@@ -534,14 +528,39 @@
         copy.wait_send()
 
 
-def back_part(messages, initial_state, zero_part, lead, value_gate, head_gain, delta_output, hidden):
+def inverse_rms(values):
+    return lax.rsqrt(jnp.mean(values * values, axis=-1, keepdims=True) + epsilon)
+
+
+def body(residual, queries, key_value_pairs, attention_out, norm_gain, query_key_weight,
+         value_gate_weight, write_strength, log_decay, initial_state, head_gain, delta_output):
+    vmem, hbm = pl.BlockSpec(memory_space=pltpu.VMEM), pl.BlockSpec(memory_space=pl.ANY)
     dma = pltpu.SemaphoreType.DMA
+    packed = jnp.concatenate([log_decay, write_strength], axis=0)
     return pl.pallas_call(
-        scan_kernel,
+        layer_kernel,
         out_shape=jax.ShapeDtypeStruct((ROWS, SHARE), bf16),
-        in_specs=[pl.BlockSpec(memory_space=pltpu.VMEM)] * 8,
-        out_specs=pl.BlockSpec(memory_space=pltpu.VMEM),
+        in_specs=[vmem, hbm, hbm, vmem, vmem, hbm, hbm, vmem, vmem, vmem, hbm],
+        out_specs=vmem,
         scratch_shapes=[
+            pltpu.VMEM((2 * ROWS, ATTEND_HEAD_SIZE), bf16),
+            pltpu.VMEM((Z + 1, ROWS, 2 * ATTEND_HEAD_SIZE), bf16),
+            pltpu.VMEM((2 * ROWS, ATTEND_HEAD_SIZE), f32),
+            pltpu.VMEM((2 * ROWS, 2 * ATTEND_HEAD_SIZE), f32),
+            pltpu.VMEM((HEADS, SHARE, SHARE), bf16),
+            pltpu.VMEM((HEADS, ROWS, SHARE), bf16),
+            pltpu.VMEM((HEADS, ROWS, SHARE), bf16),
+            pltpu.VMEM((ROWS, SHARE), f32),
+            pltpu.VMEM((ROWS, PROJECTED), f32),
+            pltpu.VMEM((ROWS, 128), f32),
+            pltpu.VMEM((MODEL, 2, KEY_HEADS * DK), bf16),
+            pltpu.VMEM((MODEL, 2, VALUE_HEADS * DV), bf16),
+            pltpu.VMEM((MODEL, PROJECTED), bf16),
+            pltpu.VMEM((VALUE_HEADS * DV, MODEL), bf16),
+            pltpu.VMEM((ROWS, VALUE_HEADS * DV), f32),
+            pltpu.VMEM((ROWS, VALUE_HEADS * DK), bf16),
+            pltpu.VMEM((Z, MESSAGE, DK), bf16),
+            pltpu.VMEM((VALUE_HEADS, DK, DK + DV), f32),
             pltpu.VMEM((Z, MESSAGE, DK), bf16),
             pltpu.VMEM((MESSAGE, DK), bf16),
             pltpu.VMEM((Y, MESSAGE, DK), bf16),
@@ -557,29 +576,17 @@
             pltpu.VMEM((2, ROWS // 2, SHARE), bf16),
             pltpu.VMEM((2, ROWS, SHARE), bf16),
             pltpu.VMEM((2, ROWS, SHARE), bf16),
+            dma((2 * Z + 2,)), dma((2 * Z + 2,)), dma((HEADS,)), dma((HEADS,)),
+            dma((11,)), dma((11,)), dma((11,)), dma((11,)), dma((5,)),
             dma((Z,)), dma((Z,)), dma((Y,)), dma((Y,)), dma((Z,)), dma((Z,)),
             dma((X,)), dma((X,)), dma((X,)), dma((X,)),
         ],
         compiler_params=pltpu.CompilerParams(
-            collective_id=1, has_side_effects=True, vmem_limit_bytes=48 * 2**20),
-        name="delta_scan_out",
-    )(messages, initial_state, zero_part, lead, value_gate, head_gain, delta_output, hidden)
-
-
-def inverse_rms(values):
-    return lax.rsqrt(jnp.mean(values * values, axis=-1, keepdims=True) + epsilon)
-
-
-def body(residual, queries, key_value_pairs, attention_out, norm_gain, query_key_weight,
-         value_gate_weight, write_strength, log_decay, initial_state, head_gain, delta_output):
-    hidden, query_key, value_gate = front_part(
-        queries, key_value_pairs.reshape(ROWS, 2 * ATTEND_HEAD_SIZE), attention_out, residual,
-        norm_gain.reshape(1, MODEL), query_key_weight.reshape(MODEL, -1),
-        value_gate_weight.reshape(MODEL, -1))
-    packed = jnp.concatenate([log_decay, write_strength], axis=0)
-    zero_part, lead, messages = local_part(query_key, value_gate, packed)
-    return back_part(messages, initial_state, zero_part, lead, value_gate,
-                     head_gain.reshape(1, DV), delta_output, hidden)
+            collective_id=0, has_side_effects=True, vmem_limit_bytes=60 * 2**20),
+        name="layer",
+    )(queries, key_value_pairs.reshape(ROWS, 2 * ATTEND_HEAD_SIZE), attention_out, residual,
+      norm_gain.reshape(1, MODEL), query_key_weight, value_gate_weight, packed, initial_state,
+      head_gain.reshape(1, DV), delta_output)
 
 
 def solution(mesh):

time: 160 us -> 143 us (0.89)
  Pallas kernels: 148 us -> 138 us
  local copies, waits for them, and re-layouts: 11.6 us -> 3.36 us
    pallas_call x3 -> x1, Pallas kernels: 148 us -> 138 us  [body(): pl.pallas_call(layer_kernel, out_shape=jax.ShapeDtypeStruct((ROWS, SHARE)...]
    unnamed x24 -> x2, local copies, waits for them, and re-layouts: 11.6 us -> 3.36 us
where the time goes in v3:
time: 143 us
  Pallas kernels  138 us (97%)
  local copies, waits for them, and re-layouts  3.36 us (2%)
    pallas_call x1, Pallas kernels, body(): pl.pallas_call(layer_kernel, out_shape=jax.ShapeDtypeStruct((ROWS, SHARE)...  138 us
    unnamed x2, local copies, waits for them, and re-layouts  3.36 us

profile of v3, /device:TPU:1, one launch (start us, length us, event | category | flops | bytes accessed | tf_op | source)
XLA Modules:
  0.0 142.5 jit_solution(5914279781048051388)
XLA Ops:
  0.0 1.3 pad_maximum_fusion.packed_ref
  1.3 1.7 %copy.15 = bf16[64,8,2,128]{3,1,2,0:T(8,128)(2,1)} copy(bf16[64,8,2,128]{3,2,1,0:T(2,128)(2,1)} %bitcast.7) | data formatting | bytes 524288
  3.0 137.9 %layer.1 = bf16[512,256]{1,0:T(8,128)(2,1)} custom-call(bf16[512,256]{1,0:T(8,128)(2,1)} %queries_ref.1, bf16[512,256]{1,0:T(8,128)(2,1)} %bitcast.6, bf16[256,2048]{1,0:T(8,128)(2,1)} %out_weight_ref.1, bf16[512,256]{1,0:T(8,128)(2,1)} %residual_ref.1, f32[1,2048]{1,0:T(1,128)} %bitcast.8, bf16[2048,2,256]{2,1,0:T(2,128)(2,1)} %qk_weight_ref.1, ...), custom_call_target="tpu_custom_call" | custom-call | tf_op jit(solution)/shard_map/layer/pallas_call | solution.py:540
  140.9 1.7 %copy.17 = bf16[512,256]{1,0:T(8,128)(2,1)} copy(bf16[512,256]{1,0:T(8,128)(2,1)} %layer.1) | data formatting | bytes 524288

commit v4 on v3

--- a/solution.py
+++ b/solution.py
@@ -211,14 +211,14 @@
     copies[4].wait_recv()
     go(8, right, sibling)
     use(1, (left, right))
+    copies[7].wait_recv()
+    use(2, (over[1],))
     copies[5].wait_recv()
     go(9, far, sibling, top)
     copies[6].wait_recv()
     go(10, far, sibling, bottom)
-    copies[7].wait_recv()
     copies[8].wait_recv()
-    use(2, (over[1], over[2]))
-    use(3, (far,))
+    use(3, (over[2], far))
     copies[9].wait_recv()
     copies[10].wait_recv()
     use(4, (over[3],))
@@ -226,14 +226,23 @@
         copy.wait_send()
 
 
-def attend_block(queries, window, place, peak, total, relation):
+def attend_block(queries, window, pair_now, place, peak, total, relation):
     scale = math.log2(math.e) / math.sqrt(ATTEND_HEAD_SIZE)
     ones = jnp.ones((ROWS, ATTEND_HEAD_SIZE), bf16)
 
+    def straighten(t, carry):
+        rows = pl.ds(pl.multiple_of(t * 128, 128), 128)
+        value = window[place, rows]
+        pair_now[rows, :ATTEND_HEAD_SIZE] = value[:, 0, :]
+        pair_now[rows, ATTEND_HEAD_SIZE:] = value[:, 1, :]
+        return carry
+
+    lax.fori_loop(0, ROWS // 128, straighten, 0)
+
     def tile(t, carry):
         rows = pl.ds(pl.multiple_of(t * TILE, TILE), TILE)
-        keys = window[place, :, :ATTEND_HEAD_SIZE]
-        values = jnp.concatenate([window[place, :, ATTEND_HEAD_SIZE:], ones], axis=1)
+        keys = pair_now[:, :ATTEND_HEAD_SIZE]
+        values = jnp.concatenate([pair_now[:, ATTEND_HEAD_SIZE:], ones], axis=1)
         scores = mm_nt(queries[rows, :], keys) * scale
         if relation is not None:
             i, j = grid_of(TILE, ROWS)
@@ -272,12 +281,12 @@
 
 
 def layer_kernel(queries_ref, pairs_ref, out_weight_ref, residual_ref, gain_ref, qk_weight_ref,
-                 vg_weight_ref, packed_ref, initial_ref, head_gain_ref, delta_weight_ref, out_ref,
-                 queries, window, peak, total_mix, out_weight, mix, normed, hidden_ref, projected,
+                 vg_weight_ref, decay_ref, strength_ref, initial_ref, head_gain_ref, delta_weight_ref, out_ref,
+                 packed_ref, pair_now, queries, window, peak, total_mix, out_weight, mix, normed, hidden_ref, projected,
                  squares, qk_raw, vg_raw, weight, delta_weight,
                  zero_ref, lead_ref, message_ref, slab_prefix,
                  row, total, column, prefix, first, back, landed,
-                 gate, gated, to_sibling, from_sibling, far, relay, near, arrived,
+                 gate, gated, to_sibling, from_sibling, far, relay, waiting, near, arrived,
                  kv_send, kv_recv, ow_send, ow_recv, mix_send, mix_recv, norm_send, norm_recv,
                  local_sem, row_send, row_recv, col_send, col_recv, back_send, back_recv,
                  pair_send, pair_recv, out_send, out_recv):
@@ -294,7 +303,7 @@
         return {"head": (head + d) % HEADS}
 
     def in_row(d):
-        return {"seq": y * Z + (z + d) % Z}
+        return {"seq": y * Z + (z + d + Z) % Z}
 
     def in_column(d):
         return {"seq": ((y + d) % Y) * Z + z}
@@ -315,24 +324,40 @@
     halves = (slice(0, half), slice(half, ROWS))
     hops = {}
 
+    def describe(d, part, source, device):
+        rows, n = halves[part], 2 * d + part
+        return pltpu.make_async_remote_copy(
+            src_ref=pairs_ref.at[rows] if source == 0 else window.at[source, rows],
+            dst_ref=window.at[d, rows], send_sem=kv_send.at[n], recv_sem=kv_recv.at[n],
+            device_id=device, device_id_type=MESH)
+
+    def first_hop(d, part, source, device):
+        describe(d, part, source, device).start()
+
     def hop(d, part, by):
-        source = {1: 0, Z: 0}.get(d, d - 1 if by == 1 else d + 1)
-        rows = halves[part]
-        n = 2 * d + part
-        source_ref = pairs_ref.at[rows] if source == 0 else window.at[source, rows]
-        hops[n] = send(source_ref, window.at[d, rows], kv_send.at[n], kv_recv.at[n], along(by))
+        source = 0 if d == Z else d - 1 if by == 1 else d + 1
+        hops[2 * d + part] = describe(d, part, source, along(by))
+        hops[2 * d + part].start()
 
     def landed_part(d, part, by):
         hops[2 * d + part].wait_recv()
+        if d == Z:
+            pl.when(z == Z - 1)(lambda: first_hop(1, part, Z, in_row(1)))
+            pl.when(z != 0)(lambda: first_hop(Z - 1, part, Z, along(-1)))
+            return
         if by == 1 and (d < 3 or (d == 3 and part == 0)):
             hop(d + 1, part, 1)
         if by == -1 and (d > 5 or (d == 5 and part == 1)):
             hop(d - 1, part, -1)
 
     hop(Z, 1, Z)
-    hop(1, 0, 1)
     hop(Z, 0, Z)
-    hop(1, 1, 1)
+    for part in range(2):
+        hops[2 + part] = describe(1, part, 0, along(1))
+        hops[2 * (Z - 1) + part] = describe(Z - 1, part, 0, along(-1))
+    for part in range(2):
+        pl.when(z != Z - 1)(lambda: first_hop(1, part, 0, along(1)))
+        pl.when(z == 0)(lambda: first_hop(Z - 1, 1 - part, 0, in_row(-1)))
     for copy in locals_[1:]:
         copy.start()
     weights = []
@@ -343,22 +368,24 @@
             out_weight.at[head], ow_send.at[d], ow_recv.at[d], other(d)))
     for g in range(2):
         queries[g * ROWS:(g + 1) * ROWS, :] = queries_ref[:, g * ATTEND_HEAD_SIZE:(g + 1) * ATTEND_HEAD_SIZE]
+    packed_ref[:VALUE_HEADS, :] = decay_ref[...]
+    packed_ref[VALUE_HEADS:, :] = strength_ref[...]
     locals_[0].wait()
-    attend_block(queries, window, 0, peak, total_mix, "causal")
+    attend_block(queries, window, pair_now, 0, peak, total_mix, "causal")
 
     def attend_earlier(d):
         @pl.when(s >= d)
         def _():
-            attend_block(queries, window, d, peak, total_mix, "window" if d == Z else None)
+            attend_block(queries, window, pair_now, d, peak, total_mix, "window" if d == Z else None)
 
     def prepare(turn):
         straight(qk_raw, weight, 0, turn)
         straight(vg_raw, weight, 2 * KEY_HEADS * DK, turn)
 
+    landed_part(Z, 1, -1)
     landed_part(1, 0, 1)
-    landed_part(Z, 1, -1)
+    landed_part(Z, 0, -1)
     landed_part(1, 1, 1)
-    landed_part(Z, 0, -1)
     attend_earlier(1)
     landed_part(7, 1, -1)
     locals_[1].wait()
@@ -498,33 +525,49 @@
 
     order, half = (2, 1, X - 1, 0), ROWS // 2
     top, bottom = slice(0, half), slice(half, ROWS)
-    pairs = []
-    for n, d in enumerate(order):
-        to_sibling[n] = partial(d, 1 - c).astype(bf16)
-        pairs.append(send(to_sibling.at[n], from_sibling.at[n], pair_send.at[n], pair_recv.at[n], sibling))
-    sends = []
+    pairs, sends = {}, {}
+
+    def over_pair(n):
+        to_sibling[n] = partial(order[n], 1 - c).astype(bf16)
+        pairs[n] = send(to_sibling.at[n], from_sibling.at[n], pair_send.at[n], pair_recv.at[n], sibling)
+
+    def out_send_rows(n, source, target, device):
+        sends[n] = send(source, target, out_send.at[n], out_recv.at[n], device)
+
+    over_pair(0)
+    over_pair(1)
+    value = partial(2, c)
     pairs[0].wait_recv()
-    far[...] = (partial(2, c) + from_sibling[0].astype(f32)).astype(bf16)
-    sends.append(send(far.at[top], relay.at[0], out_send.at[0], out_recv.at[0], to_right))
-    sends.append(send(far.at[bottom], relay.at[1], out_send.at[1], out_recv.at[1], to_left))
-    for n, rows, device in ((1, top, to_right), (2, bottom, to_left)):
-        value = partial(order[n], c)
-        pairs[n].wait_recv()
-        value = value + from_sibling[n].astype(f32)
-        sends[n - 1].wait_recv()
-        passed = relay[n - 1].astype(f32)
-        if n == 1:
-            near[0] = jnp.concatenate([value[top] + passed, value[bottom]], axis=0).astype(bf16)
-        else:
-            near[1] = jnp.concatenate([value[top], value[bottom] + passed], axis=0).astype(bf16)
-        sends.append(send(near.at[n - 1], arrived.at[n - 1], out_send.at[n + 1], out_recv.at[n + 1], device))
+    far[...] = (value + from_sibling[0].astype(f32)).astype(bf16)
+    out_send_rows(0, far.at[top], relay.at[0], to_right)
+    out_send_rows(1, far.at[bottom], relay.at[1], to_left)
+    over_pair(2)
+    value = partial(order[1], c)
+    pairs[1].wait_recv()
+    value = value + from_sibling[1].astype(f32)
+    near[0, bottom] = value[bottom].astype(bf16)
+    out_send_rows(2, near.at[0, bottom], arrived.at[0, bottom], to_right)
+    waiting[0] = value[top]
+    value = partial(order[2], c)
+    pairs[2].wait_recv()
+    value = value + from_sibling[2].astype(f32)
+    near[1, top] = value[top].astype(bf16)
+    out_send_rows(3, near.at[1, top], arrived.at[1, top], to_left)
+    waiting[1] = value[bottom]
+    over_pair(3)
+    sends[0].wait_recv()
+    near[0, top] = (waiting[0] + relay[0].astype(f32)).astype(bf16)
+    out_send_rows(4, near.at[0, top], arrived.at[0, top], to_right)
+    sends[1].wait_recv()
+    near[1, bottom] = (waiting[1] + relay[1].astype(f32)).astype(bf16)
+    out_send_rows(5, near.at[1, bottom], arrived.at[1, bottom], to_left)
     value = hidden_ref[...] + partial(0, c)
     pairs[3].wait_recv()
     value = value + from_sibling[3].astype(f32)
-    sends[2].wait_recv()
-    sends[3].wait_recv()
+    for n in range(2, 6):
+        sends[n].wait_recv()
     out_ref[...] = (value + arrived[0].astype(f32) + arrived[1].astype(f32)).astype(bf16)
-    for copy in pairs + sends:
+    for copy in list(pairs.values()) + list(sends.values()):
         copy.wait_send()
 
 
@@ -536,15 +579,16 @@
          value_gate_weight, write_strength, log_decay, initial_state, head_gain, delta_output):
     vmem, hbm = pl.BlockSpec(memory_space=pltpu.VMEM), pl.BlockSpec(memory_space=pl.ANY)
     dma = pltpu.SemaphoreType.DMA
-    packed = jnp.concatenate([log_decay, write_strength], axis=0)
     return pl.pallas_call(
         layer_kernel,
         out_shape=jax.ShapeDtypeStruct((ROWS, SHARE), bf16),
-        in_specs=[vmem, hbm, hbm, vmem, vmem, hbm, hbm, vmem, vmem, vmem, hbm],
+        in_specs=[vmem, hbm, hbm, vmem, vmem, hbm, hbm, vmem, vmem, vmem, vmem, hbm],
         out_specs=vmem,
         scratch_shapes=[
+            pltpu.VMEM((2 * VALUE_HEADS, ROWS), f32),
+            pltpu.VMEM((ROWS, 2 * ATTEND_HEAD_SIZE), bf16),
             pltpu.VMEM((2 * ROWS, ATTEND_HEAD_SIZE), bf16),
-            pltpu.VMEM((Z + 1, ROWS, 2 * ATTEND_HEAD_SIZE), bf16),
+            pltpu.VMEM((Z + 1, ROWS, 2, ATTEND_HEAD_SIZE), bf16),
             pltpu.VMEM((2 * ROWS, ATTEND_HEAD_SIZE), f32),
             pltpu.VMEM((2 * ROWS, 2 * ATTEND_HEAD_SIZE), f32),
             pltpu.VMEM((HEADS, SHARE, SHARE), bf16),
@@ -574,18 +618,20 @@
             pltpu.VMEM((X, ROWS, SHARE), bf16),
             pltpu.VMEM((ROWS, SHARE), bf16),
             pltpu.VMEM((2, ROWS // 2, SHARE), bf16),
+            pltpu.VMEM((2, ROWS // 2, SHARE), f32),
             pltpu.VMEM((2, ROWS, SHARE), bf16),
             pltpu.VMEM((2, ROWS, SHARE), bf16),
             dma((2 * Z + 2,)), dma((2 * Z + 2,)), dma((HEADS,)), dma((HEADS,)),
             dma((11,)), dma((11,)), dma((11,)), dma((11,)), dma((5,)),
             dma((Z,)), dma((Z,)), dma((Y,)), dma((Y,)), dma((Z,)), dma((Z,)),
-            dma((X,)), dma((X,)), dma((X,)), dma((X,)),
+            dma((X,)), dma((X,)), dma((6,)), dma((6,)),
         ],
         compiler_params=pltpu.CompilerParams(
             collective_id=0, has_side_effects=True, vmem_limit_bytes=60 * 2**20),
         name="layer",
-    )(queries, key_value_pairs.reshape(ROWS, 2 * ATTEND_HEAD_SIZE), attention_out, residual,
-      norm_gain.reshape(1, MODEL), query_key_weight, value_gate_weight, packed, initial_state,
+    )(queries, key_value_pairs, attention_out, residual,
+      norm_gain.reshape(1, MODEL), query_key_weight, value_gate_weight, log_decay, write_strength,
+      initial_state,
       head_gain.reshape(1, DV), delta_output)
 
 

time: 143 us -> 137 us (0.958)
  Pallas kernels: 138 us -> 136 us
  local copies, waits for them, and re-layouts: 3.36 us -> 1.67 us
    pallas_call x1, Pallas kernels: 138 us -> 136 us  [body(): pl.pallas_call(layer_kernel, out_shape=jax.ShapeDtypeStruct((ROWS, SHARE)...]
    unnamed x2 -> x1, local copies, waits for them, and re-layouts: 3.36 us -> 1.67 us
where the time goes in v4:
time: 137 us
  Pallas kernels  136 us (99%)
  local copies, waits for them, and re-layouts  1.67 us (1%)
    pallas_call x1, Pallas kernels, body(): pl.pallas_call(layer_kernel, out_shape=jax.ShapeDtypeStruct((ROWS, SHARE)...  136 us

profile of v4, /device:TPU:1, one launch (start us, length us, event | category | flops | bytes accessed | tf_op | source)
XLA Modules:
  0.0 137.3 jit_solution(13505262746964935573)
XLA Ops:
  0.0 135.7 %layer.1 = bf16[512,256]{1,0:T(8,128)(2,1)} custom-call(bf16[512,256]{1,0:T(8,128)(2,1)} %queries_ref.1, bf16[512,2,128]{2,1,0:T(2,128)(2,1)} %pairs_ref.1, bf16[256,2048]{1,0:T(8,128)(2,1)} %out_weight_ref.1, bf16[512,256]{1,0:T(8,128)(2,1)} %residual_ref.1, f32[1,2048]{1,0:T(1,128)} %bitcast.2, bf16[2048,2,256]{2,1,0:T(2,128)(2,1)} %qk_weight_ref.1, ...), custom_call_target="tpu_custom_call" | custom-call | tf_op jit(solution)/shard_map/layer/pallas_call | solution.py:582
  135.7 1.7 %copy.14 = bf16[512,256]{1,0:T(8,128)(2,1)} copy(bf16[512,256]{1,0:T(8,128)(2,1)} %layer.1) | data formatting | bytes 524288

commit v5 on v4

--- a/solution.py
+++ b/solution.py
@@ -16,7 +16,8 @@
 MODEL = 2048
 SHARE = 256
 PROJECTED = 1536
-TILE = 256
+TILE = 128
+TOGETHER = 4
 CHUNK = 128
 ROWS = 512
 KEY_HEADS = 2
@@ -185,43 +186,42 @@
 
 def gather_heads(blocks, send_sem, recv_sem, x, c, use):
     mid = ROWS // 2
-    top, bottom = slice(0, mid), slice(mid, ROWS)
-    own, left, right, far = (((x + d) % X) * 2 + c for d in (0, X - 1, 1, 2))
-    over = [((x + d) % X) * 2 + 1 - c for d in (0, X - 1, 1, 2)]
+    every, top, bottom = slice(0, ROWS), slice(0, mid), slice(mid, ROWS)
+    left, right, far = (x + X - 1) % X, (x + 1) % X, (x + 2) % X
     sibling, to_left, to_right = at_head(x, 1 - c), at_head(x + X - 1, c), at_head(x + 1, c)
+    mine = pl.ds(pl.multiple_of(c * SHARE, SHARE), SHARE)
     copies = {}
 
-    def go(n, block, device, rows=None):
-        ref = blocks.at[block] if rows is None else blocks.at[block, rows]
+    def go(n, chip, device, rows):
+        ref = blocks.at[chip, rows, mine]
         copies[n] = send(ref, ref, send_sem.at[n], recv_sem.at[n], device)
 
-    go(1, own, to_right, top)
-    go(3, own, to_left, bottom)
-    go(0, own, sibling)
-    go(2, own, to_right, bottom)
-    go(4, own, to_left, top)
+    go(1, x, to_right, top)
+    go(3, x, to_left, bottom)
+    go(0, x, sibling, every)
+    go(2, x, to_right, bottom)
+    go(4, x, to_left, top)
     copies[0].wait_recv()
-    use(0, (own, over[0]))
+    use(0, x)
     copies[1].wait_recv()
     go(5, left, to_right, top)
     copies[3].wait_recv()
     go(6, right, to_left, bottom)
     copies[2].wait_recv()
-    go(7, left, sibling)
+    go(7, left, sibling, every)
     copies[4].wait_recv()
-    go(8, right, sibling)
-    use(1, (left, right))
+    go(8, right, sibling, every)
     copies[7].wait_recv()
-    use(2, (over[1],))
+    use(1, left)
     copies[5].wait_recv()
     go(9, far, sibling, top)
     copies[6].wait_recv()
     go(10, far, sibling, bottom)
     copies[8].wait_recv()
-    use(3, (over[2], far))
+    use(2, right)
     copies[9].wait_recv()
     copies[10].wait_recv()
-    use(4, (over[3],))
+    use(3, far)
     for copy in copies.values():
         copy.wait_send()
 
@@ -239,29 +239,28 @@
 
     lax.fori_loop(0, ROWS // 128, straighten, 0)
 
-    def tile(t, carry):
-        rows = pl.ds(pl.multiple_of(t * TILE, TILE), TILE)
-        keys = pair_now[:, :ATTEND_HEAD_SIZE]
-        values = jnp.concatenate([pair_now[:, ATTEND_HEAD_SIZE:], ones], axis=1)
-        scores = mm_nt(queries[rows, :], keys) * scale
-        if relation is not None:
-            i, j = grid_of(TILE, ROWS)
-            i = i + lax.rem(t, ROWS // TILE) * TILE
-            scores = jnp.where(i >= j if relation == "causal" else i < j, scores, -jnp.inf)
-        block_peak = jnp.max(scores, axis=-1, keepdims=True)
-        if relation == "causal":
-            weights = jnp.exp2(scores - block_peak).astype(bf16)
-            total[rows, :] = dot(weights, values)
-            peak[rows, :] = jnp.broadcast_to(block_peak, (TILE, ATTEND_HEAD_SIZE))
-        else:
-            before = peak[rows, :1]
-            now = jnp.maximum(before, block_peak)
-            weights = jnp.exp2(scores - now).astype(bf16)
-            total[rows, :] = total[rows, :] * jnp.exp2(before - now) + dot(weights, values)
-            peak[rows, :] = jnp.broadcast_to(now, (TILE, ATTEND_HEAD_SIZE))
-        return carry
-
-    lax.fori_loop(0, 2 * ROWS // TILE, tile, 0)
+    keys = pair_now[:, :ATTEND_HEAD_SIZE]
+    values = jnp.concatenate([pair_now[:, ATTEND_HEAD_SIZE:], ones], axis=1)
+    tiles = 2 * ROWS // TILE
+    for start in range(0, tiles, TOGETHER):
+        group = [slice(t * TILE, (t + 1) * TILE) for t in range(start, start + TOGETHER)]
+        all_scores = [mm_nt(queries[rows, :], keys) * scale for rows in group]
+        for rows, scores in zip(group, all_scores):
+            if relation is not None:
+                i, j = grid_of(TILE, ROWS)
+                i = i + rows.start % ROWS
+                scores = jnp.where(i >= j if relation == "causal" else i < j, scores, -jnp.inf)
+            block_peak = jnp.max(scores, axis=-1, keepdims=True)
+            if relation == "causal":
+                weights = jnp.exp2(scores - block_peak).astype(bf16)
+                total[rows, :] = dot(weights, values)
+                peak[rows, :] = jnp.broadcast_to(block_peak, (TILE, ATTEND_HEAD_SIZE))
+            else:
+                before = peak[rows, :1]
+                now = jnp.maximum(before, block_peak)
+                weights = jnp.exp2(scores - now).astype(bf16)
+                total[rows, :] = total[rows, :] * jnp.exp2(before - now) + dot(weights, values)
+                peak[rows, :] = jnp.broadcast_to(now, (TILE, ATTEND_HEAD_SIZE))
 
 
 FAR_FIRST = (4, 3, 5, 2, 6, 1, 7)
@@ -313,7 +312,7 @@
         pltpu.make_async_copy(pairs_ref, window.at[0], local_sem.at[0]),
         pltpu.make_async_copy(qk_weight_ref, qk_raw, local_sem.at[1]),
         pltpu.make_async_copy(vg_weight_ref, vg_raw, local_sem.at[2]),
-        pltpu.make_async_copy(out_weight_ref.at[:, own_columns], out_weight.at[head], local_sem.at[3]),
+        pltpu.make_async_copy(out_weight_ref.at[:, own_columns], out_weight.at[own_columns], local_sem.at[3]),
         pltpu.make_async_copy(delta_weight_ref, delta_weight, local_sem.at[4]),
     ]
     locals_[0].start()
@@ -365,7 +364,7 @@
         target = (head + d) % HEADS
         weights.append(send(
             out_weight_ref.at[:, pl.ds(pl.multiple_of(target * SHARE, SHARE), SHARE)],
-            out_weight.at[head], ow_send.at[d], ow_recv.at[d], other(d)))
+            out_weight.at[own_columns], ow_send.at[d], ow_recv.at[d], other(d)))
     for g in range(2):
         queries[g * ROWS:(g + 1) * ROWS, :] = queries_ref[:, g * ATTEND_HEAD_SIZE:(g + 1) * ATTEND_HEAD_SIZE]
     packed_ref[:VALUE_HEADS, :] = decay_ref[...]
@@ -418,7 +417,8 @@
     attend_earlier(4)
     for g in range(2):
         rows = slice(g * ROWS, (g + 1) * ROWS)
-        mix[head, :, g * ATTEND_HEAD_SIZE:(g + 1) * ATTEND_HEAD_SIZE] = (
+        at = pl.ds(pl.multiple_of(c * SHARE + g * ATTEND_HEAD_SIZE, ATTEND_HEAD_SIZE), ATTEND_HEAD_SIZE)
+        mix[x, :, at] = (
             total_mix[rows, :ATTEND_HEAD_SIZE] / total_mix[rows, ATTEND_HEAD_SIZE:]).astype(bf16)
     for copy in weights:
         copy.wait()
@@ -427,30 +427,28 @@
     for copy in hops.values():
         copy.wait_send()
 
-    def add_branch(turn, blocks):
-        part = sum(dot(mix[b], out_weight[b]) for b in blocks)
+    def of_chip(chip):
+        return pl.ds(pl.multiple_of(chip * 2 * SHARE, 2 * SHARE), 2 * SHARE)
+
+    def add_branch(turn, chip):
+        part = dot(mix[chip], out_weight[of_chip(chip), :])
         hidden_ref[...] = part if turn == 0 else hidden_ref[...] + part
 
     gather_heads(mix, mix_send, mix_recv, x, c, add_branch)
     hidden = residual_ref[...].astype(f32) + hidden_ref[...]
     hidden_ref[...] = hidden
-    normed[head] = (hidden * gain_ref[:, own_columns]).astype(bf16)
-
-    def add_projected(turn, blocks):
-        square = None
-        for block in blocks:
-            cols = pl.ds(pl.multiple_of(block * SHARE, SHARE), SHARE)
-            value = normed[block].astype(f32) * (1.0 / gain_ref[:, cols])
-            value = value * value
-            value = value[:, :128] + value[:, 128:]
-            square = value if square is None else square + value
-        squares[...] = square if turn == 0 else squares[...] + square
+    normed[x, :, pl.ds(pl.multiple_of(c * SHARE, SHARE), SHARE)] = (hidden * gain_ref[:, own_columns]).astype(bf16)
+
+    def add_projected(turn, chip):
         for at in range(0, PROJECTED, 256):
             cols = slice(at, at + 256)
-            part = sum(
-                dot(normed[b], weight[pl.ds(pl.multiple_of(b * SHARE, SHARE), SHARE), cols])
-                for b in blocks)
+            part = dot(normed[chip], weight[of_chip(chip), cols])
             projected[:, cols] = part if turn == 0 else projected[:, cols] + part
+        value = normed[chip].astype(f32) * (1.0 / gain_ref[:, of_chip(chip)])
+        value = value * value
+        value = value[:, :256] + value[:, 256:]
+        square = value[:, :128] + value[:, 128:]
+        squares[...] = square if turn == 0 else squares[...] + square
 
     gather_heads(normed, norm_send, norm_recv, x, c, add_projected)
     inverse = lax.rsqrt(jnp.sum(squares[...], axis=-1, keepdims=True) * (1.0 / MODEL) + epsilon)
@@ -591,9 +589,9 @@
             pltpu.VMEM((Z + 1, ROWS, 2, ATTEND_HEAD_SIZE), bf16),
             pltpu.VMEM((2 * ROWS, ATTEND_HEAD_SIZE), f32),
             pltpu.VMEM((2 * ROWS, 2 * ATTEND_HEAD_SIZE), f32),
-            pltpu.VMEM((HEADS, SHARE, SHARE), bf16),
-            pltpu.VMEM((HEADS, ROWS, SHARE), bf16),
-            pltpu.VMEM((HEADS, ROWS, SHARE), bf16),
+            pltpu.VMEM((MODEL, SHARE), bf16),
+            pltpu.VMEM((X, ROWS, 2 * SHARE), bf16),
+            pltpu.VMEM((X, ROWS, 2 * SHARE), bf16),
             pltpu.VMEM((ROWS, SHARE), f32),
             pltpu.VMEM((ROWS, PROJECTED), f32),
             pltpu.VMEM((ROWS, 128), f32),

time: 137 us -> 130 us (0.949)
  Pallas kernels: 136 us -> 128 us
    pallas_call x1, Pallas kernels: 136 us -> 128 us  [body(): pl.pallas_call(layer_kernel, out_shape=jax.ShapeDtypeStruct((ROWS, SHARE)...]
where the time goes in v5:
time: 130 us
  Pallas kernels  128 us (98%)
  local copies, waits for them, and re-layouts  1.67 us (1%)
    pallas_call x1, Pallas kernels, body(): pl.pallas_call(layer_kernel, out_shape=jax.ShapeDtypeStruct((ROWS, SHARE)...  128 us

profile of v5, /device:TPU:1, one launch (start us, length us, event | category | flops | bytes accessed | tf_op | source)
XLA Modules:
  0.0 130.0 jit_solution(9084312095848655228)
XLA Ops:
  0.0 128.4 %layer.1 = bf16[512,256]{1,0:T(8,128)(2,1)} custom-call(bf16[512,256]{1,0:T(8,128)(2,1)} %queries_ref.1, bf16[512,2,128]{2,1,0:T(2,128)(2,1)} %pairs_ref.1, bf16[256,2048]{1,0:T(8,128)(2,1)} %out_weight_ref.1, bf16[512,256]{1,0:T(8,128)(2,1)} %residual_ref.1, f32[1,2048]{1,0:T(1,128)} %bitcast.2, bf16[2048,2,256]{2,1,0:T(2,128)(2,1)} %qk_weight_ref.1, ...), custom_call_target="tpu_custom_call" | custom-call | tf_op jit(solution)/shard_map/layer/pallas_call | solution.py:580
  128.4 1.7 %copy.14 = bf16[512,256]{1,0:T(8,128)(2,1)} copy(bf16[512,256]{1,0:T(8,128)(2,1)} %layer.1) | data formatting | bytes 524288

commit v6 on v5

--- a/solution.py
+++ b/solution.py
@@ -22,6 +22,7 @@
 ROWS = 512
 KEY_HEADS = 2
 VALUE_HEADS = 4
+CHUNKS = VALUE_HEADS * ROWS // CHUNK
 Z = 8
 Y = 4
 HALF = DV // 2
@@ -79,7 +80,7 @@
     return jnp.sum(block.astype(f32), axis=0, keepdims=True)
 
 
-def local_slab(projected, inverse_ref, packed_ref, zero_ref, lead_ref, message_ref, prefix):
+def local_slab(projected, inverse_ref, packed_ref, message_ref, prefix, mixing, both, before_ref, query):
     i, j = grid_of(CHUNK, CHUNK)
     inclusive, strict = i >= j, i > j
     eye = (i == j).astype(f32)
@@ -117,7 +118,7 @@
                 ratio = jnp.where(inclusive, jnp.exp(jnp.minimum(cum_col - cum_row, 0.0)), 0.0)
                 coupling = jnp.where(strict, strength_col * ratio * key_key, 0.0)
                 items.append(dict(
-                    h=h, rows=rows, q=q, k=k, k_t=k_t, coupling=coupling, mixing=ratio * query_key,
+                    h=h, n=(t * per_turn + u) * VALUE_HEADS + h, rows=rows, q=q, k=k, k_t=k_t, coupling=coupling, mixing=ratio * query_key,
                     cum_col=cum_col, cum_row=cum_row, strength_row=strength_row,
                     inverse=eye - jnp.where((i // 2) == (j // 2), coupling, 0.0)))
         size = 2
@@ -135,19 +136,17 @@
             w = mm(scaled * jnp.exp(it["cum_row"]), it["k"])
             u = mm(scaled, v)
             it["wu"] = jnp.concatenate([w, u], axis=1).astype(bf16)
+            both[it["n"]] = it["wu"]
+            mixing[it["n"]] = it["mixing"].astype(bf16)
+            query[it["n"]] = jnp.exp(it["cum_col"]) * it["q"]
         for it in items:
-            mixed = mm(it["mixing"], it["wu"])
-            it["lead"] = jnp.exp(it["cum_col"]) * it["q"] - mixed[:, :DK]
-            it["own"] = mixed[:, DK:]
             end = it["cum_row"][:, CHUNK - 1:]
             it["end"] = jnp.exp(end)
             it["step"] = mm(it["k_t"] * jnp.exp(end - it["cum_row"]), it["wu"])
         for it in items:
             h = it["h"]
             before = prefix[h]
-            out = mm(it["lead"], before)
-            lead_ref[it["rows"], h * DK:(h + 1) * DK] = out[:, :DK].astype(bf16)
-            zero_ref[it["rows"], h * DV:(h + 1) * DV] = out[:, DK:] + it["own"]
+            before_ref[it["n"]] = before.astype(bf16)
             offset = jnp.concatenate([jnp.zeros((DK, DK), f32), it["step"][:, DK:]], axis=1)
             prefix[h] = it["end"] * before - mm(it["step"][:, :DK], before) + offset
         return carry
@@ -163,6 +162,20 @@
             message_ref[2 * h + c, :DK] = change
             message_ref[2 * h + c, DK:DK + HALF] = offset[c * HALF:(c + 1) * HALF]
             message_ref[2 * h + c, DK + HALF:] = tail
+
+
+def slab_outputs(zero_ref, lead_ref, mixing, both, before_ref, query):
+    def turn(t, carry):
+        rows = pl.ds(pl.multiple_of(t * CHUNK, CHUNK), CHUNK)
+        places = [t * VALUE_HEADS + h for h in range(VALUE_HEADS)]
+        mixed = [dot(mixing[n], both[n]) for n in places]
+        out = [mm(query[n] - m[:, :DK], before_ref[n]) for n, m in zip(places, mixed)]
+        for h in range(VALUE_HEADS):
+            lead_ref[rows, h * DK:(h + 1) * DK] = out[h][:, :DK].astype(bf16)
+            zero_ref[rows, h * DV:(h + 1) * DV] = out[h][:, DK:] + mixed[h][:, DK:]
+        return carry
+
+    lax.fori_loop(0, ROWS // CHUNK, turn, 0)
 
 
 def at_head(x, c):
@@ -283,7 +296,7 @@
                  vg_weight_ref, decay_ref, strength_ref, initial_ref, head_gain_ref, delta_weight_ref, out_ref,
                  packed_ref, pair_now, queries, window, peak, total_mix, out_weight, mix, normed, hidden_ref, projected,
                  squares, qk_raw, vg_raw, weight, delta_weight,
-                 zero_ref, lead_ref, message_ref, slab_prefix,
+                 zero_ref, lead_ref, message_ref, slab_prefix, mixing, both, before_ref, query,
                  row, total, column, prefix, first, back, landed,
                  gate, gated, to_sibling, from_sibling, far, relay, waiting, near, arrived,
                  kv_send, kv_recv, ow_send, ow_recv, mix_send, mix_recv, norm_send, norm_recv,
@@ -440,7 +453,7 @@
     normed[x, :, pl.ds(pl.multiple_of(c * SHARE, SHARE), SHARE)] = (hidden * gain_ref[:, own_columns]).astype(bf16)
 
     def add_projected(turn, chip):
-        for at in range(0, PROJECTED, 256):
+        for at in range(0, PROJECTED - VALUE_HEADS * DV, 256):
             cols = slice(at, at + 256)
             part = dot(normed[chip], weight[of_chip(chip), cols])
             projected[:, cols] = part if turn == 0 else projected[:, cols] + part
@@ -453,7 +466,7 @@
     gather_heads(normed, norm_send, norm_recv, x, c, add_projected)
     inverse = lax.rsqrt(jnp.sum(squares[...], axis=-1, keepdims=True) * (1.0 / MODEL) + epsilon)
     squares[...] = jnp.broadcast_to(inverse, (ROWS, 128))
-    local_slab(projected, squares, packed_ref, zero_ref, lead_ref, message_ref, slab_prefix)
+    local_slab(projected, squares, packed_ref, message_ref, slab_prefix, mixing, both, before_ref, query)
 
     sends = []
     for d in FAR_FIRST:
@@ -467,6 +480,10 @@
     i, j = grid_of(DK + HALF, DK)
     run = (i == j).astype(f32)
     decay = jnp.ones((1, DK), f32)
+    slab_outputs(zero_ref, lead_ref, mixing, both, before_ref, query)
+    for at in range(PROJECTED - VALUE_HEADS * DV, PROJECTED, 256):
+        projected[:, at:at + 256] = sum(
+            dot(normed[chip], weight[of_chip(chip), at:at + 256]) for chip in range(X))
     for h in range(VALUE_HEADS):
         cols = slice(h * DV, (h + 1) * DV)
         at = 2 * KEY_HEADS * DK + (VALUE_HEADS + h) * DV
@@ -603,6 +620,10 @@
             pltpu.VMEM((ROWS, VALUE_HEADS * DK), bf16),
             pltpu.VMEM((Z, MESSAGE, DK), bf16),
             pltpu.VMEM((VALUE_HEADS, DK, DK + DV), f32),
+            pltpu.VMEM((CHUNKS, CHUNK, CHUNK), bf16),
+            pltpu.VMEM((CHUNKS, CHUNK, DK + DV), bf16),
+            pltpu.VMEM((CHUNKS, DK, DK + DV), bf16),
+            pltpu.VMEM((CHUNKS, CHUNK, DK), f32),
             pltpu.VMEM((Z, MESSAGE, DK), bf16),
             pltpu.VMEM((MESSAGE, DK), bf16),
             pltpu.VMEM((Y, MESSAGE, DK), bf16),

time: 130 us -> 129 us (level)
  no operation moved by 1% of the time
where the time goes in v6:
time: 129 us
  Pallas kernels  128 us (99%)
  local copies, waits for them, and re-layouts  1.67 us (1%)
    pallas_call x1, Pallas kernels, body(): pl.pallas_call(layer_kernel, out_shape=jax.ShapeDtypeStruct((ROWS, SHARE)...  128 us

profile of v6, /device:TPU:1, one launch (start us, length us, event | category | flops | bytes accessed | tf_op | source)
XLA Modules:
  0.0 129.4 jit_solution(13042602077779569093)
XLA Ops:
  0.0 127.7 %layer.1 = bf16[512,256]{1,0:T(8,128)(2,1)} custom-call(bf16[512,256]{1,0:T(8,128)(2,1)} %queries_ref.1, bf16[512,2,128]{2,1,0:T(2,128)(2,1)} %pairs_ref.1, bf16[256,2048]{1,0:T(8,128)(2,1)} %out_weight_ref.1, bf16[512,256]{1,0:T(8,128)(2,1)} %residual_ref.1, f32[1,2048]{1,0:T(1,128)} %bitcast.2, bf16[2048,2,256]{2,1,0:T(2,128)(2,1)} %qk_weight_ref.1, ...), custom_call_target="tpu_custom_call" | custom-call | tf_op jit(solution)/shard_map/layer/pallas_call | solution.py:597
  127.7 1.7 %copy.14 = bf16[512,256]{1,0:T(8,128)(2,1)} copy(bf16[512,256]{1,0:T(8,128)(2,1)} %layer.1) | data formatting | bytes 524288

commit v7 on v6

--- a/solution.py
+++ b/solution.py
@@ -25,8 +25,8 @@
 CHUNKS = VALUE_HEADS * ROWS // CHUNK
 Z = 8
 Y = 4
-HALF = DV // 2
-MESSAGE = DK + HALF + 16
+MESSAGE = DK + DV + 16
+PER_TURN = 2
 MESH = pl.DeviceIdType.MESH
 f32 = jnp.float32
 bf16 = jnp.bfloat16
@@ -87,7 +87,7 @@
     lower = inclusive.astype(f32)
     for h in range(VALUE_HEADS):
         prefix[h] = jnp.concatenate([eye, jnp.zeros_like(eye)], axis=1)
-    per_turn = 2
+    per_turn = PER_TURN
 
     def turn(t, carry):
         items = []
@@ -158,10 +158,9 @@
         change = (prefix[h, :, :DK] - decay * eye).T.astype(bf16)
         offset = prefix[h, :, DK:].T.astype(bf16)
         tail = three_rows(jnp.broadcast_to(decay, (1, DK)))
-        for c in range(2):
-            message_ref[2 * h + c, :DK] = change
-            message_ref[2 * h + c, DK:DK + HALF] = offset[c * HALF:(c + 1) * HALF]
-            message_ref[2 * h + c, DK + HALF:] = tail
+        message_ref[h, :DK] = change
+        message_ref[h, DK:DK + DV] = offset
+        message_ref[h, DK + DV:] = tail
 
 
 def slab_outputs(zero_ref, lead_ref, mixing, both, before_ref, query):
@@ -297,7 +296,7 @@
                  packed_ref, pair_now, queries, window, peak, total_mix, out_weight, mix, normed, hidden_ref, projected,
                  squares, qk_raw, vg_raw, weight, delta_weight,
                  zero_ref, lead_ref, message_ref, slab_prefix, mixing, both, before_ref, query,
-                 row, total, column, prefix, first, back, landed,
+                 row, total, column, prefix, back, landed,
                  gate, gated, to_sibling, from_sibling, far, relay, waiting, near, arrived,
                  kv_send, kv_recv, ow_send, ow_recv, mix_send, mix_recv, norm_send, norm_recv,
                  local_sem, row_send, row_recv, col_send, col_recv, back_send, back_recv,
@@ -468,18 +467,35 @@
     squares[...] = jnp.broadcast_to(inverse, (ROWS, 128))
     local_slab(projected, squares, packed_ref, message_ref, slab_prefix, mixing, both, before_ref, query)
 
-    sends = []
-    for d in FAR_FIRST:
-        copy = pltpu.make_async_remote_copy(
-            src_ref=message_ref.at[(z + d) % Z], dst_ref=row.at[z], send_sem=row_send.at[d],
-            recv_sem=row_recv.at[d], device_id=in_row(d), device_id_type=MESH)
-        copy.start()
-        sends.append(copy)
-    row[z] = message_ref[z]
-    first[...] = initial_ref[z // 2].T
-    i, j = grid_of(DK + HALF, DK)
-    run = (i == j).astype(f32)
-    decay = jnp.ones((1, DK), f32)
+    def to_job(h):
+        return pltpu.make_async_remote_copy(
+            src_ref=message_ref.at[h], dst_ref=row.at[z], send_sem=row_send.at[h],
+            recv_sem=row_recv.at[z], device_id={"seq": y * Z + 2 * h}, device_id_type=MESH)
+
+    def from_place(place):
+        return pltpu.make_async_remote_copy(
+            src_ref=message_ref.at[0], dst_ref=row.at[place], send_sem=row_send.at[0],
+            recv_sem=row_recv.at[place], device_id={"seq": y * Z + 2 * 0}, device_id_type=MESH)
+
+    def entering_to(d):
+        return pltpu.make_async_remote_copy(
+            src_ref=back.at[(z + d) % Z], dst_ref=landed.at[z // 2], send_sem=back_send.at[d],
+            recv_sem=back_recv.at[z // 2], device_id=in_row(d), device_id_type=MESH)
+
+    def entering_from(h):
+        return pltpu.make_async_remote_copy(
+            src_ref=back.at[0], dst_ref=landed.at[h], send_sem=back_send.at[0],
+            recv_sem=back_recv.at[h], device_id=in_row(1), device_id_type=MESH)
+
+    for h in range(VALUE_HEADS):
+        @pl.when(z != 2 * h)
+        def _():
+            to_job(h).start()
+
+        @pl.when(z == 2 * h)
+        def _():
+            row[z] = message_ref[h]
+
     slab_outputs(zero_ref, lead_ref, mixing, both, before_ref, query)
     for at in range(PROJECTED - VALUE_HEADS * DV, PROJECTED, 256):
         projected[:, at:at + 256] = sum(
@@ -489,49 +505,59 @@
         at = 2 * KEY_HEADS * DK + (VALUE_HEADS + h) * DV
         u = projected[:, at:at + DV] * squares[...]
         gate[:, cols] = head_gain_ref[...] * (u / (1.0 + jnp.exp(-u)))
-    for copy in sends:
-        copy.wait()
-    zero = jnp.zeros((DK, DK), f32)
-    for place in range(Z):
-        prefix[place] = run
-        a = sum_rows(row[place, DK + HALF:])
-        offset = jnp.concatenate([zero, row[place, DK:DK + HALF].astype(f32)], axis=0)
-        run = a * run + mm2(run, row[place, :DK]) + offset
-        decay = decay * a
-    total[:DK + HALF] = jnp.where(i == j, run - decay, run).astype(bf16)
-    total[DK + HALF:] = three_rows(decay)
-    sends = []
-    for d in (2, 1, 3):
-        copy = pltpu.make_async_remote_copy(
-            src_ref=total, dst_ref=column.at[y], send_sem=col_send.at[d], recv_sem=col_recv.at[d],
-            device_id=in_column(d), device_id_type=MESH)
-        copy.start()
-        sends.append(copy)
-    column[y] = total[...]
-    state = first[pl.ds(pl.multiple_of((z % 2) * HALF, HALF), HALF), :]
-    for copy in sends:
-        copy.wait()
-    for place in range(Y - 1):
-        a = sum_rows(column[place, DK + HALF:])
-        after = a * state + mm2(state, column[place, :DK]) + column[place, DK:DK + HALF].astype(f32)
-        state = jnp.where(place < y, after, state)
-    for place in range(Z):
-        entering = mm3(state, prefix[place, :DK]) + prefix[place, DK:]
-        back[place] = entering.astype(bf16)
-    sends = []
-    for d in FAR_FIRST:
-        copy = pltpu.make_async_remote_copy(
-            src_ref=back.at[(z + d) % Z], dst_ref=landed.at[z], send_sem=back_send.at[d],
-            recv_sem=back_recv.at[d], device_id=in_row(d), device_id_type=MESH)
-        copy.start()
-        sends.append(copy)
-    landed[z] = back[z]
-    for copy in sends:
-        copy.wait()
+    is_job = z % 2 == 0
+
+    @pl.when(is_job)
+    def _():
+        for place in range(Z):
+            @pl.when(z != place)
+            def _():
+                from_place(place).wait_recv()
+
+        i, j = grid_of(DK + DV, DK)
+        run = (i == j).astype(f32)
+        decay = jnp.ones((1, DK), f32)
+        zero = jnp.zeros((DK, DK), f32)
+        for place in range(Z):
+            prefix[place] = run
+            a = sum_rows(row[place, DK + DV:])
+            offset = jnp.concatenate([zero, row[place, DK:DK + DV].astype(f32)], axis=0)
+            run = a * run + mm2(run, row[place, :DK]) + offset
+            decay = decay * a
+        total[:DK + DV] = jnp.where(i == j, run - decay, run).astype(bf16)
+        total[DK + DV:] = three_rows(decay)
+        sends = []
+        for d in (2, 1, 3):
+            sends.append(send(total, column.at[y], col_send.at[d], col_recv.at[d], in_column(d)))
+        column[y] = total[...]
+        state = initial_ref[z // 2].T
+        for copy in sends:
+            copy.wait()
+        for place in range(Y - 1):
+            a = sum_rows(column[place, DK + DV:])
+            after = a * state + mm2(state, column[place, :DK]) + column[place, DK:DK + DV].astype(f32)
+            state = jnp.where(place < y, after, state)
+        for place in range(Z):
+            entering = mm3(state, prefix[place, :DK]) + prefix[place, DK:]
+            back[place] = entering.astype(bf16)
+        for d in FAR_FIRST:
+            entering_to(d).start()
+        landed[z // 2] = back[z]
+
+    for h in range(VALUE_HEADS):
+        @pl.when(z != 2 * h)
+        def _():
+            to_job(h).wait_send()
+            entering_from(h).wait_recv()
+
+    @pl.when(is_job)
+    def _():
+        for d in FAR_FIRST:
+            entering_to(d).wait_send()
+
     for h in range(VALUE_HEADS):
         cols = slice(h * DV, (h + 1) * DV)
-        state = jnp.concatenate([landed[2 * h], landed[2 * h + 1]], axis=0)
-        delta = zero_ref[:, cols] + mm_nt(lead_ref[:, cols], state)
+        delta = zero_ref[:, cols] + mm_nt(lead_ref[:, cols], landed[h])
         gated[:, cols] = (delta * inverse_rms(delta) * gate[:, cols]).astype(bf16)
 
     def partial(d, core):
@@ -618,7 +644,7 @@
             pltpu.VMEM((VALUE_HEADS * DV, MODEL), bf16),
             pltpu.VMEM((ROWS, VALUE_HEADS * DV), f32),
             pltpu.VMEM((ROWS, VALUE_HEADS * DK), bf16),
-            pltpu.VMEM((Z, MESSAGE, DK), bf16),
+            pltpu.VMEM((VALUE_HEADS, MESSAGE, DK), bf16),
             pltpu.VMEM((VALUE_HEADS, DK, DK + DV), f32),
             pltpu.VMEM((CHUNKS, CHUNK, CHUNK), bf16),
             pltpu.VMEM((CHUNKS, CHUNK, DK + DV), bf16),
@@ -627,10 +653,9 @@
             pltpu.VMEM((Z, MESSAGE, DK), bf16),
             pltpu.VMEM((MESSAGE, DK), bf16),
             pltpu.VMEM((Y, MESSAGE, DK), bf16),
-            pltpu.VMEM((Z, DK + HALF, DK), f32),
-            pltpu.VMEM((DV, DK), f32),
-            pltpu.VMEM((Z, HALF, DK), bf16),
-            pltpu.VMEM((Z, HALF, DK), bf16),
+            pltpu.VMEM((Z, DK + DV, DK), f32),
+            pltpu.VMEM((Z, DV, DK), bf16),
+            pltpu.VMEM((VALUE_HEADS, DV, DK), bf16),
             pltpu.VMEM((ROWS, VALUE_HEADS * DV), f32),
             pltpu.VMEM((ROWS, VALUE_HEADS * DV), bf16),
             pltpu.VMEM((X, ROWS, SHARE), bf16),

time: 129 us -> 133 us (1.031)
  Pallas kernels: 128 us -> 131 us
    pallas_call x1, Pallas kernels: 128 us -> 131 us  [body(): pl.pallas_call(layer_kernel, out_shape=jax.ShapeDtypeStruct((ROWS, SHARE)...]
where the time goes in v7:
time: 133 us
  Pallas kernels  131 us (98%)
  local copies, waits for them, and re-layouts  1.67 us (1%)
    pallas_call x1, Pallas kernels, body(): pl.pallas_call(layer_kernel, out_shape=jax.ShapeDtypeStruct((ROWS, SHARE)...  131 us

profile of v7, /device:TPU:1, one launch (start us, length us, event | category | flops | bytes accessed | tf_op | source)
XLA Modules:
  0.0 132.6 jit_solution(4396338762608170205)
XLA Ops:
  0.0 130.9 %layer.1 = bf16[512,256]{1,0:T(8,128)(2,1)} custom-call(bf16[512,256]{1,0:T(8,128)(2,1)} %queries_ref.1, bf16[512,2,128]{2,1,0:T(2,128)(2,1)} %pairs_ref.1, bf16[256,2048]{1,0:T(8,128)(2,1)} %out_weight_ref.1, bf16[512,256]{1,0:T(8,128)(2,1)} %residual_ref.1, f32[1,2048]{1,0:T(1,128)} %bitcast.2, bf16[2048,2,256]{2,1,0:T(2,128)(2,1)} %qk_weight_ref.1, ...), custom_call_target="tpu_custom_call" | custom-call | tf_op jit(solution)/shard_map/layer/pallas_call | solution.py:623
  130.9 1.7 %copy.14 = bf16[512,256]{1,0:T(8,128)(2,1)} copy(bf16[512,256]{1,0:T(8,128)(2,1)} %layer.1) | data formatting | bytes 524288

commit v8 on v6

--- a/solution.py
+++ b/solution.py
@@ -87,7 +87,7 @@
     lower = inclusive.astype(f32)
     for h in range(VALUE_HEADS):
         prefix[h] = jnp.concatenate([eye, jnp.zeros_like(eye)], axis=1)
-    per_turn = 2
+    per_turn = 4
 
     def turn(t, carry):
         items = []

time: 129 us -> 128 us (level)
  Pallas kernels: 128 us -> 126 us
    pallas_call x1, Pallas kernels: 128 us -> 126 us  [body(): pl.pallas_call(layer_kernel, out_shape=jax.ShapeDtypeStruct((ROWS, SHARE)...]
where the time goes in v8:
time: 128 us
  Pallas kernels  126 us (98%)
  local copies, waits for them, and re-layouts  1.67 us (1%)
    pallas_call x1, Pallas kernels, body(): pl.pallas_call(layer_kernel, out_shape=jax.ShapeDtypeStruct((ROWS, SHARE)...  126 us

profile of v8, /device:TPU:1, one launch (start us, length us, event | category | flops | bytes accessed | tf_op | source)
XLA Modules:
  0.0 128.0 jit_solution(10939403727087903566)
XLA Ops:
  0.0 126.3 %layer.1 = bf16[512,256]{1,0:T(8,128)(2,1)} custom-call(bf16[512,256]{1,0:T(8,128)(2,1)} %queries_ref.1, bf16[512,2,128]{2,1,0:T(2,128)(2,1)} %pairs_ref.1, bf16[256,2048]{1,0:T(8,128)(2,1)} %out_weight_ref.1, bf16[512,256]{1,0:T(8,128)(2,1)} %residual_ref.1, f32[1,2048]{1,0:T(1,128)} %bitcast.2, bf16[2048,2,256]{2,1,0:T(2,128)(2,1)} %qk_weight_ref.1, ...), custom_call_target="tpu_custom_call" | custom-call | tf_op jit(solution)/shard_map/layer/pallas_call | solution.py:597
  126.4 1.7 %copy.14 = bf16[512,256]{1,0:T(8,128)(2,1)} copy(bf16[512,256]{1,0:T(8,128)(2,1)} %layer.1) | data formatting | bytes 524288
